TPU v7x, 512 devices: a whole 4x8x8 slice. The times are simulated.
512 devices in a mesh: section: 16 (over y, z_lo), tile: 32 (over x, z_hi, core).
Axes of the slice: x: 4, y: 8, z: 8 (z_hi: 4, z_lo: 2; z = z_hi * 2 + z_lo), core: 2. Of those that a mesh axis runs over, the one named last changes fastest.
Arguments:
- acts: float32 [16, 1, 256, 16, 256], P('section', None, 'tile')
- kernels: float32 [16, 3, 3, 256, 256], P('section'), may hold values from -0.125 to 0.125
- gammas: float32 [16, 256], P('section'), may hold values from 0.5 to 1.5
- pass_mask: int32 [16, 1, 256, 16, 256], P('section', None, 'tile'), may hold values 0 or 1
- drop_mask: int32 [16, 1, 256, 16], P('section', None, 'tile'), may hold values 0 or 1
- path_mask: int32 [16, 1], P('section'), may hold values from 0 to 1, as said below
- cotangent: float32 [1, 256, 16, 256], P(None, 'tile')
Outputs:
- act_grads: float32 [16, 1, 256, 16, 256], P('section', None, 'tile')
- kernel_grads: float32 [16, 3, 3, 256, 256], P('section', None, None, None, 'tile')
- gain_grads: float32 [16, 2, 256], P('section')
Inputs may be any that keep to these rules, and one draw needn't show every extreme that they name: `path_mask`: both values occur among the 16 entries.
All inputs are finite; a program needn't handle non-finite values. No bound on the sum of `pass_mask` or of `drop_mask` on one device may be relied on, other than what follows from the above.
Results may differ from a plain program's by a relative error of at most 0.00014.
Values sent between devices are 32-bit elements; how exact they have to be, the bound alone decides.
No kernel may reach another device: no remote copies, remote signals or barrier semaphores. Data moves between devices by JAX's collectives and lax.ppermute only.
A program may use at most 64 MiB of HBM per device.

v0:
```python
import jax
import jax.numpy as jnp
from jax import lax
from jax.sharding import PartitionSpec as P

GROUPS = 32


keep_drop = 0.9
keep_path = 0.75
eps = 1e-05
highest = lax.Precision.HIGHEST


def extended(cells, sides, width):
    for axis, dim in sides:
        count = lax.axis_size(axis)
        ends = count - 1
        head = lax.slice_in_dim(cells, 0, width, axis=dim)
        tail = lax.slice_in_dim(cells, cells.shape[dim] - width, cells.shape[dim], axis=dim)
        cells = jnp.concatenate(
            [
                lax.ppermute(tail, axis, [(i, (i + 1) % count) for i in range(ends)]),
                cells,
                lax.ppermute(head, axis, [((i + 1) % count, i) for i in range(ends)]),
            ],
            axis=dim,
        )
    return cells


def from_behind(value, axis, steps):
    count = lax.axis_size(axis)
    leading, last = (max(0, -steps), min(count, count - steps))
    return lax.ppermute(value, axis, [(source, source + steps) for source in range(leading, last)])


def conv_apply(padded, kernel, row_count, col_count):
    summed = None
    for row_tap in range(3):
        for col_tap in range(3):
            window = padded[:, row_tap : row_tap + row_count, col_tap : col_tap + col_count]
            product = jnp.einsum(
                "mhwc,cd->mhwd", window, kernel[row_tap, col_tap], precision=highest
            )
            summed = product if summed is None else summed + product
    return summed


def group_sums(values):
    shaped = values.reshape(values.shape[:3] + (GROUPS, values.shape[3] // GROUPS))
    return jnp.sum(shaped, axis=(1, 2, 4))


def spread_groups(group_values, channels):
    return jnp.repeat(group_values, channels // group_values.shape[1], axis=1)[:, None, None, :]


def on_device(acts, kernels, gammas, pass_mask, drop_mask, path_mask, cotangent):
    inputs = acts[0]
    kernel = kernels[0]
    gain = gammas[0]
    micro_count, local_rows, columns, channels = inputs.shape
    sections = lax.axis_size("section")
    section_index = lax.axis_index("section")
    group_count = lax.axis_size("tile") * local_rows * columns * (channels // GROUPS)
    rimmed = extended(inputs, (("tile", 1),), 1)
    padded = jnp.pad(rimmed, ((0, 0), (0, 0), (1, 1), (0, 0)))
    conv_out = conv_apply(padded, kernel, local_rows, columns)
    plain_sum, square_sum = lax.psum(
        (group_sums(conv_out), group_sums(conv_out * conv_out)), "tile"
    )
    group_mean = plain_sum / group_count
    inverse_std = lax.rsqrt(square_sum / group_count - group_mean * group_mean + eps)
    normed = (conv_out - spread_groups(group_mean, channels)) * spread_groups(inverse_std, channels)
    passing = (
        pass_mask[0].astype(jnp.float32)
        * (drop_mask[0].astype(jnp.float32)[..., None] / keep_drop)
        * (path_mask[0].astype(jnp.float32)[:, None, None, None] / keep_path)
    )
    flipped = jnp.transpose(kernel[::-1, ::-1], (0, 1, 3, 2))
    steps_total = sections + micro_count - 1

    def advance(step, carry):
        received, act_store, grad_store, gain_total = carry
        position = step - (sections - 1 - section_index)
        valid = (position >= 0) & (position < micro_count)
        incoming = jnp.where(section_index == sections - 1, cotangent, received)
        grad_out = incoming * passing
        grad_norm = grad_out * gain
        plain_grad, cross_grad = lax.psum(
            (group_sums(grad_norm), group_sums(grad_norm * normed)), "tile"
        )
        grad_conv = spread_groups(inverse_std, channels) * (
            grad_norm
            - spread_groups(plain_grad / group_count, channels)
            - normed * spread_groups(cross_grad / group_count, channels)
        )
        rim_grad = extended(grad_conv, (("tile", 1),), 1)
        padded_grad = jnp.pad(rim_grad, ((0, 0), (0, 0), (1, 1), (0, 0)))
        backward = conv_apply(padded_grad, flipped, local_rows, columns)
        outgoing = incoming + backward
        old_act = act_store
        act_store = jnp.where(valid, outgoing, old_act)
        old_grad = grad_store
        grad_store = jnp.where(valid, grad_conv, old_grad)
        gain_step = jnp.stack(
            [jnp.sum(grad_out * normed, axis=(0, 1, 2)), jnp.sum(grad_out, axis=(0, 1, 2))]
        )
        gain_total = gain_total + jnp.where(valid, gain_step, 0.0)
        passed = from_behind(outgoing, "section", -1)
        return (passed, act_store, grad_store, gain_total)

    start_carry = (
        jnp.zeros((1, local_rows, columns, channels), jnp.float32),
        jnp.zeros_like(inputs),
        jnp.zeros_like(inputs),
        jnp.zeros((2, channels), jnp.float32),
    )
    received, act_store, grad_store, gain_total = lax.fori_loop(
        0, steps_total, advance, start_carry
    )
    kernel_grad = jnp.stack(
        [
            jnp.stack(
                [
                    jnp.einsum(
                        "mhwc,mhwd->cd",
                        padded[:, row_tap : row_tap + local_rows, col_tap : col_tap + columns],
                        grad_store,
                        precision=highest,
                    )
                    for col_tap in range(3)
                ]
            )
            for row_tap in range(3)
        ]
    )
    kernel_share = lax.psum_scatter(kernel_grad, "tile", scatter_dimension=3, tiled=True)
    gain_summed = lax.psum(gain_total, "tile")
    return (act_store[None], kernel_share[None], gain_summed[None])


def solution(mesh):
    return jax.shard_map(
        on_device,
        mesh=mesh,
        in_specs=(
            P("section", None, "tile", None, None),
            P("section", None, None, None, None),
            P("section", None),
            P("section", None, "tile", None, None),
            P("section", None, "tile", None),
            P("section", None),
            P(None, "tile", None, None),
        ),
        out_specs=(
            P("section", None, "tile", None, None),
            P("section", None, None, None, "tile"),
            P("section", None, None),
        ),
        check_vma=False,
    )
```

profile of v0, /device:TPU:8, one launch (start us, length us, event | category | flops | bytes accessed | tf_op | source)
XLA Modules:
  0.0 1889.2 jit_solution(9294767769718607818)
XLA Ops:
  25.8 82.0 %all-reduce.4 = (f32[1,32]{1,0:T(1,128)S(1)}, f32[1,32]{1,0:T(1,128)S(1)}) all-reduce(f32[1,32]{1,0:T(1,128)S(1)} %bitcast.326, f32[1,32]{1,0:T(1,128)S(1)} %bitcast.327), channel_id=1, replica_groups=mesh['section'=16,'tile'=32] {'tile'}, use_global_device_ids=true, to_apply=%region_5.6 | all-reduce | flops 64 | bytes 512 | tf_op jit(solution)/shard_map/psum | solution.py:70
  109.5 1454.4 %while.22 = (s32[]{:T(128)}, f32[1,8,16,256]{3,2,1,0:T(8,128)S(1)}, f32[1,8,16,256]{3,2,1,0:T(8,128)}, f32[1,8,16,256]{3,2,1,0:T(8,128)S(1)}, f32[2,256]{1,0:T(2...) while((s32[]{:T(128)}, f32[1,8,16,256]{3,2,1,0:T(8,128)S(1)}, ...), condition=%wide.region_15.16_spmd.clone, body=%wide.region_6.15_spmd.clone.sunk | while | flops 907322944 | bytes 9810031 | solution.py:120
  111.2 69.9 %all-reduce.6 = (f32[1,32]{1,0:T(1,128)S(1)}, f32[1,32]{1,0:T(1,128)S(1)}) all-reduce(f32[1,32]{1,0:T(1,128)S(1)} %bitcast.324, f32[1,32]{1,0:T(1,128)S(1)} %bitcast.325), channel_id=1, replica_groups=mesh['section'=16,'tile'=32] {'tile'}, use_global_device_ids=true, to_apply=%region_12.12 | all-reduce | flops 64 | bytes 512 | tf_op jit(solution)/shard_map/while/body/eval_jaxpr/psum | solution.py:91
  199.9 70.7 %all-reduce.6 = (f32[1,32]{1,0:T(1,128)S(1)}, f32[1,32]{1,0:T(1,128)S(1)}) all-reduce(f32[1,32]{1,0:T(1,128)S(1)} %bitcast.324, f32[1,32]{1,0:T(1,128)S(1)} %bitcast.325), channel_id=1, replica_groups=mesh['section'=16,'tile'=32] {'tile'}, use_global_device_ids=true, to_apply=%region_12.12 | all-reduce | flops 64 | bytes 512 | tf_op jit(solution)/shard_map/while/body/eval_jaxpr/psum | solution.py:91
  290.6 70.0 %all-reduce.6 = (f32[1,32]{1,0:T(1,128)S(1)}, f32[1,32]{1,0:T(1,128)S(1)}) all-reduce(f32[1,32]{1,0:T(1,128)S(1)} %bitcast.324, f32[1,32]{1,0:T(1,128)S(1)} %bitcast.325), channel_id=1, replica_groups=mesh['section'=16,'tile'=32] {'tile'}, use_global_device_ids=true, to_apply=%region_12.12 | all-reduce | flops 64 | bytes 512 | tf_op jit(solution)/shard_map/while/body/eval_jaxpr/psum | solution.py:91
  380.2 71.0 %all-reduce.6 = (f32[1,32]{1,0:T(1,128)S(1)}, f32[1,32]{1,0:T(1,128)S(1)}) all-reduce(f32[1,32]{1,0:T(1,128)S(1)} %bitcast.324, f32[1,32]{1,0:T(1,128)S(1)} %bitcast.325), channel_id=1, replica_groups=mesh['section'=16,'tile'=32] {'tile'}, use_global_device_ids=true, to_apply=%region_12.12 | all-reduce | flops 64 | bytes 512 | tf_op jit(solution)/shard_map/while/body/eval_jaxpr/psum | solution.py:91
  471.7 70.0 %all-reduce.6 = (f32[1,32]{1,0:T(1,128)S(1)}, f32[1,32]{1,0:T(1,128)S(1)}) all-reduce(f32[1,32]{1,0:T(1,128)S(1)} %bitcast.324, f32[1,32]{1,0:T(1,128)S(1)} %bitcast.325), channel_id=1, replica_groups=mesh['section'=16,'tile'=32] {'tile'}, use_global_device_ids=true, to_apply=%region_12.12 | all-reduce | flops 64 | bytes 512 | tf_op jit(solution)/shard_map/while/body/eval_jaxpr/psum | solution.py:91
  561.3 71.0 %all-reduce.6 = (f32[1,32]{1,0:T(1,128)S(1)}, f32[1,32]{1,0:T(1,128)S(1)}) all-reduce(f32[1,32]{1,0:T(1,128)S(1)} %bitcast.324, f32[1,32]{1,0:T(1,128)S(1)} %bitcast.325), channel_id=1, replica_groups=mesh['section'=16,'tile'=32] {'tile'}, use_global_device_ids=true, to_apply=%region_12.12 | all-reduce | flops 64 | bytes 512 | tf_op jit(solution)/shard_map/while/body/eval_jaxpr/psum | solution.py:91
  652.7 70.1 %all-reduce.6 = (f32[1,32]{1,0:T(1,128)S(1)}, f32[1,32]{1,0:T(1,128)S(1)}) all-reduce(f32[1,32]{1,0:T(1,128)S(1)} %bitcast.324, f32[1,32]{1,0:T(1,128)S(1)} %bitcast.325), channel_id=1, replica_groups=mesh['section'=16,'tile'=32] {'tile'}, use_global_device_ids=true, to_apply=%region_12.12 | all-reduce | flops 64 | bytes 512 | tf_op jit(solution)/shard_map/while/body/eval_jaxpr/psum | solution.py:91
  742.4 71.0 %all-reduce.6 = (f32[1,32]{1,0:T(1,128)S(1)}, f32[1,32]{1,0:T(1,128)S(1)}) all-reduce(f32[1,32]{1,0:T(1,128)S(1)} %bitcast.324, f32[1,32]{1,0:T(1,128)S(1)} %bitcast.325), channel_id=1, replica_groups=mesh['section'=16,'tile'=32] {'tile'}, use_global_device_ids=true, to_apply=%region_12.12 | all-reduce | flops 64 | bytes 512 | tf_op jit(solution)/shard_map/while/body/eval_jaxpr/psum | solution.py:91
  833.8 70.1 %all-reduce.6 = (f32[1,32]{1,0:T(1,128)S(1)}, f32[1,32]{1,0:T(1,128)S(1)}) all-reduce(f32[1,32]{1,0:T(1,128)S(1)} %bitcast.324, f32[1,32]{1,0:T(1,128)S(1)} %bitcast.325), channel_id=1, replica_groups=mesh['section'=16,'tile'=32] {'tile'}, use_global_device_ids=true, to_apply=%region_12.12 | all-reduce | flops 64 | bytes 512 | tf_op jit(solution)/shard_map/while/body/eval_jaxpr/psum | solution.py:91
  923.4 71.0 %all-reduce.6 = (f32[1,32]{1,0:T(1,128)S(1)}, f32[1,32]{1,0:T(1,128)S(1)}) all-reduce(f32[1,32]{1,0:T(1,128)S(1)} %bitcast.324, f32[1,32]{1,0:T(1,128)S(1)} %bitcast.325), channel_id=1, replica_groups=mesh['section'=16,'tile'=32] {'tile'}, use_global_device_ids=true, to_apply=%region_12.12 | all-reduce | flops 64 | bytes 512 | tf_op jit(solution)/shard_map/while/body/eval_jaxpr/psum | solution.py:91
  1015.2 70.0 %all-reduce.6 = (f32[1,32]{1,0:T(1,128)S(1)}, f32[1,32]{1,0:T(1,128)S(1)}) all-reduce(f32[1,32]{1,0:T(1,128)S(1)} %bitcast.324, f32[1,32]{1,0:T(1,128)S(1)} %bitcast.325), channel_id=1, replica_groups=mesh['section'=16,'tile'=32] {'tile'}, use_global_device_ids=true, to_apply=%region_12.12 | all-reduce | flops 64 | bytes 512 | tf_op jit(solution)/shard_map/while/body/eval_jaxpr/psum | solution.py:91
  1105.9 71.0 %all-reduce.6 = (f32[1,32]{1,0:T(1,128)S(1)}, f32[1,32]{1,0:T(1,128)S(1)}) all-reduce(f32[1,32]{1,0:T(1,128)S(1)} %bitcast.324, f32[1,32]{1,0:T(1,128)S(1)} %bitcast.325), channel_id=1, replica_groups=mesh['section'=16,'tile'=32] {'tile'}, use_global_device_ids=true, to_apply=%region_12.12 | all-reduce | flops 64 | bytes 512 | tf_op jit(solution)/shard_map/while/body/eval_jaxpr/psum | solution.py:91
  1198.7 70.0 %all-reduce.6 = (f32[1,32]{1,0:T(1,128)S(1)}, f32[1,32]{1,0:T(1,128)S(1)}) all-reduce(f32[1,32]{1,0:T(1,128)S(1)} %bitcast.324, f32[1,32]{1,0:T(1,128)S(1)} %bitcast.325), channel_id=1, replica_groups=mesh['section'=16,'tile'=32] {'tile'}, use_global_device_ids=true, to_apply=%region_12.12 | all-reduce | flops 64 | bytes 512 | tf_op jit(solution)/shard_map/while/body/eval_jaxpr/psum | solution.py:91
  1280.7 7.0 collective-permute-done.2
  1289.4 71.0 %all-reduce.6 = (f32[1,32]{1,0:T(1,128)S(1)}, f32[1,32]{1,0:T(1,128)S(1)}) all-reduce(f32[1,32]{1,0:T(1,128)S(1)} %bitcast.324, f32[1,32]{1,0:T(1,128)S(1)} %bitcast.325), channel_id=1, replica_groups=mesh['section'=16,'tile'=32] {'tile'}, use_global_device_ids=true, to_apply=%region_12.12 | all-reduce | flops 64 | bytes 512 | tf_op jit(solution)/shard_map/while/body/eval_jaxpr/psum | solution.py:91
  1372.2 8.2 collective-permute-done.2
  1382.1 70.0 %all-reduce.6 = (f32[1,32]{1,0:T(1,128)S(1)}, f32[1,32]{1,0:T(1,128)S(1)}) all-reduce(f32[1,32]{1,0:T(1,128)S(1)} %bitcast.324, f32[1,32]{1,0:T(1,128)S(1)} %bitcast.325), channel_id=1, replica_groups=mesh['section'=16,'tile'=32] {'tile'}, use_global_device_ids=true, to_apply=%region_12.12 | all-reduce | flops 64 | bytes 512 | tf_op jit(solution)/shard_map/while/body/eval_jaxpr/psum | solution.py:91
  1464.0 7.1 collective-permute-done.2
  1472.8 71.0 %all-reduce.6 = (f32[1,32]{1,0:T(1,128)S(1)}, f32[1,32]{1,0:T(1,128)S(1)}) all-reduce(f32[1,32]{1,0:T(1,128)S(1)} %bitcast.324, f32[1,32]{1,0:T(1,128)S(1)} %bitcast.325), channel_id=1, replica_groups=mesh['section'=16,'tile'=32] {'tile'}, use_global_device_ids=true, to_apply=%region_12.12 | all-reduce | flops 64 | bytes 512 | tf_op jit(solution)/shard_map/while/body/eval_jaxpr/psum | solution.py:91
  1555.7 8.2 collective-permute-done.2
  1572.9 71.0 %psum.51 = f32[1,2,256]{2,1,0:T(2,128)} all-reduce(f32[1,2,256]{2,1,0:T(2,128)S(1)} %bitcast.323), channel_id=1, replica_groups=mesh['section'=16,'tile'=32] {'tile'}, use_global_device_ids=true, to_apply=%region_17.18 | all-reduce | flops 512 | bytes 4096 | tf_op jit(solution)/shard_map/psum | solution.py:140
  1644.0 236.8 %all-reduce.9.cloned.1.call-done = f32[3,3,256,256]{2,1,0,3:T(4,128)} async-done(((f32[3,3,256,256]{2,1,0,3:T(4,128)}), f32[3,3,256,256]{2,1,0,3:T(4,128)}) %all-reduce.9.cloned.1.call-update) | async-done | bytes 2359312
  (753 shorter events, 321.6 us)
Async XLA Ops:
  7.2 1873.6 %all-reduce.9.cloned.1.call-start = ((), (), s32[]{:S(2)}) async-start(), calls=%async_computation | async-start | bytes 6291456
  8.0 10.7 collective-permute-start.3
  9.7 9.0 collective-permute-start.4
  183.0 4.3 collective-permute-start
  190.9 7.2 collective-permute-start.2
  272.6 4.3 collective-permute-start
  280.5 8.4 collective-permute-start.2
  362.6 4.3 collective-permute-start
  370.5 8.0 collective-permute-start.2
  453.2 4.3 collective-permute-start
  461.1 8.9 collective-permute-start.2
  543.7 4.3 collective-permute-start
  551.6 8.0 collective-permute-start.2
  642.2 8.8 collective-permute-start.2
  732.7 7.9 collective-permute-start.2
  823.2 8.8 collective-permute-start.2
  913.7 7.9 collective-permute-start.2
  1004.3 9.2 collective-permute-start.2
  1095.1 9.1 collective-permute-start.2
  1186.8 10.2 collective-permute-start.2
  1278.5 9.1 collective-permute-start.2
  1370.3 10.2 collective-permute-start.2
  1462.0 9.1 collective-permute-start.2
  1553.7 10.2 collective-permute-start.2
  (132 other events, 750.3 us)
Sparse Core Ops, SparseCore 0:
  1571.1 309.6 all-reduce.8
where the time goes:
time: 1890 us
  blocking collectives  1280 us (68%)
  waiting for transfers between devices  328 us (17%)
  starting transfers between devices  134 us (7%)
  matrix products  51.6 us (3%)
  other arithmetic  41 us (2%)
  local copies, waits for them, and re-layouts  34.5 us (2%)
    psum x16, blocking collectives, advance(): lax.psum((group_sums(grad_norm), group_sums(grad_norm * normed)), 'tile')  1130 us
    unnamed x2, waiting for transfers between devices  237 us
    psum x1, blocking collectives, on_device(): lax.psum((group_sums(conv_out), group_sums(conv_out * conv_out)), 'tile')  82 us
    ppermute x16, waiting for transfers between devices, from_behind(): lax.ppermute(value, axis, [(source, source + steps) for source in range(l...  78.2 us
    psum x1, blocking collectives, on_device(): gain_summed = lax.psum(gain_total, 'tile')  71 us
    ppermute x16, starting transfers between devices, from_behind(): lax.ppermute(value, axis, [(source, source + steps) for source in range(l...  61.5 us
    ppermute x17, starting transfers between devices, extended(): lax.ppermute(tail, axis, [(i, (i + 1) % count) for i in range(ends)])  50.2 us
    dot_general x153, matrix products, conv_apply(): jnp.einsum('mhwc,cd->mhwd', window, kernel[row_tap, col_tap], precision=h...  47.9 us
  transfers between devices with their start and end apart: 51, of which 33 were waited for; matrix products, arithmetic and copies ran while one was open for 0% of the time, Pallas kernels for 0%

commit v1 on v0

v1 whole, which is shorter than its diff:
```python
import functools

import jax
import jax.numpy as jnp
from jax import lax
from jax.experimental import pallas as pl
from jax.experimental.pallas import tpu as pltpu
from jax.sharding import Mesh
from jax.sharding import PartitionSpec as P

GROUPS = 32
C = 256
COLS = 16
ROWS = 8
OWN = ROWS * COLS

keep_drop = 0.9
keep_path = 0.75
eps = 1e-05
highest = lax.Precision.HIGHEST
f32 = jnp.float32
bf16 = jnp.bfloat16

SECTION = ("pair", "member")
TILE = ("x", "z", "core")
ALL = SECTION + TILE


def split(values):
    high = values.astype(bf16)
    return high, (values - high.astype(f32)).astype(bf16)


def dot(left, right, precision=None):
    return jnp.dot(left, right, preferred_element_type=f32, precision=precision)


def dot3(left, right):
    lh, ll = left
    rh, rl = right
    return dot(lh, rh) + dot(ll, rh) + dot(lh, rl)


def shifted(values, offset):
    if offset == 0:
        return values
    count = values.shape[0]
    column = lax.broadcasted_iota(jnp.int32, values.shape, 0) & (COLS - 1)
    rolled = pltpu.roll(values, (-offset) % count, 0)
    edge = COLS - 1 if offset > 0 else 0
    return jnp.where(column == edge, 0.0, rolled)


def conv_back(field, high_ref, low_ref):
    wide = jnp.concatenate([shifted(field, 1), field, shifted(field, -1)], axis=1)
    high, low = split(wide)
    count = field.shape[0] - 2 * COLS
    total = None
    for tap in range(3):
        start = (2 - tap) * COLS
        part = dot3(
            (high[start : start + count], low[start : start + count]),
            (high_ref[tap], low_ref[tap]),
        )
        total = part if total is None else total + part
    return total


def group_matrix():
    channel = lax.broadcasted_iota(jnp.int32, (C, GROUPS), 0)
    group = lax.broadcasted_iota(jnp.int32, (C, GROUPS), 1)
    return jnp.where((channel >> 3) == group, 1.0, 0.0).astype(f32)


def spread_matrix():
    channel = lax.broadcasted_iota(jnp.int32, (GROUPS, C), 1)
    group = lax.broadcasted_iota(jnp.int32, (GROUPS, C), 0)
    return jnp.where((channel >> 3) == group, 1.0, 0.0).astype(f32)


def column_sum(values):
    return jnp.sum(values, axis=0, keepdims=True)


def forward_kernel(top, main, bottom, kernel, conv_out, sums):
    image = jnp.concatenate([top[...], main[...], bottom[...]], axis=0)
    count = image.shape[0] - 2 * COLS
    total = None
    for col_tap in range(3):
        high, low = split(shifted(image, col_tap - 1))
        for row_tap in range(3):
            start = row_tap * COLS
            part = dot3(
                (high[start : start + count], low[start : start + count]),
                split(kernel[row_tap * 3 + col_tap]),
            )
            total = part if total is None else total + part
    conv_out[...] = total
    own = total[2 * COLS : 2 * COLS + OWN]
    sums[...] = jnp.concatenate([column_sum(own), column_sum(own * own)], axis=0)


def prepare_kernel(
    flags, own, near, far, pass_b, norm_a, norm_b, valid, scale,
    a_high, a_low, b_high, b_low, response, weight_scr, flat_scr, full_scr,
):
    tap = pl.program_id(0)
    core = flags[3]
    member = flags[1]
    near_tap, far_tap = near[0], far[0]
    partner = jnp.concatenate(
        [jnp.where(core == 0, near_tap, far_tap), jnp.where(core == 0, far_tap, near_tap)], axis=0
    )
    kernel_a = jnp.where(member == 1, own[0], partner)
    kernel_b = jnp.where(member == 1, partner, own[0])
    high, low = split(kernel_a.T)
    a_high[0] = high
    a_low[0] = low
    high, low = split(kernel_b.T)
    b_high[0] = high
    b_low[0] = low

    @pl.when(tap == 0)
    def _():
        passing = pass_b[2 * COLS : 2 * COLS + OWN]
        normed = norm_b[2 * COLS : 2 * COLS + OWN]
        weight_scr[...] = jnp.concatenate([passing.T, (passing * normed).T], axis=0)
        flat_scr[...] = jnp.zeros_like(flat_scr)
        full_scr[...] = jnp.zeros_like(full_scr)

    row_tap = tap // 3
    col_tap = tap - row_tap * 3
    begin = pl.multiple_of((3 - row_tap) * COLS, COLS)
    fields = jnp.concatenate(
        [norm_a[pl.ds(begin, OWN), :], valid[pl.ds(begin, OWN), :]], axis=1
    )
    moved = jnp.where(
        col_tap == 1,
        fields,
        jnp.where(col_tap == 0, shifted(fields, 1), shifted(fields, -1)),
    )
    moment = dot3(split(weight_scr[...]), split(moved))
    both = jnp.concatenate([kernel_a, kernel_a], axis=0)
    full_scr[...] += moment[:, :C] * both
    flat_scr[...] += moment[:, C : C + 1] * both

    @pl.when(tap == 8)
    def _():
        groups = group_matrix()
        contract = (((0,), (1,)), ((), ()))
        for index, scratch in enumerate((flat_scr, full_scr)):
            response[GROUPS * index : GROUPS * (index + 1), :] = lax.dot_general(
                groups, scratch[...] * scale[...], contract,
                preferred_element_type=f32, precision=highest,
            )


def first_kernel(top, main, bottom, pass_a, norm_a, pass_b, norm_b, params, a_high, a_low, sums):
    incoming = jnp.concatenate([top[...], main[...], bottom[...]], axis=0)
    grad_out = incoming * pass_a[...]
    own = slice(2 * COLS, 2 * COLS + OWN)
    scaled = grad_out[COLS:-COLS] * (params[0:1, :] * params[1:2, :])
    rest = incoming[own] + conv_back(scaled, a_high, a_low)
    grad_b = rest * pass_b[own, :]
    parts = jnp.concatenate(
        [
            column_sum(grad_out[own]),
            column_sum(grad_out[own] * norm_a[own, :]),
            column_sum(grad_b),
            column_sum(grad_b * norm_b[own, :]),
        ],
        axis=0,
    )
    sums[...] = jnp.broadcast_to(parts[None], sums.shape)


def second_kernel(
    count, flags, received, response, top, main, bottom, pass_a, norm_a, pass_b, norm_b, valid,
    params, a_high, a_low, b_high, b_low, old_act, old_grad, old_gain,
    out, out_head, out_tail, act, grad, gain,
):
    incoming = jnp.concatenate([top[...], main[...], bottom[...]], axis=0)
    gamma_a, inverse_a, gamma_b, inverse_b = (params[i : i + 1, :] for i in range(4))
    totals = jnp.sum(received[...], axis=0)
    groups, spread = group_matrix(), spread_matrix()
    means_a = dot(totals[0:2] * gamma_a, groups, highest) * (1.0 / count)
    shift = dot(means_a[0:1], response[:GROUPS, :], highest) + dot(
        means_a[1:2], response[GROUPS:, :], highest
    )
    totals_b = totals[2:4] - jnp.concatenate([shift[:, :C], shift[:, C:]], axis=0)
    means_b = dot(totals_b * gamma_b, groups, highest) * (1.0 / count)
    wide_a = dot(means_a, spread, highest)
    wide_b = dot(means_b, spread, highest)
    inside = jnp.concatenate([valid[...], valid[...]], axis=1)
    grad_a = inverse_a * (
        incoming * pass_a[...] * gamma_a - inside * wide_a[0:1] - norm_a[...] * wide_a[1:2]
    )
    middle = incoming[COLS:-COLS] + conv_back(grad_a, a_high, a_low)
    grad_b = inverse_b * (
        middle * pass_b[COLS:-COLS, :] * gamma_b
        - inside[COLS:-COLS] * wide_b[0:1]
        - norm_b[COLS:-COLS, :] * wide_b[1:2]
    )
    last = middle[COLS:-COLS] + conv_back(grad_b, b_high, b_low)
    out[...] = last
    out_head[...] = last[: 2 * COLS]
    out_tail[...] = last[-2 * COLS :]
    active = flags[0] == 1
    upper = flags[1] == 1
    act[...] = jnp.where(
        active, jnp.where(upper, middle[COLS:-COLS], last), old_act[...]
    )
    grad[...] = jnp.where(
        active, jnp.where(upper, grad_a[2 * COLS : -2 * COLS], grad_b[COLS:-COLS]), old_grad[...]
    )
    pair_a = jnp.concatenate([totals[1:2], totals[0:1]], axis=0)
    pair_b = jnp.concatenate([totals_b[1:2], totals_b[0:1]], axis=0)
    gain[...] = jnp.where(active, jnp.where(upper, pair_a, pair_b), old_gain[...])


def kernel_grad_kernel(tiles, flags, top, main, bottom, grad, mine, other):
    share = C // tiles
    image = jnp.concatenate([top[...], main[...], bottom[...]], axis=0)
    turned = grad[...].T.reshape(tiles // 2, 2, share, OWN)
    even = turned[:, 0].reshape(C // 2, OWN)
    odd = turned[:, 1].reshape(C // 2, OWN)
    core = flags[3]
    left = split(
        jnp.concatenate(
            [jnp.where(core == 0, even, odd), jnp.where(core == 0, odd, even)], axis=0
        )
    )
    for col_tap in range(3):
        high, low = split(shifted(image, col_tap - 1))
        for row_tap in range(3):
            start = (row_tap + 2) * COLS
            product = dot3(left, (high[start : start + OWN], low[start : start + OWN]))
            where = slice((row_tap * 3 + col_tap) * C, (row_tap * 3 + col_tap + 1) * C)
            mine[:, where] = product[: C // 2]
            other[:, where] = product[C // 2 :]


def call(body, out_shape, operands, flagged, **options):
    spec = pl.BlockSpec(memory_space=pltpu.VMEM)
    in_specs = [spec] * len(operands)
    if flagged:
        in_specs[0] = pl.BlockSpec(memory_space=pltpu.SMEM)
    many = isinstance(out_shape, tuple)
    return pl.pallas_call(
        body,
        out_shape=out_shape,
        in_specs=in_specs,
        out_specs=tuple(spec for _ in out_shape) if many else spec,
        compiler_params=pltpu.CompilerParams(vmem_limit_bytes=40 * 2**20),
        **options,
    )(*operands)


def shape(*dims, dtype=f32):
    return jax.ShapeDtypeStruct(dims, dtype)


def prepare(flags, kernel, near, far, pass_b, norm_a, norm_b, valid, scale):
    tap = lambda rows: pl.BlockSpec((1, rows, C), lambda i: (i, 0, 0))
    whole = lambda a: pl.BlockSpec(a.shape, lambda i: (0,) * a.ndim)
    return pl.pallas_call(
        prepare_kernel,
        grid=(9,),
        out_shape=tuple(shape(9, C, C, dtype=bf16) for _ in range(4))
        + (shape(2 * GROUPS, 2 * C),),
        in_specs=[
            pl.BlockSpec(memory_space=pltpu.SMEM),
            tap(C),
            tap(C // 2),
            tap(C // 2),
            whole(pass_b),
            whole(norm_a),
            whole(norm_b),
            whole(valid),
            whole(scale),
        ],
        out_specs=tuple(tap(C) for _ in range(4))
        + (pl.BlockSpec((2 * GROUPS, 2 * C), lambda i: (0, 0)),),
        scratch_shapes=[
            pltpu.VMEM((2 * C, OWN), f32),
            pltpu.VMEM((2 * C, C), f32),
            pltpu.VMEM((2 * C, C), f32),
        ],
        compiler_params=pltpu.CompilerParams(vmem_limit_bytes=40 * 2**20),
    )(flags, kernel, near, far, pass_b, norm_a, norm_b, valid, scale)


def on_device(acts, kernels, gammas, pass_mask, drop_mask, path_mask, cotangent):
    pairs = lax.axis_size("pair")
    tiles = lax.axis_size(TILE)
    devices = 2 * pairs * tiles
    pair, member, core = (lax.axis_index(a) for a in ("pair", "member", "core"))
    tile = lax.axis_index(TILE)
    count = tiles * OWN * (C // GROUPS)
    swap = [(0, 1), (1, 0)]

    own_kernel = kernels[0].reshape(9, C, C)
    half = lax.dynamic_slice_in_dim(own_kernel, core * (C // 2), C // 2, axis=1)
    near = lax.ppermute(half, "member", swap)
    far = lax.ppermute(near, "core", swap)

    passing = (
        pass_mask[0, 0].astype(f32)
        * (drop_mask[0, 0].astype(f32)[..., None] / keep_drop)
        * (path_mask[0].astype(f32)[:, None, None] / keep_path)
    ).reshape(OWN, C)
    image = acts[0, 0].reshape(OWN, C)
    start = cotangent[0].reshape(OWN, C)

    def neighbours(value, step, jump):
        return lax.ppermute(
            value,
            ALL,
            [
                (i, i - jump * 2 * tiles + step)
                for i in range(jump * 2 * tiles, devices)
                if 0 <= i % tiles + step < tiles
            ],
        )

    from_above = neighbours(
        jnp.concatenate([image[-3 * COLS :], passing[-2 * COLS :], start[-2 * COLS :]]), 1, 0
    )
    from_below = neighbours(
        jnp.concatenate([image[: 3 * COLS], passing[: 2 * COLS], start[: 2 * COLS]]), -1, 0
    )
    cuts = (0, 3 * COLS, 5 * COLS, 7 * COLS)
    above = [from_above[a:b] for a, b in zip(cuts, cuts[1:])]
    below = [from_below[a:b] for a, b in zip(cuts, cuts[1:])]
    image_parts = (above[0], image, below[0])
    passing = jnp.concatenate([above[1], passing, below[1]])
    tall = 12 * COLS
    conv_out, sums = call(
        forward_kernel,
        (shape(tall, C), shape(2, C)),
        image_parts + (own_kernel,),
        False,
    )
    fields = jnp.stack([conv_out, passing])
    partner_fields = lax.ppermute(fields, "member", swap)
    packed = jnp.concatenate([sums, gammas, jnp.zeros((1, C), f32)])
    gathered = lax.all_to_all(
        jnp.broadcast_to(packed, (2 * tiles, 4, C)), ("member",) + TILE, 0, 0
    ).reshape(2, tiles, 4, C)
    totals = jnp.sum(gathered[:, :, :2], axis=1)
    gamma_both = gathered[:, 0, 2]
    group_totals = jnp.sum(totals.reshape(2, 2, GROUPS, C // GROUPS), axis=3) / count
    mean = group_totals[:, 0]
    inverse = lax.rsqrt(group_totals[:, 1] - mean * mean + eps)
    mean = jnp.repeat(mean, C // GROUPS, axis=1)
    inverse = jnp.repeat(inverse, C // GROUPS, axis=1)
    row = jnp.arange(tall, dtype=jnp.int32)[:, None]
    inside = ((tile > 0) | (row >= 2 * COLS)) & ((tile < tiles - 1) | (row < 10 * COLS))
    valid = jnp.broadcast_to(inside.astype(f32), (tall, C // 2))
    inside = inside.astype(f32)

    upper = member == 1
    conv_a = jnp.where(upper, fields[0], partner_fields[0])
    conv_b = jnp.where(upper, partner_fields[0], fields[0])
    pass_a = jnp.where(upper, fields[1], partner_fields[1])
    pass_b = jnp.where(upper, partner_fields[1], fields[1])
    norm_a = (conv_a - mean[1:2]) * inverse[1:2] * inside
    norm_b = (conv_b - mean[0:1]) * inverse[0:1] * inside
    params = jnp.concatenate(
        [gamma_both[1:2], inverse[1:2], gamma_both[0:1], inverse[0:1], jnp.zeros((4, C), f32)]
    )

    flags = jnp.stack([pair * 0, member, tile, core]).astype(jnp.int32)
    a_high, a_low, b_high, b_low, response = prepare(
        flags, own_kernel, near, far, pass_b, norm_a, norm_b, valid, inverse[1:2]
    )
    a_high, a_low, b_high, b_low = (
        w.reshape(3, 3 * C, C) for w in (a_high, a_low, b_high, b_low)
    )
    piece = 2 * GROUPS // tiles
    response = jnp.sum(
        lax.all_to_all(response.reshape(tiles, piece, 2 * C), TILE, 0, 0), axis=0
    )
    response_share = jnp.broadcast_to(
        response.reshape(1, 2 * piece, C), (tiles, 2 * piece, C)
    )

    top, main, bottom = above[2], start, below[2]
    act = jnp.zeros((OWN, C), f32)
    grad = jnp.zeros((OWN, C), f32)
    gain = jnp.zeros((2, C), f32)
    response = None
    for step in range(pairs):
        rows = (top, main, bottom)
        masks = (pass_a, norm_a, pass_b, norm_b)
        sums = call(
            first_kernel,
            shape(tiles, 4, C),
            rows + masks + (params, a_high, a_low),
            False,
        )
        if step == 0:
            exchanged = lax.all_to_all(
                jnp.concatenate([sums, response_share], axis=1), TILE, 0, 0
            )
            received = exchanged[:, :4]
            response = exchanged[:, 4:].reshape(2 * GROUPS, 2 * C)
        else:
            received = lax.all_to_all(sums, TILE, 0, 0)
        here = jnp.stack([(pair == pairs - 1 - step).astype(jnp.int32), member, tile, core])
        main, head, tail, act, grad, gain = call(
            functools.partial(second_kernel, count),
            (
                shape(OWN, C),
                shape(2 * COLS, C),
                shape(2 * COLS, C),
                shape(OWN, C),
                shape(OWN, C),
                shape(2, C),
            ),
            (here, received, response)
            + rows
            + masks
            + (valid, params, a_high, a_low, b_high, b_low, act, grad, gain),
            True,
        )
        if step < pairs - 1:
            main, top, bottom = (
                neighbours(main, 0, 1),
                neighbours(tail, 1, 1),
                neighbours(head, -1, 1),
            )

    mine, other = call(
        functools.partial(kernel_grad_kernel, tiles),
        (shape(C // 2, 9 * C), shape(C // 2, 9 * C)),
        (flags,) + image_parts + (grad,),
        True,
    )
    share = C // tiles
    mine = mine + lax.ppermute(other, "core", swap)
    for axis in ("x", "z"):
        parts = lax.axis_size(axis)
        mine = jnp.sum(
            lax.all_to_all(mine.reshape(parts, mine.shape[0] // parts, 9 * C), axis, 0, 0), axis=0
        )
    kernel_share = jnp.transpose(mine.reshape(share, 3, 3, C), (1, 2, 3, 0))
    return (
        act.reshape(1, 1, ROWS, COLS, C),
        kernel_share[None],
        gain[None],
    )


def solution(mesh):
    sections, tiles = mesh.shape["section"], mesh.shape["tile"]
    across = 4 if tiles == 32 else 1
    finer = Mesh(
        mesh.devices.reshape(sections // 2, 2, tiles // (2 * across), across, 2), ALL
    )
    return jax.shard_map(
        on_device,
        mesh=finer,
        in_specs=(
            P(SECTION, None, TILE, None, None),
            P(SECTION, None, None, None, None),
            P(SECTION, None),
            P(SECTION, None, TILE, None, None),
            P(SECTION, None, TILE, None),
            P(SECTION, None),
            P(None, TILE, None, None),
        ),
        out_specs=(
            P(SECTION, None, TILE, None, None),
            P(SECTION, None, None, None, TILE),
            P(SECTION, None, None),
        ),
        check_vma=False,
    )
```

time: 1890 us -> 550 us (0.29)
  the two profiles are of different devices: /device:TPU:8 before, /device:TPU:48 now
where the time goes in v1:
time: 550 us; the launch traced here: 544 us
  starting transfers between devices  158 us (29%)
  local copies, waits for them, and re-layouts  157 us (29%)
  waiting for transfers between devices  129 us (23%)
  Pallas kernels  47.3 us (9%)
  blocking collectives  33.9 us (6%)
  other arithmetic  16.6 us (3%)
    unnamed x369, local copies, waits for them, and re-layouts  136 us
    all_to_all x7, waiting for transfers between devices, on_device(): received = lax.all_to_all(sums, TILE, 0, 0)  71.6 us
    all_to_all x7, starting transfers between devices, on_device(): received = lax.all_to_all(sums, TILE, 0, 0)  71.3 us
    ppermute x23, starting transfers between devices, neighbours(): lax.ppermute(value, ALL, [(i, i - jump * 2 * tiles + step) for i in range...  44.3 us
    pallas_call x18, Pallas kernels, call(): pl.pallas_call(body, out_shape=out_shape, in_specs=in_specs, out_specs=tu...  38.4 us
    all_to_all x2, blocking collectives, on_device(): lax.all_to_all(mine.reshape(parts, mine.shape[0] // parts, 9 * C), axis,...  33.9 us
    ppermute x23, waiting for transfers between devices, neighbours(): lax.ppermute(value, ALL, [(i, i - jump * 2 * tiles + step) for i in range...  28 us
    all_to_all x1, starting transfers between devices, on_device(): lax.all_to_all(jnp.broadcast_to(packed, (2 * tiles, 4, C)), ('member',) +...  15.7 us
  transfers between devices with their start and end apart: 37, of which 24 were waited for; matrix products, arithmetic and copies ran while one was open for 4% of the time, Pallas kernels for 0%

profile of v1, /device:TPU:48, one launch (start us, length us, event | category | flops | bytes accessed | tf_op | source)
XLA Modules:
  0.0 544.4 jit_solution(3755284836548696552)
XLA Ops:
  13.4 4.3 collective-permute-start.3
  25.1 15.7 %all-to-all-start = ((f32[64,4,256]{2,1,0:T(4,128)}), f32[64,4,256]{2,1,0:T(4,128)S(1)}, u32[]{:S(2)}, u32[]{:S(2)}) async-start(f32[64,4,256]{2,1,0:T(4,128)} %broadcast_in_dim.56), calls=%async_computation | async-start | bytes 524288 | tf_op jit(solution)/shard_map/all_to_all | solution.py:347
  48.9 13.6 %all-to-all-done = f32[64,4,256]{2,1,0:T(4,128)S(1)} async-done(((f32[64,4,256]{2,1,0:T(4,128)}), f32[64,4,256]{2,1,0:T(4,128)S(1)}, u32[]{:S(2)}, u32[]{:S(2)}) %all-to-all-start) | async-done | bytes 262176 | tf_op jit(solution)/shard_map/all_to_all | solution.py:347
  72.8 8.9 %shard_map.95 = (bf16[9,256,256]{2,1,0:T(8,128)(2,1)S(1)}, bf16[9,256,256]{2,1,0:T(8,128)(2,1)S(1)}, bf16[9,256,256]{2,1,0:T(8,128)(2,1)S(1)}, bf16[9,256,256]{2,1,0:T(8,128)(2,1)S(1)}, f32[64,512]{1,0:T(8,128)S(1)}) custom-call(s32[4]{0:T(128)S(1)} %add_add_fusion.8.flags, f32[9,256,256]{2,1,0:T(8,128)S(1)} %bitcast.125, f32[9,128,256]{2,1,0:T(8,128)S(1)} %copy-done.68, ...), custom_call_target="tpu_custom_call" | custom-call | tf_op jit(solution)/shard_map/pallas_call | solution.py:266
  85.0 5.0 all-to-all-start.1
  105.5 9.8 %all-to-all-start.2 = ((f32[32,8,256]{2,1,0:T(8,128)}), f32[32,8,256]{2,1,0:T(8,128)}, u32[]{:S(2)}, u32[]{:S(2)}) async-start(f32[32,8,256]{2,1,0:T(8,128)} %pad_maximum_fusion.1), calls=%async_computation.2 | async-start | bytes 524288 | tf_op jit(solution)/shard_map/all_to_all | solution.py:403
  115.4 13.5 %all-to-all-done.2 = f32[32,8,256]{2,1,0:T(8,128)} async-done(((f32[32,8,256]{2,1,0:T(8,128)}), f32[32,8,256]{2,1,0:T(8,128)}, u32[]{:S(2)}, u32[]{:S(2)}) %all-to-all-start.2) | async-done | bytes 262176 | tf_op jit(solution)/shard_map/all_to_all | solution.py:403
  161.6 10.9 %all-to-all-start.3 = ((f32[32,4,256]{2,1,0:T(4,128)}), f32[32,4,256]{2,1,0:T(4,128)}, u32[]{:S(2)}, u32[]{:S(2)}) async-start(f32[32,4,256]{2,1,0:T(4,128)} %copy-done.93), calls=%async_computation.3 | async-start | bytes 262144 | tf_op jit(solution)/shard_map/all_to_all | solution.py:409
  173.1 10.2 %all-to-all-done.3.received = f32[32,4,256]{2,1,0:T(4,128)} async-done(((f32[32,4,256]{2,1,0:T(4,128)}), f32[32,4,256]{2,1,0:T(4,128)}, u32[]{:S(2)}, u32[]{:S(2)}) %all-to-all-start.3) | async-done | bytes 131104 | tf_op jit(solution)/shard_map/all_to_all | solution.py:409
  213.6 10.5 %all-to-all-start.4 = ((f32[32,4,256]{2,1,0:T(4,128)}), f32[32,4,256]{2,1,0:T(4,128)}, u32[]{:S(2)}, u32[]{:S(2)}) async-start(f32[32,4,256]{2,1,0:T(4,128)} %copy-done.94), calls=%async_computation.4 | async-start | bytes 262144 | tf_op jit(solution)/shard_map/all_to_all | solution.py:409
  224.8 10.2 %all-to-all-done.4.received = f32[32,4,256]{2,1,0:T(4,128)} async-done(((f32[32,4,256]{2,1,0:T(4,128)}), f32[32,4,256]{2,1,0:T(4,128)}, u32[]{:S(2)}, u32[]{:S(2)}) %all-to-all-start.4) | async-done | bytes 131104 | tf_op jit(solution)/shard_map/all_to_all | solution.py:409
  265.7 10.2 %all-to-all-start.5 = ((f32[32,4,256]{2,1,0:T(4,128)}), f32[32,4,256]{2,1,0:T(4,128)}, u32[]{:S(2)}, u32[]{:S(2)}) async-start(f32[32,4,256]{2,1,0:T(4,128)} %copy-done.95), calls=%async_computation.5 | async-start | bytes 262144 | tf_op jit(solution)/shard_map/all_to_all | solution.py:409
  276.6 10.2 %all-to-all-done.5.received = f32[32,4,256]{2,1,0:T(4,128)} async-done(((f32[32,4,256]{2,1,0:T(4,128)}), f32[32,4,256]{2,1,0:T(4,128)}, u32[]{:S(2)}, u32[]{:S(2)}) %all-to-all-start.5) | async-done | bytes 131104 | tf_op jit(solution)/shard_map/all_to_all | solution.py:409
  317.0 10.4 %all-to-all-start.6 = ((f32[32,4,256]{2,1,0:T(4,128)}), f32[32,4,256]{2,1,0:T(4,128)}, u32[]{:S(2)}, u32[]{:S(2)}) async-start(f32[32,4,256]{2,1,0:T(4,128)} %copy-done.96), calls=%async_computation.6 | async-start | bytes 262144 | tf_op jit(solution)/shard_map/all_to_all | solution.py:409
  328.0 10.0 %all-to-all-done.6.received = f32[32,4,256]{2,1,0:T(4,128)} async-done(((f32[32,4,256]{2,1,0:T(4,128)}), f32[32,4,256]{2,1,0:T(4,128)}, u32[]{:S(2)}, u32[]{:S(2)}) %all-to-all-start.6) | async-done | bytes 131104 | tf_op jit(solution)/shard_map/all_to_all | solution.py:409
  367.1 10.2 %all-to-all-start.7 = ((f32[32,4,256]{2,1,0:T(4,128)}), f32[32,4,256]{2,1,0:T(4,128)}, u32[]{:S(2)}, u32[]{:S(2)}) async-start(f32[32,4,256]{2,1,0:T(4,128)} %copy-done.97), calls=%async_computation.7 | async-start | bytes 262144 | tf_op jit(solution)/shard_map/all_to_all | solution.py:409
  377.3 10.8 %all-to-all-done.7.received = f32[32,4,256]{2,1,0:T(4,128)} async-done(((f32[32,4,256]{2,1,0:T(4,128)}), f32[32,4,256]{2,1,0:T(4,128)}, u32[]{:S(2)}, u32[]{:S(2)}) %all-to-all-start.7) | async-done | bytes 131104 | tf_op jit(solution)/shard_map/all_to_all | solution.py:409
  416.8 10.0 %all-to-all-start.8 = ((f32[32,4,256]{2,1,0:T(4,128)}), f32[32,4,256]{2,1,0:T(4,128)}, u32[]{:S(2)}, u32[]{:S(2)}) async-start(f32[32,4,256]{2,1,0:T(4,128)} %copy-done.98), calls=%async_computation.8 | async-start | bytes 262144 | tf_op jit(solution)/shard_map/all_to_all | solution.py:409
  427.5 10.2 %all-to-all-done.8.received = f32[32,4,256]{2,1,0:T(4,128)} async-done(((f32[32,4,256]{2,1,0:T(4,128)}), f32[32,4,256]{2,1,0:T(4,128)}, u32[]{:S(2)}, u32[]{:S(2)}) %all-to-all-start.8) | async-done | bytes 131104 | tf_op jit(solution)/shard_map/all_to_all | solution.py:409
  467.1 9.3 %all-to-all-start.9 = ((f32[32,4,256]{2,1,0:T(4,128)}), f32[32,4,256]{2,1,0:T(4,128)}, u32[]{:S(2)}, u32[]{:S(2)}) async-start(f32[32,4,256]{2,1,0:T(4,128)} %copy-done.92), calls=%async_computation.9 | async-start | bytes 262144 | tf_op jit(solution)/shard_map/all_to_all | solution.py:409
  477.0 10.0 %all-to-all-done.9.received = f32[32,4,256]{2,1,0:T(4,128)} async-done(((f32[32,4,256]{2,1,0:T(4,128)}), f32[32,4,256]{2,1,0:T(4,128)}, u32[]{:S(2)}, u32[]{:S(2)}) %all-to-all-start.9) | async-done | bytes 131104 | tf_op jit(solution)/shard_map/all_to_all | solution.py:409
  498.7 4.5 shard_map.111
  509.8 19.7 %all_to_all.60 = f32[4,32,2304]{2,1,0:T(8,128)S(1)} all-to-all(f32[4,32,2304]{2,1,0:T(8,128)S(1)} %bitcast.131), channel_id=1, replica_groups=mesh['pair'=8,'member'=2,'x'=4,'z'=4,'core'=2] {'x'}, dimensions={0} | all-to-all | bytes 2359296 | tf_op jit(solution)/shard_map/all_to_all | solution.py:445
  529.6 14.2 %all_to_all.61 = f32[4,8,2304]{2,1,0:T(8,128)S(1)} all-to-all(f32[4,8,2304]{2,1,0:T(8,128)S(1)} %bitcast.132), channel_id=1, replica_groups=mesh['pair'=8,'member'=2,'x'=4,'z'=4,'core'=2] {'z'}, dimensions={0} | all-to-all | bytes 589824 | tf_op jit(solution)/shard_map/all_to_all | solution.py:445
  (504 shorter events, 290.0 us)
Async XLA Ops:
  5.2 14.9 %collective-permute-start.1 = (f32[112,256]{1,0:T(8,128)}, f32[112,256]{1,0:T(8,128)}, u32[]{:S(2)}, u32[]{:S(2)}) collective-permute-start(f32[112,256]{1,0:T(8,128)} %pad_maximum_fusion.4), channel_id=1, source_target_pairs={{1,0},{2,1},{3,2},{4,3},{5,4},{6,5},{7,6},{8,7},{9,8},{10,9},{11,1... | collective-permute-start | bytes 344072 | tf_op jit(solution)/shard_map/ppermute | solution.py:316
  7.2 13.7 %collective-permute-start = (f32[112,256]{1,0:T(8,128)}, f32[112,256]{1,0:T(8,128)}, u32[]{:S(2)}, u32[]{:S(2)}) collective-permute-start(f32[112,256]{1,0:T(8,128)} %pad_maximum_fusion.3), channel_id=1, source_target_pairs={{0,1},{1,2},{2,3},{3,4},{4,5},{5,6},{6,7},{7,8},{8,9},{9,10},{10,1... | collective-permute-start | bytes 344072 | tf_op jit(solution)/shard_map/ppermute | solution.py:316
  13.4 49.1 %collective-permute-start.3 = (f32[9,128,256]{2,1,0:T(8,128)}, f32[9,128,256]{2,1,0:T(8,128)S(1)}, u32[]{:S(2)}, u32[]{:S(2)}) collective-permute-start(f32[9,128,256]{2,1,0:T(8,128)} %constant_dynamic-slice_fusion), channel_id=1, source_target_pairs={{0,32},{32,0},{1,33},{33,1},{2,34},{34,2},{3,35},{35,3},{4,36},{36... | collective-permute-start | bytes 3538952 | tf_op jit(solution)/shard_map/ppermute | solution.py:304
  25.1 37.3 %all-to-all-start = ((f32[64,4,256]{2,1,0:T(4,128)}), f32[64,4,256]{2,1,0:T(4,128)S(1)}, u32[]{:S(2)}, u32[]{:S(2)}) async-start(f32[64,4,256]{2,1,0:T(4,128)} %broadcast_in_dim.56), calls=%async_computation | async-start | bytes 524288 | tf_op jit(solution)/shard_map/all_to_all | solution.py:347
  45.3 20.3 %collective-permute-start.2 = (f32[2,192,256]{2,1,0:T(8,128)}, f32[2,192,256]{2,1,0:T(8,128)}, u32[]{:S(2)}, u32[]{:S(2)}) collective-permute-start(f32[2,192,256]{2,1,0:T(8,128)} %pad_maximum_fusion), channel_id=1, source_target_pairs={{0,32},{32,0},{1,33},{33,1},{2,34},{34,2},{3,35},{35,3},{4,36},{36... | collective-permute-start | bytes 1179656 | tf_op jit(solution)/shard_map/ppermute | solution.py:345
  85.0 16.5 %all-to-all-start.1 = ((f32[32,2,512]{2,1,0:T(2,128)}), f32[32,2,512]{2,1,0:T(2,128)}, u32[]{:S(2)}, u32[]{:S(2)}) async-start(f32[32,2,512]{2,1,0:T(2,128)} %reshape.137), calls=%async_computation.1 | async-start | bytes 262144 | tf_op jit(solution)/shard_map/all_to_all | solution.py:382
  105.5 23.5 %all-to-all-start.2 = ((f32[32,8,256]{2,1,0:T(8,128)}), f32[32,8,256]{2,1,0:T(8,128)}, u32[]{:S(2)}, u32[]{:S(2)}) async-start(f32[32,8,256]{2,1,0:T(8,128)} %pad_maximum_fusion.1), calls=%async_computation.2 | async-start | bytes 524288 | tf_op jit(solution)/shard_map/all_to_all | solution.py:403
  147.2 11.2 %collective-permute-start.6 = (f32[128,256]{1,0:T(8,128)S(1)}, f32[128,256]{1,0:T(8,128)S(1)}, u32[]{:S(2)}, u32[]{:S(2)}) collective-permute-start(f32[128,256]{1,0:T(8,128)S(1)} %get-tuple-element.65), channel_id=1, source_target_pairs={{64,0},{65,1},{66,2},{67,3},{68,4},{69,5},{70,6},{71,7},{72,8},{73... | collective-permute-start | bytes 393224 | tf_op jit(solution)/shard_map/ppermute | solution.py:316
  161.6 21.7 %all-to-all-start.3 = ((f32[32,4,256]{2,1,0:T(4,128)}), f32[32,4,256]{2,1,0:T(4,128)}, u32[]{:S(2)}, u32[]{:S(2)}) async-start(f32[32,4,256]{2,1,0:T(4,128)} %copy-done.93), calls=%async_computation.3 | async-start | bytes 262144 | tf_op jit(solution)/shard_map/all_to_all | solution.py:409
  200.8 9.6 %collective-permute-start.9 = (f32[128,256]{1,0:T(8,128)S(1)}, f32[128,256]{1,0:T(8,128)S(1)}, u32[]{:S(2)}, u32[]{:S(2)}) collective-permute-start(f32[128,256]{1,0:T(8,128)S(1)} %get-tuple-element.71), channel_id=1, source_target_pairs={{64,0},{65,1},{66,2},{67,3},{68,4},{69,5},{70,6},{71,7},{72,8},{73... | collective-permute-start | bytes 393224 | tf_op jit(solution)/shard_map/ppermute | solution.py:316
  213.6 21.4 %all-to-all-start.4 = ((f32[32,4,256]{2,1,0:T(4,128)}), f32[32,4,256]{2,1,0:T(4,128)}, u32[]{:S(2)}, u32[]{:S(2)}) async-start(f32[32,4,256]{2,1,0:T(4,128)} %copy-done.94), calls=%async_computation.4 | async-start | bytes 262144 | tf_op jit(solution)/shard_map/all_to_all | solution.py:409
  251.8 10.7 %collective-permute-start.12 = (f32[128,256]{1,0:T(8,128)S(1)}, f32[128,256]{1,0:T(8,128)S(1)}, u32[]{:S(2)}, u32[]{:S(2)}) collective-permute-start(f32[128,256]{1,0:T(8,128)S(1)} %get-tuple-element.77), channel_id=1, source_target_pairs={{64,0},{65,1},{66,2},{67,3},{68,4},{69,5},{70,6},{71,7},{72,8},{73... | collective-permute-start | bytes 393224 | tf_op jit(solution)/shard_map/ppermute | solution.py:316
  257.3 5.2 collective-permute-start.13
  265.7 21.1 %all-to-all-start.5 = ((f32[32,4,256]{2,1,0:T(4,128)}), f32[32,4,256]{2,1,0:T(4,128)}, u32[]{:S(2)}, u32[]{:S(2)}) async-start(f32[32,4,256]{2,1,0:T(4,128)} %copy-done.95), calls=%async_computation.5 | async-start | bytes 262144 | tf_op jit(solution)/shard_map/all_to_all | solution.py:409
  304.2 9.5 %collective-permute-start.15 = (f32[128,256]{1,0:T(8,128)S(1)}, f32[128,256]{1,0:T(8,128)S(1)}, u32[]{:S(2)}, u32[]{:S(2)}) collective-permute-start(f32[128,256]{1,0:T(8,128)S(1)} %get-tuple-element.83), channel_id=1, source_target_pairs={{64,0},{65,1},{66,2},{67,3},{68,4},{69,5},{70,6},{71,7},{72,8},{73... | collective-permute-start | bytes 393224 | tf_op jit(solution)/shard_map/ppermute | solution.py:316
  317.0 21.0 %all-to-all-start.6 = ((f32[32,4,256]{2,1,0:T(4,128)}), f32[32,4,256]{2,1,0:T(4,128)}, u32[]{:S(2)}, u32[]{:S(2)}) async-start(f32[32,4,256]{2,1,0:T(4,128)} %copy-done.96), calls=%async_computation.6 | async-start | bytes 262144 | tf_op jit(solution)/shard_map/all_to_all | solution.py:409
  354.8 9.1 %collective-permute-start.18 = (f32[128,256]{1,0:T(8,128)S(1)}, f32[128,256]{1,0:T(8,128)S(1)}, u32[]{:S(2)}, u32[]{:S(2)}) collective-permute-start(f32[128,256]{1,0:T(8,128)S(1)} %get-tuple-element.89), channel_id=1, source_target_pairs={{64,0},{65,1},{66,2},{67,3},{68,4},{69,5},{70,6},{71,7},{72,8},{73... | collective-permute-start | bytes 393224 | tf_op jit(solution)/shard_map/ppermute | solution.py:316
  367.1 21.0 %all-to-all-start.7 = ((f32[32,4,256]{2,1,0:T(4,128)}), f32[32,4,256]{2,1,0:T(4,128)}, u32[]{:S(2)}, u32[]{:S(2)}) async-start(f32[32,4,256]{2,1,0:T(4,128)} %copy-done.97), calls=%async_computation.7 | async-start | bytes 262144 | tf_op jit(solution)/shard_map/all_to_all | solution.py:409
  404.9 8.7 %collective-permute-start.21 = (f32[128,256]{1,0:T(8,128)S(1)}, f32[128,256]{1,0:T(8,128)S(1)}, u32[]{:S(2)}, u32[]{:S(2)}) collective-permute-start(f32[128,256]{1,0:T(8,128)S(1)} %get-tuple-element.95), channel_id=1, source_target_pairs={{64,0},{65,1},{66,2},{67,3},{68,4},{69,5},{70,6},{71,7},{72,8},{73... | collective-permute-start | bytes 393224 | tf_op jit(solution)/shard_map/ppermute | solution.py:316
  408.2 5.4 collective-permute-start.22
  416.8 20.9 %all-to-all-start.8 = ((f32[32,4,256]{2,1,0:T(4,128)}), f32[32,4,256]{2,1,0:T(4,128)}, u32[]{:S(2)}, u32[]{:S(2)}) async-start(f32[32,4,256]{2,1,0:T(4,128)} %copy-done.98), calls=%async_computation.8 | async-start | bytes 262144 | tf_op jit(solution)/shard_map/all_to_all | solution.py:409
  455.1 8.7 %collective-permute-start.24 = (f32[128,256]{1,0:T(8,128)S(1)}, f32[128,256]{1,0:T(8,128)S(1)}, u32[]{:S(2)}, u32[]{:S(2)}) collective-permute-start(f32[128,256]{1,0:T(8,128)S(1)} %get-tuple-element.101), channel_id=1, source_target_pairs={{64,0},{65,1},{66,2},{67,3},{68,4},{69,5},{70,6},{71,7},{72,8},{73... | collective-permute-start | bytes 393224 | tf_op jit(solution)/shard_map/ppermute | solution.py:316
  458.4 5.5 %collective-permute-start.25 = (f32[32,256]{1,0:T(8,128)S(1)}, f32[32,256]{1,0:T(8,128)S(1)}, u32[]{:S(2)}, u32[]{:S(2)}) collective-permute-start(f32[32,256]{1,0:T(8,128)S(1)} %get-tuple-element.102), channel_id=1, source_target_pairs={{65,0},{66,1},{67,2},{68,3},{69,4},{70,5},{71,6},{72,7},{73,8},{74... | collective-permute-start | bytes 98312 | tf_op jit(solution)/shard_map/ppermute | solution.py:316
  467.1 19.9 %all-to-all-start.9 = ((f32[32,4,256]{2,1,0:T(4,128)}), f32[32,4,256]{2,1,0:T(4,128)}, u32[]{:S(2)}, u32[]{:S(2)}) async-start(f32[32,4,256]{2,1,0:T(4,128)} %copy-done.92), calls=%async_computation.9 | async-start | bytes 262144 | tf_op jit(solution)/shard_map/all_to_all | solution.py:409
  (197 other events, 404.8 us)

commit v2 on v1

--- a/solution.py
+++ b/solution.py
@@ -82,7 +82,7 @@
     return jnp.sum(values, axis=0, keepdims=True)
 
 
-def forward_kernel(top, main, bottom, kernel, conv_out, sums):
+def forward_kernel(top, main, bottom, kernel, gamma, conv_out, sums):
     image = jnp.concatenate([top[...], main[...], bottom[...]], axis=0)
     count = image.shape[0] - 2 * COLS
     total = None
@@ -97,16 +97,61 @@
             total = part if total is None else total + part
     conv_out[...] = total
     own = total[2 * COLS : 2 * COLS + OWN]
-    sums[...] = jnp.concatenate([column_sum(own), column_sum(own * own)], axis=0)
+    block = jnp.concatenate(
+        [column_sum(own), column_sum(own * own), gamma[...], jnp.zeros((1, C), f32)], axis=0
+    )
+    sums[...] = jnp.broadcast_to(folded(block)[None], sums.shape)
 
 
 def prepare_kernel(
-    flags, own, near, far, pass_b, norm_a, norm_b, valid, scale,
-    a_high, a_low, b_high, b_low, response, weight_scr, flat_scr, full_scr,
+    tiles, count, flags, own, near, far, gathered, fields, partner_fields,
+    a_high, a_low, b_high, b_low, pass_a, norm_a, pass_b, norm_b, params, response,
+    high_scr, low_scr, field_scr, flat_scr, full_scr,
 ):
     tap = pl.program_id(0)
     core = flags[3]
     member = flags[1]
+
+    @pl.when(tap == 0)
+    def _():
+        stats = gathered[...].reshape(2, tiles, 8, C // 2)
+        groups, spread = group_matrix(), spread_matrix()
+        inside = inside_rows(flags, tiles)
+
+        def section(which, conv_out, passing, pass_ref, norm_ref, row):
+            block = jnp.sum(stats[which], axis=0)
+            totals = jnp.concatenate([block[0:2], block[4:6]], axis=1)
+            gamma = jnp.concatenate([stats[which, 0, 2:3], stats[which, 0, 6:7]], axis=1)
+            grouped = dot(totals, groups, highest) * (1.0 / count)
+            mean = grouped[0:1]
+            inverse = lax.rsqrt(grouped[1:2] - mean * mean + eps)
+            wide = dot(jnp.concatenate([mean, inverse], axis=0), spread, highest)
+            mean, inverse = wide[0:1], wide[1:2]
+            pass_ref[...] = passing
+            norm_ref[...] = (conv_out - mean) * inverse * inside
+            params[row : row + 1, :] = gamma
+            params[row + 1 : row + 2, :] = inverse
+
+        upper = member == 1
+        mine, other = fields[0], partner_fields[0]
+        my_pass, other_pass = fields[1], partner_fields[1]
+        section(1, jnp.where(upper, mine, other), jnp.where(upper, my_pass, other_pass),
+                pass_a, norm_a, 0)
+        section(0, jnp.where(upper, other, mine), jnp.where(upper, other_pass, my_pass),
+                pass_b, norm_b, 2)
+        params[4:8, :] = jnp.zeros((4, C), f32)
+        passing = pass_b[2 * COLS : 2 * COLS + OWN]
+        normed = norm_b[2 * COLS : 2 * COLS + OWN]
+        high, low = split(jnp.concatenate([passing.T, (passing * normed).T], axis=0))
+        high_scr[...] = high
+        low_scr[...] = low
+        both = jnp.concatenate([norm_a[...], inside[:, : C // 2]], axis=1)
+        field_scr[0] = shifted(both, 1)
+        field_scr[1] = both
+        field_scr[2] = shifted(both, -1)
+        flat_scr[...] = jnp.zeros_like(flat_scr)
+        full_scr[...] = jnp.zeros_like(full_scr)
+
     near_tap, far_tap = near[0], far[0]
     partner = jnp.concatenate(
         [jnp.where(core == 0, near_tap, far_tap), jnp.where(core == 0, far_tap, near_tap)], axis=0
@@ -120,78 +165,95 @@
     b_high[0] = high
     b_low[0] = low
 
-    @pl.when(tap == 0)
-    def _():
-        passing = pass_b[2 * COLS : 2 * COLS + OWN]
-        normed = norm_b[2 * COLS : 2 * COLS + OWN]
-        weight_scr[...] = jnp.concatenate([passing.T, (passing * normed).T], axis=0)
-        flat_scr[...] = jnp.zeros_like(flat_scr)
-        full_scr[...] = jnp.zeros_like(full_scr)
-
     row_tap = tap // 3
     col_tap = tap - row_tap * 3
     begin = pl.multiple_of((3 - row_tap) * COLS, COLS)
-    fields = jnp.concatenate(
-        [norm_a[pl.ds(begin, OWN), :], valid[pl.ds(begin, OWN), :]], axis=1
-    )
-    moved = jnp.where(
-        col_tap == 1,
-        fields,
-        jnp.where(col_tap == 0, shifted(fields, 1), shifted(fields, -1)),
-    )
-    moment = dot3(split(weight_scr[...]), split(moved))
-    both = jnp.concatenate([kernel_a, kernel_a], axis=0)
-    full_scr[...] += moment[:, :C] * both
-    flat_scr[...] += moment[:, C : C + 1] * both
+    moved = split(field_scr[col_tap, pl.ds(begin, OWN), :])
+    moment = dot3((high_scr[...], low_scr[...]), moved)
+    full_scr[:C, :] += moment[:C, :C] * kernel_a
+    full_scr[C:, :] += moment[C:, :C] * kernel_a
+    flat_scr[:C, :] += moment[:C, C : C + 1] * kernel_a
+    flat_scr[C:, :] += moment[C:, C : C + 1] * kernel_a
 
     @pl.when(tap == 8)
     def _():
         groups = group_matrix()
         contract = (((0,), (1,)), ((), ()))
         for index, scratch in enumerate((flat_scr, full_scr)):
-            response[GROUPS * index : GROUPS * (index + 1), :] = lax.dot_general(
-                groups, scratch[...] * scale[...], contract,
+            part = lax.dot_general(
+                groups, scratch[...] * params[1:2, :], contract,
                 preferred_element_type=f32, precision=highest,
             )
-
-
-def first_kernel(top, main, bottom, pass_a, norm_a, pass_b, norm_b, params, a_high, a_low, sums):
-    incoming = jnp.concatenate([top[...], main[...], bottom[...]], axis=0)
-    grad_out = incoming * pass_a[...]
+            for chunk in range(4):
+                response[:, index * 4 + chunk, :] = part[:, chunk * 128 : (chunk + 1) * 128]
+
+
+def inside_rows(flags, tiles):
+    row = lax.broadcasted_iota(jnp.int32, (12 * COLS, C), 0)
+    first = jnp.where(flags[2] == 0, 2 * COLS, 0)
+    last = jnp.where(flags[2] == tiles - 1, 10 * COLS, 12 * COLS)
+    return jnp.where((row >= first) & (row < last), 1.0, 0.0).astype(f32)
+
+
+def folded(values):
+    return jnp.concatenate([values[:, : C // 2], values[:, C // 2 :]], axis=0)
+
+
+def first_sums(main, pass_a, norm_a, pass_b, norm_b, params, a_high, a_low):
     own = slice(2 * COLS, 2 * COLS + OWN)
-    scaled = grad_out[COLS:-COLS] * (params[0:1, :] * params[1:2, :])
-    rest = incoming[own] + conv_back(scaled, a_high, a_low)
-    grad_b = rest * pass_b[own, :]
-    parts = jnp.concatenate(
-        [
-            column_sum(grad_out[own]),
-            column_sum(grad_out[own] * norm_a[own, :]),
-            column_sum(grad_b),
-            column_sum(grad_b * norm_b[own, :]),
-        ],
-        axis=0,
-    )
+    incoming = main[...]
+    grad_out = incoming * pass_a[own, :]
+    blank = jnp.zeros((2 * COLS, C), f32)
+    scaled = jnp.concatenate([blank, grad_out * (params[0:1, :] * params[1:2, :]), blank], axis=0)
+    spread = conv_back(scaled, a_high, a_low) * pass_b[COLS:-COLS, :]
+    straight = incoming * pass_b[own, :]
+    return folded(
+        jnp.concatenate(
+            [
+                column_sum(grad_out),
+                column_sum(grad_out * norm_a[own, :]),
+                column_sum(spread) + column_sum(straight),
+                column_sum(spread * norm_b[COLS:-COLS, :])
+                + column_sum(straight * norm_b[own, :]),
+            ],
+            axis=0,
+        )
+    )
+
+
+def first_kernel(main, pass_a, norm_a, pass_b, norm_b, params, a_high, a_low, sums):
+    parts = first_sums(main, pass_a, norm_a, pass_b, norm_b, params, a_high, a_low)
     sums[...] = jnp.broadcast_to(parts[None], sums.shape)
 
 
+def opening_kernel(share, main, pass_a, norm_a, pass_b, norm_b, params, a_high, a_low, sums):
+    parts = first_sums(main, pass_a, norm_a, pass_b, norm_b, params, a_high, a_low)
+    parts = jnp.concatenate([parts, jnp.sum(share[...], axis=0)], axis=0)
+    sums[...] = jnp.broadcast_to(parts[None], sums.shape)
+
+
 def second_kernel(
-    count, flags, received, response, top, main, bottom, pass_a, norm_a, pass_b, norm_b, valid,
+    count, tiles, step, flags, received, exchanged, top, main, bottom, pass_a, norm_a, pass_b, norm_b,
     params, a_high, a_low, b_high, b_low, old_act, old_grad, old_gain,
     out, out_head, out_tail, act, grad, gain,
 ):
     incoming = jnp.concatenate([top[...], main[...], bottom[...]], axis=0)
     gamma_a, inverse_a, gamma_b, inverse_b = (params[i : i + 1, :] for i in range(4))
-    totals = jnp.sum(received[...], axis=0)
+    totals = jnp.sum(received[:, :8, :], axis=0)
+    totals = jnp.concatenate([totals[:4], totals[4:]], axis=1)
+    response = exchanged[:, 8:, :].reshape(GROUPS, 8, C // 2)
+    flat, full = (
+        jnp.concatenate([response[:, start + chunk, :] for chunk in range(4)], axis=1)
+        for start in (0, 4)
+    )
     groups, spread = group_matrix(), spread_matrix()
     means_a = dot(totals[0:2] * gamma_a, groups, highest) * (1.0 / count)
-    shift = dot(means_a[0:1], response[:GROUPS, :], highest) + dot(
-        means_a[1:2], response[GROUPS:, :], highest
-    )
+    shift = dot(means_a[0:1], flat, highest) + dot(means_a[1:2], full, highest)
     totals_b = totals[2:4] - jnp.concatenate([shift[:, :C], shift[:, C:]], axis=0)
     means_b = dot(totals_b * gamma_b, groups, highest) * (1.0 / count)
     wide_a = dot(means_a, spread, highest)
     wide_b = dot(means_b, spread, highest)
-    inside = jnp.concatenate([valid[...], valid[...]], axis=1)
+    inside = inside_rows(flags, tiles)
     grad_a = inverse_a * (
         incoming * pass_a[...] * gamma_a - inside * wide_a[0:1] - norm_a[...] * wide_a[1:2]
     )
@@ -205,7 +267,7 @@
     out[...] = last
     out_head[...] = last[: 2 * COLS]
     out_tail[...] = last[-2 * COLS :]
-    active = flags[0] == 1
+    active = flags[0] == step
     upper = flags[1] == 1
     act[...] = jnp.where(
         active, jnp.where(upper, middle[COLS:-COLS], last), old_act[...]
@@ -260,34 +322,37 @@
     return jax.ShapeDtypeStruct(dims, dtype)
 
 
-def prepare(flags, kernel, near, far, pass_b, norm_a, norm_b, valid, scale):
+def prepare(tiles, count, flags, kernel, near, far, gathered, fields, partner_fields):
     tap = lambda rows: pl.BlockSpec((1, rows, C), lambda i: (i, 0, 0))
-    whole = lambda a: pl.BlockSpec(a.shape, lambda i: (0,) * a.ndim)
+    whole = lambda *dims: pl.BlockSpec(dims, lambda i: (0,) * len(dims))
+    tall = 12 * COLS
     return pl.pallas_call(
-        prepare_kernel,
+        functools.partial(prepare_kernel, tiles, count),
         grid=(9,),
         out_shape=tuple(shape(9, C, C, dtype=bf16) for _ in range(4))
-        + (shape(2 * GROUPS, 2 * C),),
+        + tuple(shape(tall, C) for _ in range(4))
+        + (shape(8, C), shape(GROUPS, 8, C // 2)),
         in_specs=[
             pl.BlockSpec(memory_space=pltpu.SMEM),
             tap(C),
             tap(C // 2),
             tap(C // 2),
-            whole(pass_b),
-            whole(norm_a),
-            whole(norm_b),
-            whole(valid),
-            whole(scale),
+            whole(*gathered.shape),
+            whole(*fields.shape),
+            whole(*fields.shape),
         ],
         out_specs=tuple(tap(C) for _ in range(4))
-        + (pl.BlockSpec((2 * GROUPS, 2 * C), lambda i: (0, 0)),),
+        + tuple(whole(tall, C) for _ in range(4))
+        + (whole(8, C), whole(GROUPS, 8, C // 2)),
         scratch_shapes=[
-            pltpu.VMEM((2 * C, OWN), f32),
+            pltpu.VMEM((2 * C, OWN), bf16),
+            pltpu.VMEM((2 * C, OWN), bf16),
+            pltpu.VMEM((3, tall, C + C // 2), f32),
             pltpu.VMEM((2 * C, C), f32),
             pltpu.VMEM((2 * C, C), f32),
         ],
         compiler_params=pltpu.CompilerParams(vmem_limit_bytes=40 * 2**20),
-    )(flags, kernel, near, far, pass_b, norm_a, norm_b, valid, scale)
+    )(flags, kernel, near, far, gathered, fields, partner_fields)
 
 
 def on_device(acts, kernels, gammas, pass_mask, drop_mask, path_mask, cotangent):
@@ -302,7 +367,6 @@
     own_kernel = kernels[0].reshape(9, C, C)
     half = lax.dynamic_slice_in_dim(own_kernel, core * (C // 2), C // 2, axis=1)
     near = lax.ppermute(half, "member", swap)
-    far = lax.ppermute(near, "core", swap)
 
     passing = (
         pass_mask[0, 0].astype(f32)
@@ -337,79 +401,46 @@
     tall = 12 * COLS
     conv_out, sums = call(
         forward_kernel,
-        (shape(tall, C), shape(2, C)),
-        image_parts + (own_kernel,),
+        (shape(tall, C), shape(2 * tiles, 8, C // 2)),
+        image_parts + (own_kernel, gammas),
         False,
     )
     fields = jnp.stack([conv_out, passing])
     partner_fields = lax.ppermute(fields, "member", swap)
-    packed = jnp.concatenate([sums, gammas, jnp.zeros((1, C), f32)])
-    gathered = lax.all_to_all(
-        jnp.broadcast_to(packed, (2 * tiles, 4, C)), ("member",) + TILE, 0, 0
-    ).reshape(2, tiles, 4, C)
-    totals = jnp.sum(gathered[:, :, :2], axis=1)
-    gamma_both = gathered[:, 0, 2]
-    group_totals = jnp.sum(totals.reshape(2, 2, GROUPS, C // GROUPS), axis=3) / count
-    mean = group_totals[:, 0]
-    inverse = lax.rsqrt(group_totals[:, 1] - mean * mean + eps)
-    mean = jnp.repeat(mean, C // GROUPS, axis=1)
-    inverse = jnp.repeat(inverse, C // GROUPS, axis=1)
-    row = jnp.arange(tall, dtype=jnp.int32)[:, None]
-    inside = ((tile > 0) | (row >= 2 * COLS)) & ((tile < tiles - 1) | (row < 10 * COLS))
-    valid = jnp.broadcast_to(inside.astype(f32), (tall, C // 2))
-    inside = inside.astype(f32)
-
-    upper = member == 1
-    conv_a = jnp.where(upper, fields[0], partner_fields[0])
-    conv_b = jnp.where(upper, partner_fields[0], fields[0])
-    pass_a = jnp.where(upper, fields[1], partner_fields[1])
-    pass_b = jnp.where(upper, partner_fields[1], fields[1])
-    norm_a = (conv_a - mean[1:2]) * inverse[1:2] * inside
-    norm_b = (conv_b - mean[0:1]) * inverse[0:1] * inside
-    params = jnp.concatenate(
-        [gamma_both[1:2], inverse[1:2], gamma_both[0:1], inverse[0:1], jnp.zeros((4, C), f32)]
-    )
-
-    flags = jnp.stack([pair * 0, member, tile, core]).astype(jnp.int32)
-    a_high, a_low, b_high, b_low, response = prepare(
-        flags, own_kernel, near, far, pass_b, norm_a, norm_b, valid, inverse[1:2]
-    )
-    a_high, a_low, b_high, b_low = (
-        w.reshape(3, 3 * C, C) for w in (a_high, a_low, b_high, b_low)
-    )
-    piece = 2 * GROUPS // tiles
-    response = jnp.sum(
-        lax.all_to_all(response.reshape(tiles, piece, 2 * C), TILE, 0, 0), axis=0
-    )
-    response_share = jnp.broadcast_to(
-        response.reshape(1, 2 * piece, C), (tiles, 2 * piece, C)
-    )
+    near, sums = lax.optimization_barrier((near, sums))
+    far = lax.ppermute(near, "core", swap)
+    far, partner_fields, sums = lax.optimization_barrier((far, partner_fields, sums))
+    gathered = lax.all_to_all(sums, ("member",) + TILE, 0, 0)
+    flags = jnp.stack([pairs - 1 - pair, member, tile, core]).astype(jnp.int32)
+    prepared = prepare(
+        tiles, count, flags, own_kernel, near, far, gathered, fields, partner_fields
+    )
+    a_high, a_low, b_high, b_low = (w.reshape(3, 3 * C, C) for w in prepared[:4])
+    masks, params, response = prepared[4:8], prepared[8], prepared[9]
+    piece = GROUPS // tiles
+    response = lax.all_to_all(response.reshape(tiles, piece * 8, C // 2), TILE, 0, 0)
 
     top, main, bottom = above[2], start, below[2]
     act = jnp.zeros((OWN, C), f32)
     grad = jnp.zeros((OWN, C), f32)
     gain = jnp.zeros((2, C), f32)
-    response = None
+    exchanged = None
     for step in range(pairs):
-        rows = (top, main, bottom)
-        masks = (pass_a, norm_a, pass_b, norm_b)
-        sums = call(
-            first_kernel,
-            shape(tiles, 4, C),
-            rows + masks + (params, a_high, a_low),
-            False,
-        )
+        shared = masks + (params, a_high, a_low)
         if step == 0:
-            exchanged = lax.all_to_all(
-                jnp.concatenate([sums, response_share], axis=1), TILE, 0, 0
+            sums = call(
+                opening_kernel,
+                shape(tiles, 8 + piece * 8, C // 2),
+                (response, main) + shared,
+                False,
             )
-            received = exchanged[:, :4]
-            response = exchanged[:, 4:].reshape(2 * GROUPS, 2 * C)
+            received = exchanged = lax.all_to_all(sums, TILE, 0, 0)
         else:
+            sums = call(first_kernel, shape(tiles, 8, C // 2), (main,) + shared, False)
+            sums, top, bottom = lax.optimization_barrier((sums, top, bottom))
             received = lax.all_to_all(sums, TILE, 0, 0)
-        here = jnp.stack([(pair == pairs - 1 - step).astype(jnp.int32), member, tile, core])
         main, head, tail, act, grad, gain = call(
-            functools.partial(second_kernel, count),
+            functools.partial(second_kernel, count, tiles, step),
             (
                 shape(OWN, C),
                 shape(2 * COLS, C),
@@ -418,10 +449,9 @@
                 shape(OWN, C),
                 shape(2, C),
             ),
-            (here, received, response)
-            + rows
-            + masks
-            + (valid, params, a_high, a_low, b_high, b_low, act, grad, gain),
+            (flags, received, exchanged, top, main, bottom)
+            + shared
+            + (b_high, b_low, act, grad, gain),
             True,
         )
         if step < pairs - 1:

time: 550 us -> 409 us (0.74)
  blocking collectives: 33.9 us -> 209 us
  local copies, waits for them, and re-layouts: 157 us -> 7.39 us
  starting transfers between devices: 158 us -> 73.1 us
  waiting for transfers between devices: 129 us -> 66.7 us
  other arithmetic: 16.6 us -> 2.82 us
    all_to_all x0 -> x9, blocking collectives: none -> 175 us  [the longest x7 144 us: on_device(): received = lax.all_to_all(sums, TILE, 0, 0)]
    unnamed x369 -> x24, local copies, waits for them, and re-layouts: 136 us -> 4.72 us
    all_to_all x10 -> x1, starting transfers between devices: 102 us -> 11.6 us  [on_device(): gathered = lax.all_to_all(sums, ('member',) + TILE, 0, 0)]
    all_to_all x10 -> x1, waiting for transfers between devices: 98.7 us -> 14 us  [on_device(): gathered = lax.all_to_all(sums, ('member',) + TILE, 0, 0)]
    ppermute x1, waiting for transfers between devices: 0.01 us -> 14.9 us  [on_device(): near = lax.ppermute(half, 'member', swap)]
    ppermute x1, waiting for transfers between devices: 0.01 us -> 9.28 us  [on_device(): partner_fields = lax.ppermute(fields, 'member', swap)]
  transfers between devices with their start and end apart: 37 -> 28, of which waited for: 24 -> 16; matrix products, arithmetic and copies ran while one was open for 4% -> 0% of each run, Pallas kernels for 0% -> 2%
where the time goes in v2:
time: 409 us; the launch traced here: 407 us
  blocking collectives  209 us (51%)
  starting transfers between devices  73.1 us (18%)
  waiting for transfers between devices  66.7 us (16%)
  Pallas kernels  46.6 us (11%)
  local copies, waits for them, and re-layouts  7.39 us (2%)
    all_to_all x7, blocking collectives, on_device(): received = lax.all_to_all(sums, TILE, 0, 0)  144 us
    ppermute x23, starting transfers between devices, neighbours(): lax.ppermute(value, ALL, [(i, i - jump * 2 * tiles + step) for i in range...  44.7 us
    pallas_call x18, Pallas kernels, call(): pl.pallas_call(body, out_shape=out_shape, in_specs=in_specs, out_specs=tu...  37.3 us
    all_to_all x2, blocking collectives, on_device(): lax.all_to_all(mine.reshape(parts, mine.shape[0] // parts, 9 * C), axis,...  33.9 us
    ppermute x23, waiting for transfers between devices, neighbours(): lax.ppermute(value, ALL, [(i, i - jump * 2 * tiles + step) for i in range...  26 us
    all_to_all x1, blocking collectives, on_device(): received = exchanged = lax.all_to_all(sums, TILE, 0, 0)  16.8 us
    ppermute x1, waiting for transfers between devices, on_device(): near = lax.ppermute(half, 'member', swap)  14.9 us
    all_to_all x1, blocking collectives, on_device(): lax.all_to_all(response.reshape(tiles, piece * 8, C // 2), TILE, 0, 0)  14 us
  transfers between devices with their start and end apart: 28, of which 16 were waited for; matrix products, arithmetic and copies ran while one was open for 0% of the time, Pallas kernels for 2%

profile of v2, /device:TPU:48, one launch (start us, length us, event | category | flops | bytes accessed | tf_op | source)
XLA Modules:
  0.0 407.2 jit_solution(7769951040520408147)
XLA Ops:
  3.2 4.4 %collective-permute-start = (f32[9,128,256]{2,1,0:T(8,128)}, f32[9,128,256]{2,1,0:T(8,128)}, u32[]{:S(2)}, u32[]{:S(2)}) collective-permute-start(f32[9,128,256]{2,1,0:T(8,128)} %constant_dynamic-slice_fusion), channel_id=1, source_target_pairs={{0,32},{32,0},{1,33},{33,1},{2,34},{34,2},{3,35},{35,3},{4,36},{36... | collective-permute-start | bytes 3538952 | tf_op jit(solution)/shard_map/ppermute | solution.py:369
  12.9 6.1 %collective-permute-done.2 = f32[112,256]{1,0:T(8,128)S(1)} collective-permute-done((f32[112,256]{1,0:T(8,128)S(1)}, f32[112,256]{1,0:T(8,128)S(1)}, u32[]{:S(2)}, u32[]{:S(2)}) %collective-permute-start.2) | collective-permute-done | bytes 114720 | tf_op jit(solution)/shard_map/ppermute | solution.py:380
  20.6 14.9 %collective-permute-done.near = f32[9,128,256]{2,1,0:T(8,128)} collective-permute-done((f32[9,128,256]{2,1,0:T(8,128)}, f32[9,128,256]{2,1,0:T(8,128)}, u32[]{:S(2)}, u32[]{:S(2)}) %collective-permute-start) | collective-permute-done | bytes 1179680 | tf_op jit(solution)/shard_map/ppermute | solution.py:369
  35.5 3.7 collective-permute-start.3
  39.4 6.5 %collective-permute-start.4 = (f32[2,192,256]{2,1,0:T(8,128)S(1)}, f32[2,192,256]{2,1,0:T(8,128)S(1)}, u32[]{:S(2)}, u32[]{:S(2)}) collective-permute-start(f32[2,192,256]{2,1,0:T(8,128)S(1)} %pad_maximum_fusion.fields), channel_id=1, source_target_pairs={{0,32},{32,0},{1,33},{33,1},{2,34},{34,2},{3,35},{35,3},{4,36},{36... | collective-permute-start | bytes 1179656 | tf_op jit(solution)/shard_map/ppermute | solution.py:409
  45.9 9.3 %collective-permute-done.4.partner_fields = f32[2,192,256]{2,1,0:T(8,128)S(1)} collective-permute-done((f32[2,192,256]{2,1,0:T(8,128)S(1)}, f32[2,192,256]{2,1,0:T(8,128)S(1)}, u32[]{:S(2)}, u32[]{:S(2)}) %collective-permute-start.4) | collective-permute-done | bytes 393248 | tf_op jit(solution)/shard_map/ppermute | solution.py:409
  56.9 11.6 %all-to-all-start = ((f32[64,8,128]{2,1,0:T(8,128)}), f32[64,8,128]{2,1,0:T(8,128)S(1)}, u32[]{:S(2)}, u32[]{:S(2)}) async-start(f32[64,8,128]{2,1,0:T(8,128)} %copy-done.7), calls=%async_computation | async-start | bytes 524288 | tf_op jit(solution)/shard_map/all_to_all | solution.py:413
  68.6 14.0 %all-to-all-done.gathered = f32[64,8,128]{2,1,0:T(8,128)S(1)} async-done(((f32[64,8,128]{2,1,0:T(8,128)}), f32[64,8,128]{2,1,0:T(8,128)S(1)}, u32[]{:S(2)}, u32[]{:S(2)}) %all-to-all-start) | async-done | bytes 262176 | tf_op jit(solution)/shard_map/all_to_all | solution.py:413
  84.9 9.4 %shard_map.95 = (bf16[9,256,256]{2,1,0:T(8,128)(2,1)S(1)}, bf16[9,256,256]{2,1,0:T(8,128)(2,1)S(1)}, bf16[9,256,256]{2,1,0:T(8,128)(2,1)S(1)}, bf16[9,256,256]{2...) custom-call(s32[4]{0:T(128)S(1)} %pad_add_fusion.flags, ...), custom_call_target="tpu_custom_call" | custom-call | tf_op jit(solution)/shard_map/pallas_call | solution.py:329
  94.2 14.0 %all_to_all.60.share = f32[32,8,128]{2,1,0:T(8,128)S(1)} all-to-all(f32[32,8,128]{2,1,0:T(8,128)S(1)} %get-tuple-element.95), channel_id=1, replica_groups=mesh['pair'=8,'member'=2,'x'=4,'z'=4,'core'=2] {'x','z','core'}, dimensions={0} | all-to-all | bytes 262144 | tf_op jit(solution)/shard_map/all_to_all | solution.py:421
  109.0 16.8 %all_to_all.61.received.exchanged = f32[32,16,128]{2,1,0:T(8,128)S(1)} all-to-all(f32[32,16,128]{2,1,0:T(8,128)S(1)} %shard_map.96), channel_id=1, replica_groups=mesh['pair'=8,'member'=2,'x'=4,'z'=4,'core'=2] {'x','z','core'}, dimensions={0} | all-to-all | bytes 524288 | tf_op jit(solution)/shard_map/all_to_all | solution.py:437
  140.5 21.3 %all_to_all.62.received = f32[32,8,128]{2,1,0:T(8,128)S(1)} all-to-all(f32[32,8,128]{2,1,0:T(8,128)S(1)} %shard_map.98), channel_id=1, replica_groups=mesh['pair'=8,'member'=2,'x'=4,'z'=4,'core'=2] {'x','z','core'}, dimensions={0} | all-to-all | bytes 262144 | tf_op jit(solution)/shard_map/all_to_all | solution.py:441
  168.9 4.6 %collective-permute-start.9 = (f32[32,256]{1,0:T(8,128)S(1)}, f32[32,256]{1,0:T(8,128)S(1)}, u32[]{:S(2)}, u32[]{:S(2)}) collective-permute-start(f32[32,256]{1,0:T(8,128)S(1)} %get-tuple-element.115), channel_id=1, source_target_pairs={{64,1},{65,2},{66,3},{67,4},{68,5},{69,6},{70,7},{71,8},{72,9},{73... | collective-permute-start | bytes 98312 | tf_op jit(solution)/shard_map/ppermute | solution.py:380
  174.9 20.2 %all_to_all.63.received = f32[32,8,128]{2,1,0:T(8,128)S(1)} all-to-all(f32[32,8,128]{2,1,0:T(8,128)S(1)} %shard_map.100), channel_id=1, replica_groups=mesh['pair'=8,'member'=2,'x'=4,'z'=4,'core'=2] {'x','z','core'}, dimensions={0} | all-to-all | bytes 262144 | tf_op jit(solution)/shard_map/all_to_all | solution.py:441
  198.6 3.5 collective-permute-start.11
  209.1 21.2 %all_to_all.64.received = f32[32,8,128]{2,1,0:T(8,128)S(1)} all-to-all(f32[32,8,128]{2,1,0:T(8,128)S(1)} %shard_map.102), channel_id=1, replica_groups=mesh['pair'=8,'member'=2,'x'=4,'z'=4,'core'=2] {'x','z','core'}, dimensions={0} | all-to-all | bytes 262144 | tf_op jit(solution)/shard_map/all_to_all | solution.py:441
  243.5 20.7 %all_to_all.65.received = f32[32,8,128]{2,1,0:T(8,128)S(1)} all-to-all(f32[32,8,128]{2,1,0:T(8,128)S(1)} %shard_map.104), channel_id=1, replica_groups=mesh['pair'=8,'member'=2,'x'=4,'z'=4,'core'=2] {'x','z','core'}, dimensions={0} | all-to-all | bytes 262144 | tf_op jit(solution)/shard_map/all_to_all | solution.py:441
  276.7 20.7 %all_to_all.66.received = f32[32,8,128]{2,1,0:T(8,128)S(1)} all-to-all(f32[32,8,128]{2,1,0:T(8,128)S(1)} %shard_map.106), channel_id=1, replica_groups=mesh['pair'=8,'member'=2,'x'=4,'z'=4,'core'=2] {'x','z','core'}, dimensions={0} | all-to-all | bytes 262144 | tf_op jit(solution)/shard_map/all_to_all | solution.py:441
  309.7 20.3 %all_to_all.67.received = f32[32,8,128]{2,1,0:T(8,128)S(1)} all-to-all(f32[32,8,128]{2,1,0:T(8,128)S(1)} %shard_map.108), channel_id=1, replica_groups=mesh['pair'=8,'member'=2,'x'=4,'z'=4,'core'=2] {'x','z','core'}, dimensions={0} | all-to-all | bytes 262144 | tf_op jit(solution)/shard_map/all_to_all | solution.py:441
  338.0 3.5 collective-permute-done.23.main
  342.3 19.4 %all_to_all.68.received = f32[32,8,128]{2,1,0:T(8,128)S(1)} all-to-all(f32[32,8,128]{2,1,0:T(8,128)S(1)} %shard_map.110), channel_id=1, replica_groups=mesh['pair'=8,'member'=2,'x'=4,'z'=4,'core'=2] {'x','z','core'}, dimensions={0} | all-to-all | bytes 262144 | tf_op jit(solution)/shard_map/all_to_all | solution.py:441
  361.8 4.2 %shard_map.111 = (f32[128,256]{1,0:T(8,128)}, f32[32,256]{1,0:T(8,128)}, f32[32,256]{1,0:T(8,128)}, f32[128,256]{1,0:T(8,128)}, f32[128,256]{1,0:T(8,128)S(1)}, /*index=5*/f32[2,256]{1,0:T(2,128)}) custom-call(s32[4]{0:T(128)S(1)} %pad_add_fusion.flags, f32[32,8,128]{2,1,0:T(8,128)S(1)} %all_to_all.68.received, ...), custom_call_target="tpu_custom_call" | custom-call | tf_op jit(solution)/shard_map/pallas_call | solution.py:311
  372.6 19.7 %all_to_all.69 = f32[4,32,2304]{2,1,0:T(8,128)S(1)} all-to-all(f32[4,32,2304]{2,1,0:T(8,128)S(1)} %bitcast.98), channel_id=1, replica_groups=mesh['pair'=8,'member'=2,'x'=4,'z'=4,'core'=2] {'x'}, dimensions={0} | all-to-all | bytes 2359296 | tf_op jit(solution)/shard_map/all_to_all | solution.py:475
  392.4 14.2 %all_to_all.70 = f32[4,8,2304]{2,1,0:T(8,128)S(1)} all-to-all(f32[4,8,2304]{2,1,0:T(8,128)S(1)} %bitcast.99), channel_id=1, replica_groups=mesh['pair'=8,'member'=2,'x'=4,'z'=4,'core'=2] {'z'}, dimensions={0} | all-to-all | bytes 589824 | tf_op jit(solution)/shard_map/all_to_all | solution.py:475
  (108 shorter events, 101.1 us)
Async XLA Ops:
  3.2 32.3 %collective-permute-start = (f32[9,128,256]{2,1,0:T(8,128)}, f32[9,128,256]{2,1,0:T(8,128)}, u32[]{:S(2)}, u32[]{:S(2)}) collective-permute-start(f32[9,128,256]{2,1,0:T(8,128)} %constant_dynamic-slice_fusion), channel_id=1, source_target_pairs={{0,32},{32,0},{1,33},{33,1},{2,34},{34,2},{3,35},{35,3},{4,36},{36... | collective-permute-start | bytes 3538952 | tf_op jit(solution)/shard_map/ppermute | solution.py:369
  11.5 7.5 %collective-permute-start.2 = (f32[112,256]{1,0:T(8,128)S(1)}, f32[112,256]{1,0:T(8,128)S(1)}, u32[]{:S(2)}, u32[]{:S(2)}) collective-permute-start(f32[112,256]{1,0:T(8,128)S(1)} %pad_maximum_fusion.2), channel_id=1, source_target_pairs={{1,0},{2,1},{3,2},{4,3},{5,4},{6,5},{7,6},{8,7},{9,8},{10,9},{11,1... | collective-permute-start | bytes 344072 | tf_op jit(solution)/shard_map/ppermute | solution.py:380
  35.5 20.4 %collective-permute-start.3 = (f32[9,128,256]{2,1,0:T(8,128)}, f32[9,128,256]{2,1,0:T(8,128)S(1)}, u32[]{:S(2)}, u32[]{:S(2)}) collective-permute-start(f32[9,128,256]{2,1,0:T(8,128)} %collective-permute-done.near), channel_id=1, source_target_pairs={{0,1},{1,0},{2,3},{3,2},{4,5},{5,4},{6,7},{7,6},{8,9},{9,8},{10,11... | collective-permute-start | bytes 3538952 | tf_op jit(solution)/shard_map/ppermute | solution.py:411
  39.4 15.7 %collective-permute-start.4 = (f32[2,192,256]{2,1,0:T(8,128)S(1)}, f32[2,192,256]{2,1,0:T(8,128)S(1)}, u32[]{:S(2)}, u32[]{:S(2)}) collective-permute-start(f32[2,192,256]{2,1,0:T(8,128)S(1)} %pad_maximum_fusion.fields), channel_id=1, source_target_pairs={{0,32},{32,0},{1,33},{33,1},{2,34},{34,2},{3,35},{35,3},{4,36},{36... | collective-permute-start | bytes 1179656 | tf_op jit(solution)/shard_map/ppermute | solution.py:409
  56.9 25.7 %all-to-all-start = ((f32[64,8,128]{2,1,0:T(8,128)}), f32[64,8,128]{2,1,0:T(8,128)S(1)}, u32[]{:S(2)}, u32[]{:S(2)}) async-start(f32[64,8,128]{2,1,0:T(8,128)} %copy-done.7), calls=%async_computation | async-start | bytes 524288 | tf_op jit(solution)/shard_map/all_to_all | solution.py:413
  129.3 7.4 %collective-permute-start.5 = (f32[128,256]{1,0:T(8,128)S(1)}, f32[128,256]{1,0:T(8,128)S(1)}, u32[]{:S(2)}, u32[]{:S(2)}) collective-permute-start(f32[128,256]{1,0:T(8,128)S(1)} %get-tuple-element.105), channel_id=1, source_target_pairs={{64,0},{65,1},{66,2},{67,3},{68,4},{69,5},{70,6},{71,7},{72,8},{73... | collective-permute-start | bytes 393224 | tf_op jit(solution)/shard_map/ppermute | solution.py:380
  135.3 5.2 %collective-permute-start.7 = (f32[32,256]{1,0:T(8,128)S(1)}, f32[32,256]{1,0:T(8,128)S(1)}, u32[]{:S(2)}, u32[]{:S(2)}) collective-permute-start(f32[32,256]{1,0:T(8,128)S(1)} %get-tuple-element.107), channel_id=1, source_target_pairs={{65,0},{66,1},{67,2},{68,3},{69,4},{70,5},{71,6},{72,7},{73,8},{74... | collective-permute-start | bytes 98312 | tf_op jit(solution)/shard_map/ppermute | solution.py:380
  165.2 8.2 %collective-permute-start.8 = (f32[128,256]{1,0:T(8,128)S(1)}, f32[128,256]{1,0:T(8,128)S(1)}, u32[]{:S(2)}, u32[]{:S(2)}) collective-permute-start(f32[128,256]{1,0:T(8,128)S(1)} %get-tuple-element.114), channel_id=1, source_target_pairs={{64,0},{65,1},{66,2},{67,3},{68,4},{69,5},{70,6},{71,7},{72,8},{73... | collective-permute-start | bytes 393224 | tf_op jit(solution)/shard_map/ppermute | solution.py:380
  167.6 6.7 %collective-permute-start.10 = (f32[32,256]{1,0:T(8,128)S(1)}, f32[32,256]{1,0:T(8,128)S(1)}, u32[]{:S(2)}, u32[]{:S(2)}) collective-permute-start(f32[32,256]{1,0:T(8,128)S(1)} %get-tuple-element.116), channel_id=1, source_target_pairs={{65,0},{66,1},{67,2},{68,3},{69,4},{70,5},{71,6},{72,7},{73,8},{74... | collective-permute-start | bytes 98312 | tf_op jit(solution)/shard_map/ppermute | solution.py:380
  168.9 6.0 %collective-permute-start.9 = (f32[32,256]{1,0:T(8,128)S(1)}, f32[32,256]{1,0:T(8,128)S(1)}, u32[]{:S(2)}, u32[]{:S(2)}) collective-permute-start(f32[32,256]{1,0:T(8,128)S(1)} %get-tuple-element.115), channel_id=1, source_target_pairs={{64,1},{65,2},{66,3},{67,4},{68,5},{69,6},{70,7},{71,8},{72,9},{73... | collective-permute-start | bytes 98312 | tf_op jit(solution)/shard_map/ppermute | solution.py:380
  198.6 7.6 %collective-permute-start.11 = (f32[128,256]{1,0:T(8,128)S(1)}, f32[128,256]{1,0:T(8,128)S(1)}, u32[]{:S(2)}, u32[]{:S(2)}) collective-permute-start(f32[128,256]{1,0:T(8,128)S(1)} %get-tuple-element.123), channel_id=1, source_target_pairs={{64,0},{65,1},{66,2},{67,3},{68,4},{69,5},{70,6},{71,7},{72,8},{73... | collective-permute-start | bytes 393224 | tf_op jit(solution)/shard_map/ppermute | solution.py:380
  203.9 5.2 %collective-permute-start.13 = (f32[32,256]{1,0:T(8,128)S(1)}, f32[32,256]{1,0:T(8,128)S(1)}, u32[]{:S(2)}, u32[]{:S(2)}) collective-permute-start(f32[32,256]{1,0:T(8,128)S(1)} %get-tuple-element.125), channel_id=1, source_target_pairs={{65,0},{66,1},{67,2},{68,3},{69,4},{70,5},{71,6},{72,7},{73,8},{74... | collective-permute-start | bytes 98312 | tf_op jit(solution)/shard_map/ppermute | solution.py:380
  233.8 7.9 %collective-permute-start.14 = (f32[128,256]{1,0:T(8,128)S(1)}, f32[128,256]{1,0:T(8,128)S(1)}, u32[]{:S(2)}, u32[]{:S(2)}) collective-permute-start(f32[128,256]{1,0:T(8,128)S(1)} %get-tuple-element.132), channel_id=1, source_target_pairs={{64,0},{65,1},{66,2},{67,3},{68,4},{69,5},{70,6},{71,7},{72,8},{73... | collective-permute-start | bytes 393224 | tf_op jit(solution)/shard_map/ppermute | solution.py:380
  236.3 6.2 %collective-permute-start.15 = (f32[32,256]{1,0:T(8,128)S(1)}, f32[32,256]{1,0:T(8,128)S(1)}, u32[]{:S(2)}, u32[]{:S(2)}) collective-permute-start(f32[32,256]{1,0:T(8,128)S(1)} %get-tuple-element.133), channel_id=1, source_target_pairs={{64,1},{65,2},{66,3},{67,4},{68,5},{69,6},{70,7},{71,8},{72,9},{73... | collective-permute-start | bytes 98312 | tf_op jit(solution)/shard_map/ppermute | solution.py:380
  238.2 5.2 %collective-permute-start.16 = (f32[32,256]{1,0:T(8,128)S(1)}, f32[32,256]{1,0:T(8,128)S(1)}, u32[]{:S(2)}, u32[]{:S(2)}) collective-permute-start(f32[32,256]{1,0:T(8,128)S(1)} %get-tuple-element.134), channel_id=1, source_target_pairs={{65,0},{66,1},{67,2},{68,3},{69,4},{70,5},{71,6},{72,7},{73,8},{74... | collective-permute-start | bytes 98312 | tf_op jit(solution)/shard_map/ppermute | solution.py:380
  267.7 8.0 %collective-permute-start.17 = (f32[128,256]{1,0:T(8,128)S(1)}, f32[128,256]{1,0:T(8,128)S(1)}, u32[]{:S(2)}, u32[]{:S(2)}) collective-permute-start(f32[128,256]{1,0:T(8,128)S(1)} %get-tuple-element.141), channel_id=1, source_target_pairs={{64,0},{65,1},{66,2},{67,3},{68,4},{69,5},{70,6},{71,7},{72,8},{73... | collective-permute-start | bytes 393224 | tf_op jit(solution)/shard_map/ppermute | solution.py:380
  269.6 6.9 %collective-permute-start.18 = (f32[32,256]{1,0:T(8,128)S(1)}, f32[32,256]{1,0:T(8,128)S(1)}, u32[]{:S(2)}, u32[]{:S(2)}) collective-permute-start(f32[32,256]{1,0:T(8,128)S(1)} %get-tuple-element.142), channel_id=1, source_target_pairs={{64,1},{65,2},{66,3},{67,4},{68,5},{69,6},{70,7},{71,8},{72,9},{73... | collective-permute-start | bytes 98312 | tf_op jit(solution)/shard_map/ppermute | solution.py:380
  271.5 5.2 %collective-permute-start.19 = (f32[32,256]{1,0:T(8,128)S(1)}, f32[32,256]{1,0:T(8,128)S(1)}, u32[]{:S(2)}, u32[]{:S(2)}) collective-permute-start(f32[32,256]{1,0:T(8,128)S(1)} %get-tuple-element.143), channel_id=1, source_target_pairs={{65,0},{66,1},{67,2},{68,3},{69,4},{70,5},{71,6},{72,7},{73,8},{74... | collective-permute-start | bytes 98312 | tf_op jit(solution)/shard_map/ppermute | solution.py:380
  300.9 8.0 %collective-permute-start.20 = (f32[128,256]{1,0:T(8,128)S(1)}, f32[128,256]{1,0:T(8,128)S(1)}, u32[]{:S(2)}, u32[]{:S(2)}) collective-permute-start(f32[128,256]{1,0:T(8,128)S(1)} %get-tuple-element.150), channel_id=1, source_target_pairs={{64,0},{65,1},{66,2},{67,3},{68,4},{69,5},{70,6},{71,7},{72,8},{73... | collective-permute-start | bytes 393224 | tf_op jit(solution)/shard_map/ppermute | solution.py:380
  302.8 6.9 %collective-permute-start.21 = (f32[32,256]{1,0:T(8,128)S(1)}, f32[32,256]{1,0:T(8,128)S(1)}, u32[]{:S(2)}, u32[]{:S(2)}) collective-permute-start(f32[32,256]{1,0:T(8,128)S(1)} %get-tuple-element.151), channel_id=1, source_target_pairs={{64,1},{65,2},{66,3},{67,4},{68,5},{69,6},{70,7},{71,8},{72,9},{73... | collective-permute-start | bytes 98312 | tf_op jit(solution)/shard_map/ppermute | solution.py:380
  304.1 5.6 %collective-permute-start.22 = (f32[32,256]{1,0:T(8,128)S(1)}, f32[32,256]{1,0:T(8,128)S(1)}, u32[]{:S(2)}, u32[]{:S(2)}) collective-permute-start(f32[32,256]{1,0:T(8,128)S(1)} %get-tuple-element.152), channel_id=1, source_target_pairs={{65,0},{66,1},{67,2},{68,3},{69,4},{70,5},{71,6},{72,7},{73,8},{74... | collective-permute-start | bytes 98312 | tf_op jit(solution)/shard_map/ppermute | solution.py:380
  333.5 8.0 %collective-permute-start.23 = (f32[128,256]{1,0:T(8,128)S(1)}, f32[128,256]{1,0:T(8,128)S(1)}, u32[]{:S(2)}, u32[]{:S(2)}) collective-permute-start(f32[128,256]{1,0:T(8,128)S(1)} %get-tuple-element.159), channel_id=1, source_target_pairs={{64,0},{65,1},{66,2},{67,3},{68,4},{69,5},{70,6},{71,7},{72,8},{73... | collective-permute-start | bytes 393224 | tf_op jit(solution)/shard_map/ppermute | solution.py:380
  335.4 6.9 %collective-permute-start.24 = (f32[32,256]{1,0:T(8,128)S(1)}, f32[32,256]{1,0:T(8,128)S(1)}, u32[]{:S(2)}, u32[]{:S(2)}) collective-permute-start(f32[32,256]{1,0:T(8,128)S(1)} %get-tuple-element.160), channel_id=1, source_target_pairs={{64,1},{65,2},{66,3},{67,4},{68,5},{69,6},{70,7},{71,8},{72,9},{73... | collective-permute-start | bytes 98312 | tf_op jit(solution)/shard_map/ppermute | solution.py:380
  336.7 5.6 %collective-permute-start.25 = (f32[32,256]{1,0:T(8,128)S(1)}, f32[32,256]{1,0:T(8,128)S(1)}, u32[]{:S(2)}, u32[]{:S(2)}) collective-permute-start(f32[32,256]{1,0:T(8,128)S(1)} %get-tuple-element.161), channel_id=1, source_target_pairs={{65,0},{66,1},{67,2},{68,3},{69,4},{70,5},{71,6},{72,7},{73,8},{74... | collective-permute-start | bytes 98312 | tf_op jit(solution)/shard_map/ppermute | solution.py:380
  (16 other events, 134.2 us)

commit v3 on v2

--- a/solution.py
+++ b/solution.py
@@ -66,46 +66,62 @@
     return total
 
 
-def group_matrix():
-    channel = lax.broadcasted_iota(jnp.int32, (C, GROUPS), 0)
-    group = lax.broadcasted_iota(jnp.int32, (C, GROUPS), 1)
-    return jnp.where((channel >> 3) == group, 1.0, 0.0).astype(f32)
-
-
-def spread_matrix():
-    channel = lax.broadcasted_iota(jnp.int32, (GROUPS, C), 1)
-    group = lax.broadcasted_iota(jnp.int32, (GROUPS, C), 0)
-    return jnp.where((channel >> 3) == group, 1.0, 0.0).astype(f32)
+def group_matrix(width=GROUPS, first=0):
+    channel = lax.broadcasted_iota(jnp.int32, (C, width), 0)
+    group = lax.broadcasted_iota(jnp.int32, (C, width), 1)
+    return jnp.where((channel >> 3) + first == group, 1.0, 0.0).astype(f32)
+
+
+def spread_matrix(width=GROUPS, first=0):
+    channel = lax.broadcasted_iota(jnp.int32, (width, C), 1)
+    group = lax.broadcasted_iota(jnp.int32, (width, C), 0)
+    return jnp.where((channel >> 3) + first == group, 1.0, 0.0).astype(f32)
 
 
 def column_sum(values):
     return jnp.sum(values, axis=0, keepdims=True)
 
 
-def forward_kernel(top, main, bottom, kernel, gamma, conv_out, sums):
-    image = jnp.concatenate([top[...], main[...], bottom[...]], axis=0)
-    count = image.shape[0] - 2 * COLS
+def forward_kernel(above, main, below, passing, start, kernel, gamma, fields, sums):
+    image = jnp.concatenate([above[: 3 * COLS, :], main[...], below[: 3 * COLS, :]], axis=0)
+    count = tall = image.shape[0] - 2 * COLS
     total = None
     for col_tap in range(3):
         high, low = split(shifted(image, col_tap - 1))
         for row_tap in range(3):
-            start = row_tap * COLS
+            start_row = row_tap * COLS
             part = dot3(
-                (high[start : start + count], low[start : start + count]),
+                (high[start_row : start_row + count], low[start_row : start_row + count]),
                 split(kernel[row_tap * 3 + col_tap]),
             )
             total = part if total is None else total + part
-    conv_out[...] = total
+    fields[:tall, :] = total
+    fields[tall : 2 * tall, :] = jnp.concatenate(
+        [above[3 * COLS : 5 * COLS, :], passing[...], below[3 * COLS : 5 * COLS, :]], axis=0
+    )
+    fields[2 * tall :, :] = jnp.concatenate([gamma[...], jnp.zeros((7, C), f32)], axis=0)
     own = total[2 * COLS : 2 * COLS + OWN]
+    grad_out = start[...] * passing[...]
+    half = C // 2
+    straight, weighted = column_sum(grad_out), column_sum(grad_out * own)
     block = jnp.concatenate(
-        [column_sum(own), column_sum(own * own), gamma[...], jnp.zeros((1, C), f32)], axis=0
-    )
-    sums[...] = jnp.broadcast_to(folded(block)[None], sums.shape)
+        [
+            dot(column_sum(own), group_matrix(half), highest)
+            + dot(column_sum(own * own), group_matrix(half, GROUPS), highest),
+            straight[:, :half],
+            straight[:, half:],
+            weighted[:, :half],
+            weighted[:, half:],
+            jnp.zeros((3, half), f32),
+        ],
+        axis=0,
+    )
+    sums[...] = jnp.broadcast_to(block[None], sums.shape)
 
 
 def prepare_kernel(
-    tiles, count, flags, own, near, far, gathered, fields, partner_fields,
-    a_high, a_low, b_high, b_low, pass_a, norm_a, pass_b, norm_b, params, response,
+    tiles, count, flags, own, near, near_two, far, far_two, gathered, fields, partner_fields,
+    a_high, a_low, b_high, b_low, pass_a, norm_a, pass_b, norm_b, params, opening, response,
     high_scr, low_scr, field_scr, flat_scr, full_scr,
 ):
     tap = pl.program_id(0)
@@ -114,31 +130,36 @@
 
     @pl.when(tap == 0)
     def _():
-        stats = gathered[...].reshape(2, tiles, 8, C // 2)
-        groups, spread = group_matrix(), spread_matrix()
+        stats = jnp.sum(gathered[...].reshape(2, tiles, 8, C // 2), axis=1)
+        half = C // 2
         inside = inside_rows(flags, tiles)
-
-        def section(which, conv_out, passing, pass_ref, norm_ref, row):
-            block = jnp.sum(stats[which], axis=0)
-            totals = jnp.concatenate([block[0:2], block[4:6]], axis=1)
-            gamma = jnp.concatenate([stats[which, 0, 2:3], stats[which, 0, 6:7]], axis=1)
-            grouped = dot(totals, groups, highest) * (1.0 / count)
-            mean = grouped[0:1]
-            inverse = lax.rsqrt(grouped[1:2] - mean * mean + eps)
-            wide = dot(jnp.concatenate([mean, inverse], axis=0), spread, highest)
-            mean, inverse = wide[0:1], wide[1:2]
+        tall = 12 * COLS
+
+        def section(which, conv_out, passing, gamma, pass_ref, norm_ref, row):
+            grouped = stats[which, 0:1] * (1.0 / count)
+            mean = dot(grouped, spread_matrix(half), highest)
+            square = dot(grouped, spread_matrix(half, GROUPS), highest)
+            inverse = lax.rsqrt(square - mean * mean + eps)
             pass_ref[...] = passing
             norm_ref[...] = (conv_out - mean) * inverse * inside
             params[row : row + 1, :] = gamma
             params[row + 1 : row + 2, :] = inverse
+            if which == 1:
+                block = stats[which]
+                straight = jnp.concatenate([block[1:2], block[2:3]], axis=1)
+                weighted = jnp.concatenate([block[3:4], block[4:5]], axis=1)
+                opening[0:1, :] = straight
+                opening[1:2, :] = inverse * (weighted - mean * straight)
 
         upper = member == 1
-        mine, other = fields[0], partner_fields[0]
-        my_pass, other_pass = fields[1], partner_fields[1]
+        mine, other = fields[:tall, :], partner_fields[:tall, :]
+        my_pass, other_pass = fields[tall : 2 * tall, :], partner_fields[tall : 2 * tall, :]
+        my_gamma = fields[2 * tall : 2 * tall + 1, :]
+        other_gamma = partner_fields[2 * tall : 2 * tall + 1, :]
         section(1, jnp.where(upper, mine, other), jnp.where(upper, my_pass, other_pass),
-                pass_a, norm_a, 0)
+                jnp.where(upper, my_gamma, other_gamma), pass_a, norm_a, 0)
         section(0, jnp.where(upper, other, mine), jnp.where(upper, other_pass, my_pass),
-                pass_b, norm_b, 2)
+                jnp.where(upper, other_gamma, my_gamma), pass_b, norm_b, 2)
         params[4:8, :] = jnp.zeros((4, C), f32)
         passing = pass_b[2 * COLS : 2 * COLS + OWN]
         normed = norm_b[2 * COLS : 2 * COLS + OWN]
@@ -152,7 +173,8 @@
         flat_scr[...] = jnp.zeros_like(flat_scr)
         full_scr[...] = jnp.zeros_like(full_scr)
 
-    near_tap, far_tap = near[0], far[0]
+    near_tap = jnp.concatenate([near[0], near_two[0]], axis=0)
+    far_tap = jnp.concatenate([far[0], far_two[0]], axis=0)
     partner = jnp.concatenate(
         [jnp.where(core == 0, near_tap, far_tap), jnp.where(core == 0, far_tap, near_tap)], axis=0
     )
@@ -226,10 +248,81 @@
     sums[...] = jnp.broadcast_to(parts[None], sums.shape)
 
 
-def opening_kernel(share, main, pass_a, norm_a, pass_b, norm_b, params, a_high, a_low, sums):
+def sharing_kernel(share, main, pass_a, norm_a, pass_b, norm_b, params, a_high, a_low, sums):
     parts = first_sums(main, pass_a, norm_a, pass_b, norm_b, params, a_high, a_low)
-    parts = jnp.concatenate([parts, jnp.sum(share[...], axis=0)], axis=0)
+    parts = jnp.concatenate([parts, share[...]], axis=0)
     sums[...] = jnp.broadcast_to(parts[None], sums.shape)
+
+
+def group_means(totals, gamma, count):
+    return dot(totals * gamma, group_matrix(), highest) * (1.0 / count)
+
+
+def through(incoming, passing, normed, inside, gamma, inverse, means, high, low):
+    wide = dot(means, spread_matrix(), highest)
+    grad = inverse * (incoming * passing * gamma - inside * wide[0:1] - normed * wide[1:2])
+    return grad, incoming[COLS:-COLS] + conv_back(grad, high, low)
+
+
+def gain_rows(totals):
+    return jnp.concatenate([totals[1:2], totals[0:1]], axis=0)
+
+
+def opening_kernel(
+    count, tiles, flags, opening, above, main, below, response, pass_a, norm_a, pass_b, norm_b,
+    params, a_high, a_low, sums, middle, grad_a,
+):
+    incoming = jnp.concatenate(
+        [above[5 * COLS :, :], main[...], below[5 * COLS :, :]], axis=0
+    )
+    means = group_means(opening[...], params[0:1, :], count)
+    grad, passed = through(
+        incoming, pass_a[...], norm_a[...], inside_rows(flags, tiles),
+        params[0:1, :], params[1:2, :], means, a_high, a_low,
+    )
+    middle[...] = passed
+    grad_a[...] = grad[2 * COLS : -2 * COLS]
+    own = slice(2 * COLS, 2 * COLS + OWN)
+    grad_b = passed[COLS:-COLS] * pass_b[own, :]
+    parts = folded(
+        jnp.concatenate(
+            [
+                jnp.zeros((2, C), f32),
+                column_sum(grad_b),
+                column_sum(grad_b * norm_b[own, :]),
+            ],
+            axis=0,
+        )
+    )
+    sums[...] = jnp.concatenate(
+        [jnp.broadcast_to(parts[None], (tiles, 8, C // 2)), response[...]], axis=1
+    )
+
+
+def closing_kernel(
+    count, tiles, flags, received, opening, middle, grad_a, pass_b, norm_b, params, b_high, b_low,
+    out, out_head, out_tail, act, grad, gain, share,
+):
+    totals = jnp.sum(received[...], axis=0)
+    share[...] = totals[8:]
+    totals = jnp.concatenate([totals[:4], totals[4:8]], axis=1)[2:4]
+    means = group_means(totals, params[2:3, :], count)
+    near = middle[...]
+    grad_b, last = through(
+        near, pass_b[COLS:-COLS, :], norm_b[COLS:-COLS, :],
+        inside_rows(flags, tiles)[COLS:-COLS], params[2:3, :], params[3:4, :],
+        means, b_high, b_low,
+    )
+    out[...] = last
+    out_head[...] = last[: 2 * COLS]
+    out_tail[...] = last[-2 * COLS :]
+    active = flags[0] == 0
+    upper = flags[1] == 1
+    act[...] = jnp.where(active, jnp.where(upper, near[COLS:-COLS], last), 0.0)
+    grad[...] = jnp.where(active, jnp.where(upper, grad_a[...], grad_b[COLS:-COLS]), 0.0)
+    gain[...] = jnp.where(
+        active, jnp.where(upper, gain_rows(opening[...]), gain_rows(totals)), 0.0
+    )
 
 
 def second_kernel(
@@ -238,7 +331,6 @@
     out, out_head, out_tail, act, grad, gain,
 ):
     incoming = jnp.concatenate([top[...], main[...], bottom[...]], axis=0)
-    gamma_a, inverse_a, gamma_b, inverse_b = (params[i : i + 1, :] for i in range(4))
     totals = jnp.sum(received[:, :8, :], axis=0)
     totals = jnp.concatenate([totals[:4], totals[4:]], axis=1)
     response = exchanged[:, 8:, :].reshape(GROUPS, 8, C // 2)
@@ -246,43 +338,36 @@
         jnp.concatenate([response[:, start + chunk, :] for chunk in range(4)], axis=1)
         for start in (0, 4)
     )
-    groups, spread = group_matrix(), spread_matrix()
-    means_a = dot(totals[0:2] * gamma_a, groups, highest) * (1.0 / count)
+    inside = inside_rows(flags, tiles)
+    means_a = group_means(totals[0:2], params[0:1, :], count)
     shift = dot(means_a[0:1], flat, highest) + dot(means_a[1:2], full, highest)
     totals_b = totals[2:4] - jnp.concatenate([shift[:, :C], shift[:, C:]], axis=0)
-    means_b = dot(totals_b * gamma_b, groups, highest) * (1.0 / count)
-    wide_a = dot(means_a, spread, highest)
-    wide_b = dot(means_b, spread, highest)
-    inside = inside_rows(flags, tiles)
-    grad_a = inverse_a * (
-        incoming * pass_a[...] * gamma_a - inside * wide_a[0:1] - norm_a[...] * wide_a[1:2]
-    )
-    middle = incoming[COLS:-COLS] + conv_back(grad_a, a_high, a_low)
-    grad_b = inverse_b * (
-        middle * pass_b[COLS:-COLS, :] * gamma_b
-        - inside[COLS:-COLS] * wide_b[0:1]
-        - norm_b[COLS:-COLS, :] * wide_b[1:2]
-    )
-    last = middle[COLS:-COLS] + conv_back(grad_b, b_high, b_low)
+    means_b = group_means(totals_b, params[2:3, :], count)
+    grad_a, middle = through(
+        incoming, pass_a[...], norm_a[...], inside, params[0:1, :], params[1:2, :],
+        means_a, a_high, a_low,
+    )
+    grad_b, last = through(
+        middle, pass_b[COLS:-COLS, :], norm_b[COLS:-COLS, :], inside[COLS:-COLS],
+        params[2:3, :], params[3:4, :], means_b, b_high, b_low,
+    )
     out[...] = last
     out_head[...] = last[: 2 * COLS]
     out_tail[...] = last[-2 * COLS :]
     active = flags[0] == step
     upper = flags[1] == 1
-    act[...] = jnp.where(
-        active, jnp.where(upper, middle[COLS:-COLS], last), old_act[...]
-    )
+    act[...] = jnp.where(active, jnp.where(upper, middle[COLS:-COLS], last), old_act[...])
     grad[...] = jnp.where(
         active, jnp.where(upper, grad_a[2 * COLS : -2 * COLS], grad_b[COLS:-COLS]), old_grad[...]
     )
-    pair_a = jnp.concatenate([totals[1:2], totals[0:1]], axis=0)
-    pair_b = jnp.concatenate([totals_b[1:2], totals_b[0:1]], axis=0)
-    gain[...] = jnp.where(active, jnp.where(upper, pair_a, pair_b), old_gain[...])
-
-
-def kernel_grad_kernel(tiles, flags, top, main, bottom, grad, mine, other):
+    gain[...] = jnp.where(
+        active, jnp.where(upper, gain_rows(totals[0:2]), gain_rows(totals_b)), old_gain[...]
+    )
+
+
+def kernel_grad_kernel(tiles, flags, above, main, below, grad, mine, other):
     share = C // tiles
-    image = jnp.concatenate([top[...], main[...], bottom[...]], axis=0)
+    image = jnp.concatenate([above[: 3 * COLS, :], main[...], below[: 3 * COLS, :]], axis=0)
     turned = grad[...].T.reshape(tiles // 2, 2, share, OWN)
     even = turned[:, 0].reshape(C // 2, OWN)
     odd = turned[:, 1].reshape(C // 2, OWN)
@@ -322,7 +407,7 @@
     return jax.ShapeDtypeStruct(dims, dtype)
 
 
-def prepare(tiles, count, flags, kernel, near, far, gathered, fields, partner_fields):
+def prepare(tiles, count, flags, kernel, pieces, gathered, fields, partner_fields):
     tap = lambda rows: pl.BlockSpec((1, rows, C), lambda i: (i, 0, 0))
     whole = lambda *dims: pl.BlockSpec(dims, lambda i: (0,) * len(dims))
     tall = 12 * COLS
@@ -331,19 +416,18 @@
         grid=(9,),
         out_shape=tuple(shape(9, C, C, dtype=bf16) for _ in range(4))
         + tuple(shape(tall, C) for _ in range(4))
-        + (shape(8, C), shape(GROUPS, 8, C // 2)),
+        + (shape(8, C), shape(2, C), shape(GROUPS, 8, C // 2)),
         in_specs=[
             pl.BlockSpec(memory_space=pltpu.SMEM),
             tap(C),
-            tap(C // 2),
-            tap(C // 2),
+            *(tap(C // 4) for _ in range(4)),
             whole(*gathered.shape),
             whole(*fields.shape),
             whole(*fields.shape),
         ],
         out_specs=tuple(tap(C) for _ in range(4))
         + tuple(whole(tall, C) for _ in range(4))
-        + (whole(8, C), whole(GROUPS, 8, C // 2)),
+        + (whole(8, C), whole(2, C), whole(GROUPS, 8, C // 2)),
         scratch_shapes=[
             pltpu.VMEM((2 * C, OWN), bf16),
             pltpu.VMEM((2 * C, OWN), bf16),
@@ -352,7 +436,7 @@
             pltpu.VMEM((2 * C, C), f32),
         ],
         compiler_params=pltpu.CompilerParams(vmem_limit_bytes=40 * 2**20),
-    )(flags, kernel, near, far, gathered, fields, partner_fields)
+    )(flags, kernel, *pieces, gathered, fields, partner_fields)
 
 
 def on_device(acts, kernels, gammas, pass_mask, drop_mask, path_mask, cotangent):
@@ -365,8 +449,21 @@
     swap = [(0, 1), (1, 0)]
 
     own_kernel = kernels[0].reshape(9, C, C)
-    half = lax.dynamic_slice_in_dim(own_kernel, core * (C // 2), C // 2, axis=1)
-    near = lax.ppermute(half, "member", swap)
+    quarters = [
+        lax.dynamic_slice_in_dim(own_kernel, core * (C // 2) + q * (C // 4), C // 4, axis=1)
+        for q in range(2)
+    ]
+    layers = lax.axis_size("z")
+    route = [(i, layers + i) for i in range(layers)] + [(layers + i, i) for i in range(layers)]
+    route_two = [(i, layers + (i - 1) % layers) for i in range(layers)] + [
+        (layers + (i - 1) % layers, i) for i in range(layers)
+    ]
+    near = lax.ppermute(quarters[0], ("member", "z"), route)
+    near_two = lax.ppermute(quarters[1], ("member", "z"), route_two)
+    flags = jnp.stack([pairs - 1 - pair, member, tile, core]).astype(jnp.int32)
+    acts, pass_mask, cotangent, flags, *quarters = lax.optimization_barrier(
+        (acts, pass_mask, cotangent, flags, *quarters)
+    )
 
     passing = (
         pass_mask[0, 0].astype(f32)
@@ -376,95 +473,103 @@
     image = acts[0, 0].reshape(OWN, C)
     start = cotangent[0].reshape(OWN, C)
 
-    def neighbours(value, step, jump):
+    def neighbours(value, step, source=None):
+        size = 2 * tiles
+        first, last, jump = (0, devices, 0) if source is None else (
+            source * size, (source + 1) * size, size,
+        )
         return lax.ppermute(
             value,
             ALL,
             [
-                (i, i - jump * 2 * tiles + step)
-                for i in range(jump * 2 * tiles, devices)
+                (i, i - jump + step)
+                for i in range(first, last)
                 if 0 <= i % tiles + step < tiles
             ],
         )
 
     from_above = neighbours(
-        jnp.concatenate([image[-3 * COLS :], passing[-2 * COLS :], start[-2 * COLS :]]), 1, 0
+        jnp.concatenate([image[-3 * COLS :], passing[-2 * COLS :], start[-2 * COLS :]]), 1
     )
     from_below = neighbours(
-        jnp.concatenate([image[: 3 * COLS], passing[: 2 * COLS], start[: 2 * COLS]]), -1, 0
-    )
-    cuts = (0, 3 * COLS, 5 * COLS, 7 * COLS)
-    above = [from_above[a:b] for a, b in zip(cuts, cuts[1:])]
-    below = [from_below[a:b] for a, b in zip(cuts, cuts[1:])]
-    image_parts = (above[0], image, below[0])
-    passing = jnp.concatenate([above[1], passing, below[1]])
+        jnp.concatenate([image[: 3 * COLS], passing[: 2 * COLS], start[: 2 * COLS]]), -1
+    )
     tall = 12 * COLS
-    conv_out, sums = call(
+    edges = (from_above, image, from_below)
+    fields, sums = call(
         forward_kernel,
-        (shape(tall, C), shape(2 * tiles, 8, C // 2)),
-        image_parts + (own_kernel, gammas),
+        (shape(2 * tall + 8, C), shape(2 * tiles, 8, C // 2)),
+        edges + (passing, start, own_kernel, gammas),
         False,
     )
-    fields = jnp.stack([conv_out, passing])
     partner_fields = lax.ppermute(fields, "member", swap)
-    near, sums = lax.optimization_barrier((near, sums))
+    near, near_two, partner_fields, sums = lax.optimization_barrier(
+        (near, near_two, partner_fields, sums)
+    )
     far = lax.ppermute(near, "core", swap)
-    far, partner_fields, sums = lax.optimization_barrier((far, partner_fields, sums))
+    far_two = lax.ppermute(near_two, "core", swap)
+    far, far_two, sums = lax.optimization_barrier((far, far_two, sums))
     gathered = lax.all_to_all(sums, ("member",) + TILE, 0, 0)
-    flags = jnp.stack([pairs - 1 - pair, member, tile, core]).astype(jnp.int32)
     prepared = prepare(
-        tiles, count, flags, own_kernel, near, far, gathered, fields, partner_fields
+        tiles, count, flags, own_kernel, (near, near_two, far, far_two), gathered, fields,
+        partner_fields,
     )
     a_high, a_low, b_high, b_low = (w.reshape(3, 3 * C, C) for w in prepared[:4])
-    masks, params, response = prepared[4:8], prepared[8], prepared[9]
+    masks, params, opening, response = prepared[4:8], prepared[8], prepared[9], prepared[10]
     piece = GROUPS // tiles
-    response = lax.all_to_all(response.reshape(tiles, piece * 8, C // 2), TILE, 0, 0)
-
-    top, main, bottom = above[2], start, below[2]
-    act = jnp.zeros((OWN, C), f32)
-    grad = jnp.zeros((OWN, C), f32)
-    gain = jnp.zeros((2, C), f32)
+    block = 8 + piece * 8
+    response = response.reshape(tiles, piece * 8, C // 2)
+    shared = masks + (params, a_high, a_low)
+    rows_out = (
+        shape(OWN, C),
+        shape(2 * COLS, C),
+        shape(2 * COLS, C),
+        shape(OWN, C),
+        shape(OWN, C),
+        shape(2, C),
+    )
+
+    sums, middle, grad_a = call(
+        functools.partial(opening_kernel, count, tiles),
+        (shape(tiles, block, C // 2), shape(OWN + 2 * COLS, C), shape(OWN, C)),
+        (flags, opening, from_above, start, from_below, response) + shared,
+        True,
+    )
+    received = lax.all_to_all(sums, TILE, 0, 0)
+    main, head, tail, act, grad, gain, share = call(
+        functools.partial(closing_kernel, count, tiles),
+        rows_out + (shape(piece * 8, C // 2),),
+        (flags, received, opening, middle, grad_a) + masks[2:] + (params, b_high, b_low),
+        True,
+    )
     exchanged = None
-    for step in range(pairs):
-        shared = masks + (params, a_high, a_low)
-        if step == 0:
-            sums = call(
-                opening_kernel,
-                shape(tiles, 8 + piece * 8, C // 2),
-                (response, main) + shared,
-                False,
-            )
-            received = exchanged = lax.all_to_all(sums, TILE, 0, 0)
+    for step in range(1, pairs):
+        main, top, bottom = (
+            neighbours(main, 0, pairs - step),
+            neighbours(tail, 1, pairs - step),
+            neighbours(head, -1, pairs - step),
+        )
+        if step == 1:
+            sums = call(sharing_kernel, shape(tiles, block, C // 2), (share, main) + shared, False)
         else:
             sums = call(first_kernel, shape(tiles, 8, C // 2), (main,) + shared, False)
-            sums, top, bottom = lax.optimization_barrier((sums, top, bottom))
-            received = lax.all_to_all(sums, TILE, 0, 0)
+        sums, top, bottom = lax.optimization_barrier((sums, top, bottom))
+        received = lax.all_to_all(sums, TILE, 0, 0)
+        if step == 1:
+            exchanged = received
         main, head, tail, act, grad, gain = call(
             functools.partial(second_kernel, count, tiles, step),
-            (
-                shape(OWN, C),
-                shape(2 * COLS, C),
-                shape(2 * COLS, C),
-                shape(OWN, C),
-                shape(OWN, C),
-                shape(2, C),
-            ),
+            rows_out,
             (flags, received, exchanged, top, main, bottom)
             + shared
             + (b_high, b_low, act, grad, gain),
             True,
         )
-        if step < pairs - 1:
-            main, top, bottom = (
-                neighbours(main, 0, 1),
-                neighbours(tail, 1, 1),
-                neighbours(head, -1, 1),
-            )
 
     mine, other = call(
         functools.partial(kernel_grad_kernel, tiles),
         (shape(C // 2, 9 * C), shape(C // 2, 9 * C)),
-        (flags,) + image_parts + (grad,),
+        (flags,) + edges + (grad,),
         True,
     )
     share = C // tiles
@@ -484,7 +589,7 @@
 
 def solution(mesh):
     sections, tiles = mesh.shape["section"], mesh.shape["tile"]
-    across = 4 if tiles == 32 else 1
+    across = min(4, tiles // 2)
     finer = Mesh(
         mesh.devices.reshape(sections // 2, 2, tiles // (2 * across), across, 2), ALL
     )

time: 409 us -> 348 us (0.85)
  the two profiles are of different devices: /device:TPU:48 before, /device:TPU:2 now
where the time goes in v3:
time: 348 us; the launch traced here: 347 us
  blocking collectives  176 us (51%)
  waiting for transfers between devices  69.3 us (20%)
  starting transfers between devices  46.6 us (13%)
  Pallas kernels  45.4 us (13%)
  other arithmetic  4.05 us (1%)
    all_to_all x8, blocking collectives, on_device(): received = lax.all_to_all(sums, TILE, 0, 0)  121 us
    ppermute x23, waiting for transfers between devices, neighbours(): lax.ppermute(value, ALL, [(i, i - jump + step) for i in range(first, last...  55.7 us
    pallas_call x18, Pallas kernels, call(): pl.pallas_call(body, out_shape=out_shape, in_specs=in_specs, out_specs=tu...  36.5 us
    all_to_all x2, blocking collectives, on_device(): lax.all_to_all(mine.reshape(parts, mine.shape[0] // parts, 9 * C), axis,...  33.8 us
    ppermute x23, starting transfers between devices, neighbours(): lax.ppermute(value, ALL, [(i, i - jump + step) for i in range(first, last...  24.6 us
    all_to_all x1, blocking collectives, on_device(): gathered = lax.all_to_all(sums, ('member',) + TILE, 0, 0)  21.3 us
    ppermute x1, starting transfers between devices, on_device(): near_two = lax.ppermute(quarters[1], ('member', 'z'), route_two)  11.1 us
    ppermute x1, waiting for transfers between devices, on_device(): partner_fields = lax.ppermute(fields, 'member', swap)  9.54 us
  transfers between devices with their start and end apart: 29, of which 6 were waited for; matrix products, arithmetic and copies ran while one was open for 1% of the time, Pallas kernels for 2%

profile of v3, /device:TPU:2, one launch (start us, length us, event | category | flops | bytes accessed | tf_op | source)
XLA Modules:
  0.0 346.6 jit_solution(13666089039003339301)
XLA Ops:
  3.2 11.1 %collective-permute-start.1 = (f32[9,64,256]{2,1,0:T(8,128)}, f32[9,64,256]{2,1,0:T(8,128)S(1)}, u32[]{:S(2)}, u32[]{:S(2)}) collective-permute-start(f32[9,64,256]{2,1,0:T(8,128)} %get-tuple-element.195), channel_id=1, source_target_pairs={{0,38},{2,32},{4,34},{6,36},{38,0},{32,2},{34,4},{36,6},{1,39},{3,... | collective-permute-start | bytes 1769480 | tf_op jit(solution)/shard_map/ppermute | solution.py:462
  21.8 6.6 %collective-permute-start.3 = (f32[112,256]{1,0:T(8,128)}, f32[112,256]{1,0:T(8,128)S(1)}, u32[]{:S(2)}, u32[]{:S(2)}) collective-permute-start(f32[112,256]{1,0:T(8,128)} %pad_maximum_fusion.1), channel_id=1, source_target_pairs={{1,0},{2,1},{3,2},{4,3},{5,4},{6,5},{7,6},{8,7},{9,8},{10,9},{11,1... | collective-permute-start | bytes 344072 | tf_op jit(solution)/shard_map/ppermute | solution.py:481
  29.5 3.8 %collective-permute-done.2.above = f32[112,256]{1,0:T(8,128)S(1)} collective-permute-done((f32[112,256]{1,0:T(8,128)}, f32[112,256]{1,0:T(8,128)S(1)}, u32[]{:S(2)}, u32[]{:S(2)}) %collective-permute-start.2) | collective-permute-done | bytes 114720 | tf_op jit(solution)/shard_map/ppermute | solution.py:481
  36.7 9.5 %collective-permute-done.4.partner_fields = f32[392,256]{1,0:T(8,128)S(1)} collective-permute-done((f32[392,256]{1,0:T(8,128)S(1)}, f32[392,256]{1,0:T(8,128)S(1)}, u32[]{:S(2)}, u32[]{:S(2)}) %collective-permute-start.4) | collective-permute-done | bytes 401440 | tf_op jit(solution)/shard_map/ppermute | solution.py:505
  52.2 21.3 %all_to_all.55.gathered = f32[64,8,128]{2,1,0:T(8,128)S(1)} all-to-all(f32[64,8,128]{2,1,0:T(8,128)S(1)} %get-tuple-element.110), channel_id=1, replica_groups=mesh['pair'=8,'member'=2,'x'=4,'z'=4,'core'=2] {'member','x','z','core'}, dimensions={0} | all-to-all | bytes 524288 | tf_op jit(solution)/shard_map/all_to_all | solution.py:512
  73.4 8.9 %shard_map.95 = (bf16[9,256,256]{2,1,0:T(8,128)(2,1)S(1)}, bf16[9,256,256]{2,1,0:T(8,128)(2,1)S(1)}, bf16[9,256,256]{2,1,0:T(8,128)(2,1)S(1)}, bf16[9,256,256]{2...) custom-call(s32[4]{0:T(128)S(1)} %pad_add_fusion.flags, ...), custom_call_target="tpu_custom_call" | custom-call | tf_op jit(solution)/shard_map/pallas_call | solution.py:414
  84.0 15.4 %all_to_all.56.received = f32[32,16,128]{2,1,0:T(8,128)S(1)} all-to-all(f32[32,16,128]{2,1,0:T(8,128)S(1)} %get-tuple-element.121), channel_id=1, replica_groups=mesh['pair'=8,'member'=2,'x'=4,'z'=4,'core'=2] {'x','z','core'}, dimensions={0} | all-to-all | bytes 524288 | tf_op jit(solution)/shard_map/all_to_all | solution.py:538
  103.9 17.0 %all_to_all.57.received.exchanged = f32[32,16,128]{2,1,0:T(8,128)S(1)} all-to-all(f32[32,16,128]{2,1,0:T(8,128)S(1)} %shard_map.98), channel_id=1, replica_groups=mesh['pair'=8,'member'=2,'x'=4,'z'=4,'core'=2] {'x','z','core'}, dimensions={0} | all-to-all | bytes 524288 | tf_op jit(solution)/shard_map/all_to_all | solution.py:557
  120.8 3.4 shard_map.99
  127.1 15.2 %all_to_all.58.received = f32[32,8,128]{2,1,0:T(8,128)S(1)} all-to-all(f32[32,8,128]{2,1,0:T(8,128)S(1)} %shard_map.100), channel_id=1, replica_groups=mesh['pair'=8,'member'=2,'x'=4,'z'=4,'core'=2] {'x','z','core'}, dimensions={0} | all-to-all | bytes 262144 | tf_op jit(solution)/shard_map/all_to_all | solution.py:557
  142.3 3.4 shard_map.101
  148.6 14.1 %all_to_all.59.received = f32[32,8,128]{2,1,0:T(8,128)S(1)} all-to-all(f32[32,8,128]{2,1,0:T(8,128)S(1)} %shard_map.102), channel_id=1, replica_groups=mesh['pair'=8,'member'=2,'x'=4,'z'=4,'core'=2] {'x','z','core'}, dimensions={0} | all-to-all | bytes 262144 | tf_op jit(solution)/shard_map/all_to_all | solution.py:557
  162.8 3.4 shard_map.103
  169.0 14.2 %all_to_all.60.received = f32[32,8,128]{2,1,0:T(8,128)S(1)} all-to-all(f32[32,8,128]{2,1,0:T(8,128)S(1)} %shard_map.104), channel_id=1, replica_groups=mesh['pair'=8,'member'=2,'x'=4,'z'=4,'core'=2] {'x','z','core'}, dimensions={0} | all-to-all | bytes 262144 | tf_op jit(solution)/shard_map/all_to_all | solution.py:557
  183.2 3.4 shard_map.105
  189.5 14.2 %all_to_all.61.received = f32[32,8,128]{2,1,0:T(8,128)S(1)} all-to-all(f32[32,8,128]{2,1,0:T(8,128)S(1)} %shard_map.106), channel_id=1, replica_groups=mesh['pair'=8,'member'=2,'x'=4,'z'=4,'core'=2] {'x','z','core'}, dimensions={0} | all-to-all | bytes 262144 | tf_op jit(solution)/shard_map/all_to_all | solution.py:557
  203.7 3.4 shard_map.107
  210.2 14.2 %all_to_all.62.received = f32[32,8,128]{2,1,0:T(8,128)S(1)} all-to-all(f32[32,8,128]{2,1,0:T(8,128)S(1)} %shard_map.108), channel_id=1, replica_groups=mesh['pair'=8,'member'=2,'x'=4,'z'=4,'core'=2] {'x','z','core'}, dimensions={0} | all-to-all | bytes 262144 | tf_op jit(solution)/shard_map/all_to_all | solution.py:557
  224.4 3.4 shard_map.109
  231.8 51.0 %collective-permute-done.25.main = f32[128,256]{1,0:T(8,128)S(1)} collective-permute-done((f32[128,256]{1,0:T(8,128)S(1)}, f32[128,256]{1,0:T(8,128)S(1)}, u32[]{:S(2)}, u32[]{:S(2)}) %collective-permute-start.25) | collective-permute-done | bytes 131104 | tf_op jit(solution)/shard_map/ppermute | solution.py:481
  284.4 16.5 %all_to_all.63.received = f32[32,8,128]{2,1,0:T(8,128)S(1)} all-to-all(f32[32,8,128]{2,1,0:T(8,128)S(1)} %shard_map.110), channel_id=1, replica_groups=mesh['pair'=8,'member'=2,'x'=4,'z'=4,'core'=2] {'x','z','core'}, dimensions={0} | all-to-all | bytes 262144 | tf_op jit(solution)/shard_map/all_to_all | solution.py:557
  300.9 4.2 %shard_map.111 = (f32[128,256]{1,0:T(8,128)}, f32[32,256]{1,0:T(8,128)}, f32[32,256]{1,0:T(8,128)}, f32[128,256]{1,0:T(8,128)}, f32[128,256]{1,0:T(8,128)S(1)}, /*index=5*/f32[2,256]{1,0:T(2,128)}) custom-call(s32[4]{0:T(128)S(1)} %pad_add_fusion.flags, f32[32,8,128]{2,1,0:T(8,128)S(1)} %all_to_all.63.received, ...), custom_call_target="tpu_custom_call" | custom-call | tf_op jit(solution)/shard_map/pallas_call | solution.py:396
  312.1 19.7 %all_to_all.64 = f32[4,32,2304]{2,1,0:T(8,128)S(1)} all-to-all(f32[4,32,2304]{2,1,0:T(8,128)S(1)} %bitcast.92), channel_id=1, replica_groups=mesh['pair'=8,'member'=2,'x'=4,'z'=4,'core'=2] {'x'}, dimensions={0} | all-to-all | bytes 2359296 | tf_op jit(solution)/shard_map/all_to_all | solution.py:580
  331.9 14.1 %all_to_all.65 = f32[4,8,2304]{2,1,0:T(8,128)S(1)} all-to-all(f32[4,8,2304]{2,1,0:T(8,128)S(1)} %bitcast.93), channel_id=1, replica_groups=mesh['pair'=8,'member'=2,'x'=4,'z'=4,'core'=2] {'z'}, dimensions={0} | all-to-all | bytes 589824 | tf_op jit(solution)/shard_map/all_to_all | solution.py:580
  (88 shorter events, 53.0 us)
Async XLA Ops:
  3.2 43.0 %collective-permute-start.1 = (f32[9,64,256]{2,1,0:T(8,128)}, f32[9,64,256]{2,1,0:T(8,128)S(1)}, u32[]{:S(2)}, u32[]{:S(2)}) collective-permute-start(f32[9,64,256]{2,1,0:T(8,128)} %get-tuple-element.195), channel_id=1, source_target_pairs={{0,38},{2,32},{4,34},{6,36},{38,0},{32,2},{34,4},{36,6},{1,39},{3,... | collective-permute-start | bytes 1769480 | tf_op jit(solution)/shard_map/ppermute | solution.py:462
  14.3 31.9 %collective-permute-start = (f32[9,64,256]{2,1,0:T(8,128)}, f32[9,64,256]{2,1,0:T(8,128)}, u32[]{:S(2)}, u32[]{:S(2)}) collective-permute-start(f32[9,64,256]{2,1,0:T(8,128)} %get-tuple-element.196), channel_id=1, source_target_pairs={{0,32},{2,34},{4,36},{6,38},{32,0},{34,2},{36,4},{38,6},{1,33},{3,... | collective-permute-start | bytes 1769480 | tf_op jit(solution)/shard_map/ppermute | solution.py:461
  19.2 14.1 %collective-permute-start.2 = (f32[112,256]{1,0:T(8,128)}, f32[112,256]{1,0:T(8,128)S(1)}, u32[]{:S(2)}, u32[]{:S(2)}) collective-permute-start(f32[112,256]{1,0:T(8,128)} %pad_maximum_fusion), channel_id=1, source_target_pairs={{0,1},{1,2},{2,3},{3,4},{4,5},{5,6},{6,7},{7,8},{8,9},{9,10},{10,1... | collective-permute-start | bytes 344072 | tf_op jit(solution)/shard_map/ppermute | solution.py:481
  21.8 11.5 %collective-permute-start.3 = (f32[112,256]{1,0:T(8,128)}, f32[112,256]{1,0:T(8,128)S(1)}, u32[]{:S(2)}, u32[]{:S(2)}) collective-permute-start(f32[112,256]{1,0:T(8,128)} %pad_maximum_fusion.1), channel_id=1, source_target_pairs={{1,0},{2,1},{3,2},{4,3},{5,4},{6,5},{7,6},{8,7},{9,8},{10,9},{11,1... | collective-permute-start | bytes 344072 | tf_op jit(solution)/shard_map/ppermute | solution.py:481
  34.7 11.5 %collective-permute-start.4 = (f32[392,256]{1,0:T(8,128)S(1)}, f32[392,256]{1,0:T(8,128)S(1)}, u32[]{:S(2)}, u32[]{:S(2)}) collective-permute-start(f32[392,256]{1,0:T(8,128)S(1)} %get-tuple-element.103.fields), channel_id=1, source_target_pairs={{0,32},{32,0},{1,33},{33,1},{2,34},{34,2},{3,35},{35,3},{4,36},{36... | collective-permute-start | bytes 1204232 | tf_op jit(solution)/shard_map/ppermute | solution.py:505
  46.2 4.3 %collective-permute-start.5 = (f32[9,64,256]{2,1,0:T(8,128)}, f32[9,64,256]{2,1,0:T(8,128)S(1)}, u32[]{:S(2)}, u32[]{:S(2)}) collective-permute-start(f32[9,64,256]{2,1,0:T(8,128)} %collective-permute-done.near), channel_id=1, source_target_pairs={{0,1},{1,0},{2,3},{3,2},{4,5},{5,4},{6,7},{7,6},{8,9},{9,8},{10,11... | collective-permute-start | bytes 1769480 | tf_op jit(solution)/shard_map/ppermute | solution.py:509
  48.1 4.0 %collective-permute-start.6 = (f32[9,64,256]{2,1,0:T(8,128)S(1)}, f32[9,64,256]{2,1,0:T(8,128)S(1)}, u32[]{:S(2)}, u32[]{:S(2)}) collective-permute-start(f32[9,64,256]{2,1,0:T(8,128)S(1)} %collective-permute-done.1.near_two), channel_id=1, source_target_pairs={{0,1},{1,0},{2,3},{3,2},{4,5},{5,4},{6,7},{7,6},{8,9},{9,8},{10,11... | collective-permute-start | bytes 1769480 | tf_op jit(solution)/shard_map/ppermute | solution.py:510
  101.0 2.0 collective-permute-start.7
  101.7 2.1 collective-permute-start.8
  124.3 2.0 collective-permute-start.10
  124.9 2.1 collective-permute-start.11
  145.8 2.0 collective-permute-start.13
  146.5 2.1 collective-permute-start.14
  166.2 2.0 collective-permute-start.16
  166.9 2.1 collective-permute-start.17
  186.7 2.0 collective-permute-start.19
  187.4 2.1 collective-permute-start.20
  188.0 1.5 collective-permute-start.21
  207.1 2.2 collective-permute-start.22
  208.0 2.1 collective-permute-start.23
  227.9 54.9 %collective-permute-start.25 = (f32[128,256]{1,0:T(8,128)S(1)}, f32[128,256]{1,0:T(8,128)S(1)}, u32[]{:S(2)}, u32[]{:S(2)}) collective-permute-start(f32[128,256]{1,0:T(8,128)S(1)} %get-tuple-element.181), channel_id=1, source_target_pairs={{64,0},{65,1},{66,2},{67,3},{68,4},{69,5},{70,6},{71,7},{72,8},{73... | collective-permute-start | bytes 393224 | tf_op jit(solution)/shard_map/ppermute | solution.py:481
  229.2 55.2 %collective-permute-start.26 = (f32[32,256]{1,0:T(8,128)S(1)}, f32[32,256]{1,0:T(8,128)S(1)}, u32[]{:S(2)}, u32[]{:S(2)}) collective-permute-start(f32[32,256]{1,0:T(8,128)S(1)} %get-tuple-element.182), channel_id=1, source_target_pairs={{64,1},{65,2},{66,3},{67,4},{68,5},{69,6},{70,7},{71,8},{72,9},{73... | collective-permute-start | bytes 98312 | tf_op jit(solution)/shard_map/ppermute | solution.py:481
  230.5 53.9 %collective-permute-start.27 = (f32[32,256]{1,0:T(8,128)S(1)}, f32[32,256]{1,0:T(8,128)S(1)}, u32[]{:S(2)}, u32[]{:S(2)}) collective-permute-start(f32[32,256]{1,0:T(8,128)S(1)} %get-tuple-element.183), channel_id=1, source_target_pairs={{65,0},{66,1},{67,2},{68,3},{69,4},{70,5},{71,6},{72,7},{73,8},{74... | collective-permute-start | bytes 98312 | tf_op jit(solution)/shard_map/ppermute | solution.py:481
  306.7 5.2 %collective-permute-start.28 = (f32[128,2304]{1,0:T(8,128)S(1)}, f32[128,2304]{1,0:T(8,128)S(1)}, u32[]{:S(2)}, u32[]{:S(2)}) collective-permute-start(f32[128,2304]{1,0:T(8,128)S(1)} %get-tuple-element.193), channel_id=1, source_target_pairs={{0,1},{1,0},{2,3},{3,2},{4,5},{5,4},{6,7},{7,6},{8,9},{9,8},{10,11... | collective-permute-start | bytes 3538952 | tf_op jit(solution)/shard_map/ppermute | solution.py:576
  (10 other events, 136.0 us)

commit v4 on v3

--- a/solution.py
+++ b/solution.py
@@ -13,6 +13,7 @@
 COLS = 16
 ROWS = 8
 OWN = ROWS * COLS
+LANES = 4 * GROUPS
 
 keep_drop = 0.9
 keep_path = 0.75
@@ -72,14 +73,63 @@
     return jnp.where((channel >> 3) + first == group, 1.0, 0.0).astype(f32)
 
 
-def spread_matrix(width=GROUPS, first=0):
-    channel = lax.broadcasted_iota(jnp.int32, (width, C), 1)
-    group = lax.broadcasted_iota(jnp.int32, (width, C), 0)
-    return jnp.where((channel >> 3) + first == group, 1.0, 0.0).astype(f32)
+def exact_dot(left, right):
+    count = left.shape[0]
+    high = left.astype(bf16)
+    rest = left - high.astype(f32)
+    middle = rest.astype(bf16)
+    low = (rest - middle.astype(f32)).astype(bf16)
+    pieces = jnp.concatenate([x.astype(f32) for x in (high, middle, low)], axis=0).astype(bf16)
+    product = dot(pieces, right.astype(bf16))
+    return product[:count] + product[count : 2 * count] + product[2 * count :]
+
+
+def lane_quarter(rows):
+    return lax.broadcasted_iota(jnp.int32, (rows, LANES), 1) >> 5
+
+
+def repeated_groups():
+    channel = lax.broadcasted_iota(jnp.int32, (C, LANES), 0)
+    lane = lax.broadcasted_iota(jnp.int32, (C, LANES), 1)
+    return jnp.where((channel >> 3) == (lane & (GROUPS - 1)), 1.0, 0.0)
+
+
+def pack(rows):
+    sums = exact_dot(rows, repeated_groups())
+    row = lax.broadcasted_iota(jnp.int32, (4, LANES), 0)
+    return column_sum(jnp.where(lane_quarter(4) == row, sums, 0.0))
+
+
+def unpack(packed):
+    row = lax.broadcasted_iota(jnp.int32, (4, LANES), 0)
+    apart = jnp.where(lane_quarter(4) == row, jnp.broadcast_to(packed, (4, LANES)), 0.0)
+    lane = lax.broadcasted_iota(jnp.int32, (LANES, C), 0)
+    channel = lax.broadcasted_iota(jnp.int32, (LANES, C), 1)
+    return exact_dot(apart, jnp.where((channel >> 3) == (lane & (GROUPS - 1)), 1.0, 0.0))
 
 
 def column_sum(values):
     return jnp.sum(values, axis=0, keepdims=True)
+
+
+def edge_kernel(path, image, mask, drop, start, passing, tail, head):
+    pixel = lax.broadcasted_iota(jnp.int32, (OWN, ROWS), 0)
+    row = lax.broadcasted_iota(jnp.int32, (OWN, ROWS), 1)
+    by_row = dot(
+        jnp.where((pixel >> 4) == row, 1.0, 0.0).astype(bf16), drop[...].astype(f32).astype(bf16)
+    )
+    pixel = lax.broadcasted_iota(jnp.int32, (OWN, COLS), 0)
+    column = lax.broadcasted_iota(jnp.int32, (OWN, COLS), 1)
+    kept = jnp.sum(jnp.where((pixel & (COLS - 1)) == column, by_row, 0.0), axis=1, keepdims=True)
+    kept_path = path[0, 0].astype(f32) / keep_path
+    values = mask[...].astype(f32) * (kept / keep_drop) * kept_path
+    passing[...] = values
+    tail[: 3 * COLS, :] = image[-3 * COLS :, :]
+    tail[3 * COLS : 5 * COLS, :] = values[-2 * COLS :]
+    tail[5 * COLS :, :] = start[-2 * COLS :, :]
+    head[: 3 * COLS, :] = image[: 3 * COLS, :]
+    head[3 * COLS : 5 * COLS, :] = values[: 2 * COLS]
+    head[5 * COLS :, :] = start[: 2 * COLS, :]
 
 
 def forward_kernel(above, main, below, passing, start, kernel, gamma, fields, sums):
@@ -102,21 +152,18 @@
     fields[2 * tall :, :] = jnp.concatenate([gamma[...], jnp.zeros((7, C), f32)], axis=0)
     own = total[2 * COLS : 2 * COLS + OWN]
     grad_out = start[...] * passing[...]
-    half = C // 2
-    straight, weighted = column_sum(grad_out), column_sum(grad_out * own)
-    block = jnp.concatenate(
-        [
-            dot(column_sum(own), group_matrix(half), highest)
-            + dot(column_sum(own * own), group_matrix(half, GROUPS), highest),
-            straight[:, :half],
-            straight[:, half:],
-            weighted[:, :half],
-            weighted[:, half:],
-            jnp.zeros((3, half), f32),
-        ],
-        axis=0,
-    )
-    sums[...] = jnp.broadcast_to(block[None], sums.shape)
+    packed = pack(
+        jnp.concatenate(
+            [
+                column_sum(own),
+                column_sum(own * own),
+                column_sum(grad_out) * gamma[...],
+                column_sum(grad_out * own) * gamma[...],
+            ],
+            axis=0,
+        )
+    )
+    sums[...] = jnp.broadcast_to(packed[None], sums.shape)
 
 
 def prepare_kernel(
@@ -130,26 +177,24 @@
 
     @pl.when(tap == 0)
     def _():
-        stats = jnp.sum(gathered[...].reshape(2, tiles, 8, C // 2), axis=1)
-        half = C // 2
+        stats = [
+            jnp.sum(gathered[which * tiles : (which + 1) * tiles], axis=0) * (1.0 / count)
+            for which in range(2)
+        ]
         inside = inside_rows(flags, tiles)
         tall = 12 * COLS
 
         def section(which, conv_out, passing, gamma, pass_ref, norm_ref, row):
-            grouped = stats[which, 0:1] * (1.0 / count)
-            mean = dot(grouped, spread_matrix(half), highest)
-            square = dot(grouped, spread_matrix(half, GROUPS), highest)
+            wide = unpack(stats[which])
+            mean, square = wide[0:1], wide[1:2]
             inverse = lax.rsqrt(square - mean * mean + eps)
             pass_ref[...] = passing
             norm_ref[...] = (conv_out - mean) * inverse * inside
             params[row : row + 1, :] = gamma
             params[row + 1 : row + 2, :] = inverse
             if which == 1:
-                block = stats[which]
-                straight = jnp.concatenate([block[1:2], block[2:3]], axis=1)
-                weighted = jnp.concatenate([block[3:4], block[4:5]], axis=1)
-                opening[0:1, :] = straight
-                opening[1:2, :] = inverse * (weighted - mean * straight)
+                opening[0:1, :] = wide[2:3]
+                opening[1:2, :] = inverse * (wide[3:4] - mean * wide[2:3])
 
         upper = member == 1
         mine, other = fields[:tall, :], partner_fields[:tall, :]
@@ -201,13 +246,18 @@
     def _():
         groups = group_matrix()
         contract = (((0,), (1,)), ((), ()))
+        total = jnp.zeros((GROUPS, LANES), f32)
         for index, scratch in enumerate((flat_scr, full_scr)):
             part = lax.dot_general(
                 groups, scratch[...] * params[1:2, :], contract,
                 preferred_element_type=f32, precision=highest,
             )
-            for chunk in range(4):
-                response[:, index * 4 + chunk, :] = part[:, chunk * 128 : (chunk + 1) * 128]
+            for side in range(2):
+                sums = exact_dot(
+                    part[:, side * C : (side + 1) * C] * params[2:3, :], repeated_groups()
+                )
+                total += jnp.where(lane_quarter(GROUPS) == index * 2 + side, sums, 0.0)
+        response[...] = total * (1.0 / count)
 
 
 def inside_rows(flags, tiles):
@@ -215,10 +265,6 @@
     first = jnp.where(flags[2] == 0, 2 * COLS, 0)
     last = jnp.where(flags[2] == tiles - 1, 10 * COLS, 12 * COLS)
     return jnp.where((row >= first) & (row < last), 1.0, 0.0).astype(f32)
-
-
-def folded(values):
-    return jnp.concatenate([values[:, : C // 2], values[:, C // 2 :]], axis=0)
 
 
 def first_sums(main, pass_a, norm_a, pass_b, norm_b, params, a_high, a_low):
@@ -229,14 +275,18 @@
     scaled = jnp.concatenate([blank, grad_out * (params[0:1, :] * params[1:2, :]), blank], axis=0)
     spread = conv_back(scaled, a_high, a_low) * pass_b[COLS:-COLS, :]
     straight = incoming * pass_b[own, :]
-    return folded(
+    gamma_a, gamma_b = params[0:1, :], params[2:3, :]
+    return pack(
         jnp.concatenate(
             [
-                column_sum(grad_out),
-                column_sum(grad_out * norm_a[own, :]),
-                column_sum(spread) + column_sum(straight),
-                column_sum(spread * norm_b[COLS:-COLS, :])
-                + column_sum(straight * norm_b[own, :]),
+                column_sum(grad_out) * gamma_a,
+                column_sum(grad_out * norm_a[own, :]) * gamma_a,
+                (column_sum(spread) + column_sum(straight)) * gamma_b,
+                (
+                    column_sum(spread * norm_b[COLS:-COLS, :])
+                    + column_sum(straight * norm_b[own, :])
+                )
+                * gamma_b,
             ],
             axis=0,
         )
@@ -254,59 +304,55 @@
     sums[...] = jnp.broadcast_to(parts[None], sums.shape)
 
 
-def group_means(totals, gamma, count):
-    return dot(totals * gamma, group_matrix(), highest) * (1.0 / count)
-
-
 def through(incoming, passing, normed, inside, gamma, inverse, means, high, low):
-    wide = dot(means, spread_matrix(), highest)
-    grad = inverse * (incoming * passing * gamma - inside * wide[0:1] - normed * wide[1:2])
+    grad = inverse * (incoming * passing * gamma - inside * means[0:1] - normed * means[1:2])
     return grad, incoming[COLS:-COLS] + conv_back(grad, high, low)
 
 
-def gain_rows(totals):
-    return jnp.concatenate([totals[1:2], totals[0:1]], axis=0)
+def gain_sums(grad_out, normed):
+    return jnp.concatenate([column_sum(grad_out * normed), column_sum(grad_out)], axis=0)
 
 
 def opening_kernel(
-    count, tiles, flags, opening, above, main, below, response, pass_a, norm_a, pass_b, norm_b,
-    params, a_high, a_low, sums, middle, grad_a,
+    tiles, flags, opening, above, main, below, response, pass_a, norm_a, pass_b, norm_b,
+    params, a_high, a_low, sums, middle, grad_a, gain_a,
 ):
     incoming = jnp.concatenate(
         [above[5 * COLS :, :], main[...], below[5 * COLS :, :]], axis=0
     )
-    means = group_means(opening[...], params[0:1, :], count)
     grad, passed = through(
         incoming, pass_a[...], norm_a[...], inside_rows(flags, tiles),
-        params[0:1, :], params[1:2, :], means, a_high, a_low,
+        params[0:1, :], params[1:2, :], opening[...], a_high, a_low,
     )
     middle[...] = passed
     grad_a[...] = grad[2 * COLS : -2 * COLS]
     own = slice(2 * COLS, 2 * COLS + OWN)
+    gain_a[...] = gain_sums(main[...] * pass_a[own, :], norm_a[own, :])
     grad_b = passed[COLS:-COLS] * pass_b[own, :]
-    parts = folded(
+    gamma_b = params[2:3, :]
+    packed = pack(
         jnp.concatenate(
             [
                 jnp.zeros((2, C), f32),
-                column_sum(grad_b),
-                column_sum(grad_b * norm_b[own, :]),
+                column_sum(grad_b) * gamma_b,
+                column_sum(grad_b * norm_b[own, :]) * gamma_b,
             ],
             axis=0,
         )
     )
-    sums[...] = jnp.concatenate(
-        [jnp.broadcast_to(parts[None], (tiles, 8, C // 2)), response[...]], axis=1
-    )
+    sums[:, 0:1, :] = jnp.broadcast_to(packed[None], (tiles, 1, LANES))
+    if tiles == GROUPS:
+        sums[:, 1, :] = response[...]
+    else:
+        sums[:, 1:, :] = response[...].reshape(tiles, GROUPS // tiles, LANES)
 
 
 def closing_kernel(
-    count, tiles, flags, received, opening, middle, grad_a, pass_b, norm_b, params, b_high, b_low,
+    count, tiles, flags, received, middle, grad_a, gain_a, pass_b, norm_b, params, b_high, b_low,
     out, out_head, out_tail, act, grad, gain, share,
 ):
-    totals = jnp.sum(received[...], axis=0)
-    share[...] = totals[8:]
-    totals = jnp.concatenate([totals[:4], totals[4:8]], axis=1)[2:4]
-    means = group_means(totals, params[2:3, :], count)
+    share[...] = jnp.sum(received[:, 1:, :], axis=0)
+    means = unpack(jnp.sum(received[:, 0:1, :], axis=0) * (1.0 / count))[2:4]
     near = middle[...]
     grad_b, last = through(
         near, pass_b[COLS:-COLS, :], norm_b[COLS:-COLS, :],
@@ -318,11 +364,11 @@
     out_tail[...] = last[-2 * COLS :]
     active = flags[0] == 0
     upper = flags[1] == 1
+    own = slice(2 * COLS, 2 * COLS + OWN)
+    gain_b = gain_sums(near[COLS:-COLS] * pass_b[own, :], norm_b[own, :])
     act[...] = jnp.where(active, jnp.where(upper, near[COLS:-COLS], last), 0.0)
     grad[...] = jnp.where(active, jnp.where(upper, grad_a[...], grad_b[COLS:-COLS]), 0.0)
-    gain[...] = jnp.where(
-        active, jnp.where(upper, gain_rows(opening[...]), gain_rows(totals)), 0.0
-    )
+    gain[...] = jnp.where(active, jnp.where(upper, gain_a[...], gain_b), 0.0)
 
 
 def second_kernel(
@@ -331,18 +377,23 @@
     out, out_head, out_tail, act, grad, gain,
 ):
     incoming = jnp.concatenate([top[...], main[...], bottom[...]], axis=0)
-    totals = jnp.sum(received[:, :8, :], axis=0)
-    totals = jnp.concatenate([totals[:4], totals[4:]], axis=1)
-    response = exchanged[:, 8:, :].reshape(GROUPS, 8, C // 2)
-    flat, full = (
-        jnp.concatenate([response[:, start + chunk, :] for chunk in range(4)], axis=1)
-        for start in (0, 4)
-    )
+    means = jnp.sum(received[:, 0:1, :], axis=0) * (1.0 / count)
+    if tiles == GROUPS:
+        response = exchanged[:, 1, :]
+    else:
+        response = exchanged[:, 1:, :].reshape(GROUPS, LANES)
+    right = lane_quarter(GROUPS) >= 2
+    response = jnp.concatenate(
+        [
+            jnp.where(right, pltpu.roll(response, 2 * GROUPS, 1), 0.0),
+            jnp.where(right, response, 0.0),
+            jnp.zeros((2 * GROUPS, LANES), f32),
+        ],
+        axis=0,
+    )
+    means_a = unpack(means)[0:2]
+    means_b = unpack(means - dot(means, response, highest))[2:4]
     inside = inside_rows(flags, tiles)
-    means_a = group_means(totals[0:2], params[0:1, :], count)
-    shift = dot(means_a[0:1], flat, highest) + dot(means_a[1:2], full, highest)
-    totals_b = totals[2:4] - jnp.concatenate([shift[:, :C], shift[:, C:]], axis=0)
-    means_b = group_means(totals_b, params[2:3, :], count)
     grad_a, middle = through(
         incoming, pass_a[...], norm_a[...], inside, params[0:1, :], params[1:2, :],
         means_a, a_high, a_low,
@@ -356,16 +407,17 @@
     out_tail[...] = last[-2 * COLS :]
     active = flags[0] == step
     upper = flags[1] == 1
+    own = slice(2 * COLS, 2 * COLS + OWN)
+    gain_a = gain_sums(main[...] * pass_a[own, :], norm_a[own, :])
+    gain_b = gain_sums(middle[COLS:-COLS] * pass_b[own, :], norm_b[own, :])
     act[...] = jnp.where(active, jnp.where(upper, middle[COLS:-COLS], last), old_act[...])
     grad[...] = jnp.where(
         active, jnp.where(upper, grad_a[2 * COLS : -2 * COLS], grad_b[COLS:-COLS]), old_grad[...]
     )
-    gain[...] = jnp.where(
-        active, jnp.where(upper, gain_rows(totals[0:2]), gain_rows(totals_b)), old_gain[...]
-    )
-
-
-def kernel_grad_kernel(tiles, flags, above, main, below, grad, mine, other):
+    gain[...] = jnp.where(active, jnp.where(upper, gain_a, gain_b), old_gain[...])
+
+
+def kernel_grad_kernel(tiles, flags, above, main, below, grad, gain, mine, other):
     share = C // tiles
     image = jnp.concatenate([above[: 3 * COLS, :], main[...], below[: 3 * COLS, :]], axis=0)
     turned = grad[...].T.reshape(tiles // 2, 2, share, OWN)
@@ -385,6 +437,11 @@
             where = slice((row_tap * 3 + col_tap) * C, (row_tap * 3 + col_tap + 1) * C)
             mine[:, where] = product[: C // 2]
             other[:, where] = product[C // 2 :]
+    half = C // 2
+    eight = jnp.concatenate([gain[:, :half], gain[:, half:], jnp.zeros((4, half), f32)], axis=0)
+    copies = jnp.broadcast_to(eight[None], (half // 8, 8, half)).reshape(half, half)
+    mine[:, 9 * C :] = copies
+    other[:, 9 * C :] = copies
 
 
 def call(body, out_shape, operands, flagged, **options):
@@ -416,7 +473,7 @@
         grid=(9,),
         out_shape=tuple(shape(9, C, C, dtype=bf16) for _ in range(4))
         + tuple(shape(tall, C) for _ in range(4))
-        + (shape(8, C), shape(2, C), shape(GROUPS, 8, C // 2)),
+        + (shape(8, C), shape(2, C), shape(GROUPS, LANES)),
         in_specs=[
             pl.BlockSpec(memory_space=pltpu.SMEM),
             tap(C),
@@ -427,7 +484,7 @@
         ],
         out_specs=tuple(tap(C) for _ in range(4))
         + tuple(whole(tall, C) for _ in range(4))
-        + (whole(8, C), whole(2, C), whole(GROUPS, 8, C // 2)),
+        + (whole(8, C), whole(2, C), whole(GROUPS, LANES)),
         scratch_shapes=[
             pltpu.VMEM((2 * C, OWN), bf16),
             pltpu.VMEM((2 * C, OWN), bf16),
@@ -461,17 +518,18 @@
     near = lax.ppermute(quarters[0], ("member", "z"), route)
     near_two = lax.ppermute(quarters[1], ("member", "z"), route_two)
     flags = jnp.stack([pairs - 1 - pair, member, tile, core]).astype(jnp.int32)
-    acts, pass_mask, cotangent, flags, *quarters = lax.optimization_barrier(
-        (acts, pass_mask, cotangent, flags, *quarters)
-    )
-
-    passing = (
-        pass_mask[0, 0].astype(f32)
-        * (drop_mask[0, 0].astype(f32)[..., None] / keep_drop)
-        * (path_mask[0].astype(f32)[:, None, None] / keep_path)
-    ).reshape(OWN, C)
+    acts, pass_mask, drop_mask, cotangent, flags, *quarters = lax.optimization_barrier(
+        (acts, pass_mask, drop_mask, cotangent, flags, *quarters)
+    )
+
     image = acts[0, 0].reshape(OWN, C)
     start = cotangent[0].reshape(OWN, C)
+    passing, tail, head = call(
+        edge_kernel,
+        (shape(OWN, C), shape(7 * COLS, C), shape(7 * COLS, C)),
+        (path_mask, image, pass_mask[0, 0].reshape(OWN, C), drop_mask[0, 0], start),
+        True,
+    )
 
     def neighbours(value, step, source=None):
         size = 2 * tiles
@@ -488,28 +546,21 @@
             ],
         )
 
-    from_above = neighbours(
-        jnp.concatenate([image[-3 * COLS :], passing[-2 * COLS :], start[-2 * COLS :]]), 1
-    )
-    from_below = neighbours(
-        jnp.concatenate([image[: 3 * COLS], passing[: 2 * COLS], start[: 2 * COLS]]), -1
-    )
+    from_above = neighbours(tail, 1)
+    from_below = neighbours(head, -1)
     tall = 12 * COLS
     edges = (from_above, image, from_below)
     fields, sums = call(
         forward_kernel,
-        (shape(2 * tall + 8, C), shape(2 * tiles, 8, C // 2)),
+        (shape(2 * tall + 8, C), shape(2 * tiles, 1, LANES)),
         edges + (passing, start, own_kernel, gammas),
         False,
     )
     partner_fields = lax.ppermute(fields, "member", swap)
-    near, near_two, partner_fields, sums = lax.optimization_barrier(
-        (near, near_two, partner_fields, sums)
-    )
+    gathered = lax.all_to_all(sums, ("member",) + TILE, 0, 0)
+    near, near_two, gathered = lax.optimization_barrier((near, near_two, gathered))
     far = lax.ppermute(near, "core", swap)
     far_two = lax.ppermute(near_two, "core", swap)
-    far, far_two, sums = lax.optimization_barrier((far, far_two, sums))
-    gathered = lax.all_to_all(sums, ("member",) + TILE, 0, 0)
     prepared = prepare(
         tiles, count, flags, own_kernel, (near, near_two, far, far_two), gathered, fields,
         partner_fields,
@@ -517,8 +568,7 @@
     a_high, a_low, b_high, b_low = (w.reshape(3, 3 * C, C) for w in prepared[:4])
     masks, params, opening, response = prepared[4:8], prepared[8], prepared[9], prepared[10]
     piece = GROUPS // tiles
-    block = 8 + piece * 8
-    response = response.reshape(tiles, piece * 8, C // 2)
+    block = 1 + piece
     shared = masks + (params, a_high, a_low)
     rows_out = (
         shape(OWN, C),
@@ -529,17 +579,17 @@
         shape(2, C),
     )
 
-    sums, middle, grad_a = call(
-        functools.partial(opening_kernel, count, tiles),
-        (shape(tiles, block, C // 2), shape(OWN + 2 * COLS, C), shape(OWN, C)),
+    sums, middle, grad_a, gain_a = call(
+        functools.partial(opening_kernel, tiles),
+        (shape(tiles, block, LANES), shape(OWN + 2 * COLS, C), shape(OWN, C), shape(2, C)),
         (flags, opening, from_above, start, from_below, response) + shared,
         True,
     )
     received = lax.all_to_all(sums, TILE, 0, 0)
     main, head, tail, act, grad, gain, share = call(
         functools.partial(closing_kernel, count, tiles),
-        rows_out + (shape(piece * 8, C // 2),),
-        (flags, received, opening, middle, grad_a) + masks[2:] + (params, b_high, b_low),
+        rows_out + (shape(piece, LANES),),
+        (flags, received, middle, grad_a, gain_a) + masks[2:] + (params, b_high, b_low),
         True,
     )
     exchanged = None
@@ -550,9 +600,9 @@
             neighbours(head, -1, pairs - step),
         )
         if step == 1:
-            sums = call(sharing_kernel, shape(tiles, block, C // 2), (share, main) + shared, False)
+            sums = call(sharing_kernel, shape(tiles, block, LANES), (share, main) + shared, False)
         else:
-            sums = call(first_kernel, shape(tiles, 8, C // 2), (main,) + shared, False)
+            sums = call(first_kernel, shape(tiles, 1, LANES), (main,) + shared, False)
         sums, top, bottom = lax.optimization_barrier((sums, top, bottom))
         received = lax.all_to_all(sums, TILE, 0, 0)
         if step == 1:
@@ -566,20 +616,21 @@
             True,
         )
 
+    width = 9 * C + C // 2
     mine, other = call(
         functools.partial(kernel_grad_kernel, tiles),
-        (shape(C // 2, 9 * C), shape(C // 2, 9 * C)),
-        (flags,) + edges + (grad,),
+        (shape(C // 2, width), shape(C // 2, width)),
+        (flags,) + edges + (grad, gain),
         True,
     )
-    share = C // tiles
     mine = mine + lax.ppermute(other, "core", swap)
     for axis in ("x", "z"):
         parts = lax.axis_size(axis)
         mine = jnp.sum(
-            lax.all_to_all(mine.reshape(parts, mine.shape[0] // parts, 9 * C), axis, 0, 0), axis=0
-        )
-    kernel_share = jnp.transpose(mine.reshape(share, 3, 3, C), (1, 2, 3, 0))
+            lax.all_to_all(mine.reshape(parts, mine.shape[0] // parts, width), axis, 0, 0), axis=0
+        )
+    kernel_share = jnp.transpose(mine[:, : 9 * C].reshape(C // tiles, 3, 3, C), (1, 2, 3, 0))
+    gain = jnp.concatenate([mine[0:2, 9 * C :], mine[2:4, 9 * C :]], axis=1)
     return (
         act.reshape(1, 1, ROWS, COLS, C),
         kernel_share[None],

time: 348 us -> 324 us (0.931)
  blocking collectives: 176 us -> 156 us
    all_to_all x8, blocking collectives: 121 us -> 105 us  [on_device(): received = lax.all_to_all(sums, TILE, 0, 0)]
    all_to_all x1, blocking collectives: 21.3 us -> 16.3 us  [on_device(): gathered = lax.all_to_all(sums, ('member',) + TILE, 0, 0)]
    pallas_call x18 -> x19, Pallas kernels: 36.5 us -> 35 us  [call(): pl.pallas_call(body, out_shape=out_shape, in_specs=in_specs, out_specs=tu...]
  transfers between devices with their start and end apart: 29 -> 29, of which waited for: 6 -> 4; matrix products, arithmetic and copies ran while one was open for 1% -> 0% of each run, Pallas kernels for 2% -> 2%
where the time goes in v4:
time: 324 us; the launch traced here: 323 us
  blocking collectives  156 us (48%)
  waiting for transfers between devices  71.2 us (22%)
  starting transfers between devices  46.4 us (14%)
  Pallas kernels  43.8 us (14%)
    all_to_all x8, blocking collectives, on_device(): received = lax.all_to_all(sums, TILE, 0, 0)  105 us
    ppermute x23, waiting for transfers between devices, neighbours(): lax.ppermute(value, ALL, [(i, i - jump + step) for i in range(first, last...  57.9 us
    pallas_call x19, Pallas kernels, call(): pl.pallas_call(body, out_shape=out_shape, in_specs=in_specs, out_specs=tu...  35 us
    all_to_all x2, blocking collectives, on_device(): lax.all_to_all(mine.reshape(parts, mine.shape[0] // parts, width), axis,...  34.7 us
    ppermute x23, starting transfers between devices, neighbours(): lax.ppermute(value, ALL, [(i, i - jump + step) for i in range(first, last...  24.6 us
    all_to_all x1, blocking collectives, on_device(): gathered = lax.all_to_all(sums, ('member',) + TILE, 0, 0)  16.3 us
    ppermute x1, starting transfers between devices, on_device(): near_two = lax.ppermute(quarters[1], ('member', 'z'), route_two)  10.9 us
    ppermute x1, waiting for transfers between devices, on_device(): partner_fields = lax.ppermute(fields, 'member', swap)  10.4 us
  transfers between devices with their start and end apart: 29, of which 4 were waited for; matrix products, arithmetic and copies ran while one was open for 0% of the time, Pallas kernels for 2%

profile of v4, /device:TPU:2, one launch (start us, length us, event | category | flops | bytes accessed | tf_op | source)
XLA Modules:
  0.0 323.1 jit_solution(8795712471502149824)
XLA Ops:
  3.2 10.9 %collective-permute-start.1 = (f32[9,64,256]{2,1,0:T(8,128)}, f32[9,64,256]{2,1,0:T(8,128)S(1)}, u32[]{:S(2)}, u32[]{:S(2)}) collective-permute-start(f32[9,64,256]{2,1,0:T(8,128)} %get-tuple-element.197), channel_id=1, source_target_pairs={{0,38},{2,32},{4,34},{6,36},{38,0},{32,2},{34,4},{36,6},{1,39},{3,... | collective-permute-start | bytes 1769480 | tf_op jit(solution)/shard_map/ppermute | solution.py:519
  19.0 6.7 %collective-permute-start.3 = (f32[112,256]{1,0:T(8,128)S(1)}, f32[112,256]{1,0:T(8,128)S(1)}, u32[]{:S(2)}, u32[]{:S(2)}) collective-permute-start(f32[112,256]{1,0:T(8,128)S(1)} %get-tuple-element.106), channel_id=1, source_target_pairs={{1,0},{2,1},{3,2},{4,3},{5,4},{6,5},{7,6},{8,7},{9,8},{10,9},{11,1... | collective-permute-start | bytes 344072 | tf_op jit(solution)/shard_map/ppermute | solution.py:539
  25.7 7.6 %collective-permute-done.2.above = f32[112,256]{1,0:T(8,128)S(1)} collective-permute-done((f32[112,256]{1,0:T(8,128)S(1)}, f32[112,256]{1,0:T(8,128)S(1)}, u32[]{:S(2)}, u32[]{:S(2)}) %collective-permute-start.2) | collective-permute-done | bytes 114720 | tf_op jit(solution)/shard_map/ppermute | solution.py:539
  34.3 16.3 %all_to_all.55.gathered = f32[64,1,128]{2,1,0:T(1,128)S(1)} all-to-all(f32[64,1,128]{2,1,0:T(1,128)S(1)} %get-tuple-element.108), channel_id=1, replica_groups=mesh['pair'=8,'member'=2,'x'=4,'z'=4,'core'=2] {'member','x','z','core'}, dimensions={0} | all-to-all | bytes 65536 | tf_op jit(solution)/shard_map/all_to_all | solution.py:560
  57.6 10.4 %collective-permute-done.6.partner_fields = f32[392,256]{1,0:T(8,128)S(1)} collective-permute-done((f32[392,256]{1,0:T(8,128)S(1)}, f32[392,256]{1,0:T(8,128)S(1)}, u32[]{:S(2)}, u32[]{:S(2)}) %collective-permute-start.6) | collective-permute-done | bytes 401440 | tf_op jit(solution)/shard_map/ppermute | solution.py:559
  68.1 8.9 %shard_map.96 = (bf16[9,256,256]{2,1,0:T(8,128)(2,1)S(1)}, bf16[9,256,256]{2,1,0:T(8,128)(2,1)S(1)}, bf16[9,256,256]{2,1,0:T(8,128)(2,1)S(1)}, bf16[9,256,256]{2...) custom-call(s32[4]{0:T(128)S(1)} %pad_add_fusion.flags, ...), custom_call_target="tpu_custom_call" | custom-call | tf_op jit(solution)/shard_map/pallas_call | solution.py:471
  78.5 12.8 %all_to_all.56.received = f32[32,2,128]{2,1,0:T(2,128)S(1)} all-to-all(f32[32,2,128]{2,1,0:T(2,128)S(1)} %get-tuple-element.122), channel_id=1, replica_groups=mesh['pair'=8,'member'=2,'x'=4,'z'=4,'core'=2] {'x','z','core'}, dimensions={0} | all-to-all | bytes 65536 | tf_op jit(solution)/shard_map/all_to_all | solution.py:588
  95.6 12.8 %all_to_all.57.received.exchanged = f32[32,2,128]{2,1,0:T(2,128)S(1)} all-to-all(f32[32,2,128]{2,1,0:T(2,128)S(1)} %shard_map.99), channel_id=1, replica_groups=mesh['pair'=8,'member'=2,'x'=4,'z'=4,'core'=2] {'x','z','core'}, dimensions={0} | all-to-all | bytes 65536 | tf_op jit(solution)/shard_map/all_to_all | solution.py:607
  108.4 3.1 shard_map.100
  114.5 12.7 %all_to_all.58.received = f32[32,1,128]{2,1,0:T(1,128)S(1)} all-to-all(f32[32,1,128]{2,1,0:T(1,128)S(1)} %shard_map.101), channel_id=1, replica_groups=mesh['pair'=8,'member'=2,'x'=4,'z'=4,'core'=2] {'x','z','core'}, dimensions={0} | all-to-all | bytes 32768 | tf_op jit(solution)/shard_map/all_to_all | solution.py:607
  127.3 3.1 shard_map.102
  133.4 12.7 %all_to_all.59.received = f32[32,1,128]{2,1,0:T(1,128)S(1)} all-to-all(f32[32,1,128]{2,1,0:T(1,128)S(1)} %shard_map.103), channel_id=1, replica_groups=mesh['pair'=8,'member'=2,'x'=4,'z'=4,'core'=2] {'x','z','core'}, dimensions={0} | all-to-all | bytes 32768 | tf_op jit(solution)/shard_map/all_to_all | solution.py:607
  146.1 3.1 shard_map.104
  152.2 12.7 %all_to_all.60.received = f32[32,1,128]{2,1,0:T(1,128)S(1)} all-to-all(f32[32,1,128]{2,1,0:T(1,128)S(1)} %shard_map.105), channel_id=1, replica_groups=mesh['pair'=8,'member'=2,'x'=4,'z'=4,'core'=2] {'x','z','core'}, dimensions={0} | all-to-all | bytes 32768 | tf_op jit(solution)/shard_map/all_to_all | solution.py:607
  165.0 3.1 shard_map.106
  171.1 12.7 %all_to_all.61.received = f32[32,1,128]{2,1,0:T(1,128)S(1)} all-to-all(f32[32,1,128]{2,1,0:T(1,128)S(1)} %shard_map.107), channel_id=1, replica_groups=mesh['pair'=8,'member'=2,'x'=4,'z'=4,'core'=2] {'x','z','core'}, dimensions={0} | all-to-all | bytes 32768 | tf_op jit(solution)/shard_map/all_to_all | solution.py:607
  183.8 3.1 shard_map.108
  190.2 12.7 %all_to_all.62.received = f32[32,1,128]{2,1,0:T(1,128)S(1)} all-to-all(f32[32,1,128]{2,1,0:T(1,128)S(1)} %shard_map.109), channel_id=1, replica_groups=mesh['pair'=8,'member'=2,'x'=4,'z'=4,'core'=2] {'x','z','core'}, dimensions={0} | all-to-all | bytes 32768 | tf_op jit(solution)/shard_map/all_to_all | solution.py:607
  202.9 3.1 shard_map.110
  209.9 50.3 %collective-permute-done.25.main = f32[128,256]{1,0:T(8,128)S(1)} collective-permute-done((f32[128,256]{1,0:T(8,128)S(1)}, f32[128,256]{1,0:T(8,128)S(1)}, u32[]{:S(2)}, u32[]{:S(2)}) %collective-permute-start.25) | collective-permute-done | bytes 131104 | tf_op jit(solution)/shard_map/ppermute | solution.py:539
  261.2 15.4 %all_to_all.63.received = f32[32,1,128]{2,1,0:T(1,128)S(1)} all-to-all(f32[32,1,128]{2,1,0:T(1,128)S(1)} %shard_map.111), channel_id=1, replica_groups=mesh['pair'=8,'member'=2,'x'=4,'z'=4,'core'=2] {'x','z','core'}, dimensions={0} | all-to-all | bytes 32768 | tf_op jit(solution)/shard_map/all_to_all | solution.py:607
  276.6 3.8 %shard_map.112 = (f32[128,256]{1,0:T(8,128)}, f32[32,256]{1,0:T(8,128)}, f32[32,256]{1,0:T(8,128)}, f32[128,256]{1,0:T(8,128)}, f32[128,256]{1,0:T(8,128)S(1)}, /*index=5*/f32[2,256]{1,0:T(2,128)S(1)}) custom-call(s32[4]{0:T(128)S(1)} %pad_add_fusion.flags, f32[32,1,128]{2,1,0:T(1,128)S(1)} %all_to_all.63.received, ...), custom_call_target="tpu_custom_call" | custom-call | tf_op jit(solution)/shard_map/pallas_call | solution.py:453
  287.1 20.1 %all_to_all.64 = f32[4,32,2432]{2,1,0:T(8,128)S(1)} all-to-all(f32[4,32,2432]{2,1,0:T(8,128)S(1)} %bitcast.80), channel_id=1, replica_groups=mesh['pair'=8,'member'=2,'x'=4,'z'=4,'core'=2] {'x'}, dimensions={0} | all-to-all | bytes 2490368 | tf_op jit(solution)/shard_map/all_to_all | solution.py:630
  307.4 14.5 %all_to_all.65 = f32[4,8,2432]{2,1,0:T(8,128)S(1)} all-to-all(f32[4,8,2432]{2,1,0:T(8,128)S(1)} %bitcast.81), channel_id=1, replica_groups=mesh['pair'=8,'member'=2,'x'=4,'z'=4,'core'=2] {'z'}, dimensions={0} | all-to-all | bytes 622592 | tf_op jit(solution)/shard_map/all_to_all | solution.py:630
  (85 shorter events, 48.3 us)
Async XLA Ops:
  3.2 47.4 %collective-permute-start.1 = (f32[9,64,256]{2,1,0:T(8,128)}, f32[9,64,256]{2,1,0:T(8,128)S(1)}, u32[]{:S(2)}, u32[]{:S(2)}) collective-permute-start(f32[9,64,256]{2,1,0:T(8,128)} %get-tuple-element.197), channel_id=1, source_target_pairs={{0,38},{2,32},{4,34},{6,36},{38,0},{32,2},{34,4},{36,6},{1,39},{3,... | collective-permute-start | bytes 1769480 | tf_op jit(solution)/shard_map/ppermute | solution.py:519
  14.2 36.5 %collective-permute-start = (f32[9,64,256]{2,1,0:T(8,128)}, f32[9,64,256]{2,1,0:T(8,128)}, u32[]{:S(2)}, u32[]{:S(2)}) collective-permute-start(f32[9,64,256]{2,1,0:T(8,128)} %get-tuple-element.198), channel_id=1, source_target_pairs={{0,32},{2,34},{4,36},{6,38},{32,0},{34,2},{36,4},{38,6},{1,33},{3,... | collective-permute-start | bytes 1769480 | tf_op jit(solution)/shard_map/ppermute | solution.py:518
  17.1 16.1 %collective-permute-start.2 = (f32[112,256]{1,0:T(8,128)S(1)}, f32[112,256]{1,0:T(8,128)S(1)}, u32[]{:S(2)}, u32[]{:S(2)}) collective-permute-start(f32[112,256]{1,0:T(8,128)S(1)} %get-tuple-element.105), channel_id=1, source_target_pairs={{0,1},{1,2},{2,3},{3,4},{4,5},{5,6},{6,7},{7,8},{8,9},{9,10},{10,1... | collective-permute-start | bytes 344072 | tf_op jit(solution)/shard_map/ppermute | solution.py:539
  19.0 14.2 %collective-permute-start.3 = (f32[112,256]{1,0:T(8,128)S(1)}, f32[112,256]{1,0:T(8,128)S(1)}, u32[]{:S(2)}, u32[]{:S(2)}) collective-permute-start(f32[112,256]{1,0:T(8,128)S(1)} %get-tuple-element.106), channel_id=1, source_target_pairs={{1,0},{2,1},{3,2},{4,3},{5,4},{6,5},{7,6},{8,7},{9,8},{10,9},{11,1... | collective-permute-start | bytes 344072 | tf_op jit(solution)/shard_map/ppermute | solution.py:539
  50.6 17.4 %collective-permute-start.4 = (f32[9,64,256]{2,1,0:T(8,128)}, f32[9,64,256]{2,1,0:T(8,128)S(1)}, u32[]{:S(2)}, u32[]{:S(2)}) collective-permute-start(f32[9,64,256]{2,1,0:T(8,128)} %collective-permute-done.near), channel_id=1, source_target_pairs={{0,1},{1,0},{2,3},{3,2},{4,5},{5,4},{6,7},{7,6},{8,9},{9,8},{10,11... | collective-permute-start | bytes 1769480 | tf_op jit(solution)/shard_map/ppermute | solution.py:562
  52.6 15.5 %collective-permute-start.5 = (f32[9,64,256]{2,1,0:T(8,128)S(1)}, f32[9,64,256]{2,1,0:T(8,128)S(1)}, u32[]{:S(2)}, u32[]{:S(2)}) collective-permute-start(f32[9,64,256]{2,1,0:T(8,128)S(1)} %collective-permute-done.1.near_two), channel_id=1, source_target_pairs={{0,1},{1,0},{2,3},{3,2},{4,5},{5,4},{6,7},{7,6},{8,9},{9,8},{10,11... | collective-permute-start | bytes 1769480 | tf_op jit(solution)/shard_map/ppermute | solution.py:563
  55.0 13.1 %collective-permute-start.6 = (f32[392,256]{1,0:T(8,128)S(1)}, f32[392,256]{1,0:T(8,128)S(1)}, u32[]{:S(2)}, u32[]{:S(2)}) collective-permute-start(f32[392,256]{1,0:T(8,128)S(1)} %get-tuple-element.112.fields), channel_id=1, source_target_pairs={{0,32},{32,0},{1,33},{33,1},{2,34},{34,2},{3,35},{35,3},{4,36},{36... | collective-permute-start | bytes 1204232 | tf_op jit(solution)/shard_map/ppermute | solution.py:559
  92.6 2.0 collective-permute-start.7
  93.3 2.3 collective-permute-start.8
  111.5 2.0 collective-permute-start.10
  112.2 2.3 collective-permute-start.11
  130.4 2.0 collective-permute-start.13
  131.1 2.3 collective-permute-start.14
  149.3 2.0 collective-permute-start.16
  149.9 2.3 collective-permute-start.17
  168.1 2.0 collective-permute-start.19
  168.8 2.3 collective-permute-start.20
  187.0 2.2 collective-permute-start.22
  187.7 2.5 collective-permute-start.23
  188.3 1.9 collective-permute-start.24
  206.1 54.2 %collective-permute-start.25 = (f32[128,256]{1,0:T(8,128)S(1)}, f32[128,256]{1,0:T(8,128)S(1)}, u32[]{:S(2)}, u32[]{:S(2)}) collective-permute-start(f32[128,256]{1,0:T(8,128)S(1)} %get-tuple-element.183), channel_id=1, source_target_pairs={{64,0},{65,1},{66,2},{67,3},{68,4},{69,5},{70,6},{71,7},{72,8},{73... | collective-permute-start | bytes 393224 | tf_op jit(solution)/shard_map/ppermute | solution.py:539
  207.3 53.8 %collective-permute-start.26 = (f32[32,256]{1,0:T(8,128)S(1)}, f32[32,256]{1,0:T(8,128)S(1)}, u32[]{:S(2)}, u32[]{:S(2)}) collective-permute-start(f32[32,256]{1,0:T(8,128)S(1)} %get-tuple-element.184), channel_id=1, source_target_pairs={{64,1},{65,2},{66,3},{67,4},{68,5},{69,6},{70,7},{71,8},{72,9},{73... | collective-permute-start | bytes 98312 | tf_op jit(solution)/shard_map/ppermute | solution.py:539
  208.7 52.5 %collective-permute-start.27 = (f32[32,256]{1,0:T(8,128)S(1)}, f32[32,256]{1,0:T(8,128)S(1)}, u32[]{:S(2)}, u32[]{:S(2)}) collective-permute-start(f32[32,256]{1,0:T(8,128)S(1)} %get-tuple-element.185), channel_id=1, source_target_pairs={{65,0},{66,1},{67,2},{68,3},{69,4},{70,5},{71,6},{72,7},{73,8},{74... | collective-permute-start | bytes 98312 | tf_op jit(solution)/shard_map/ppermute | solution.py:539
  282.1 4.8 %collective-permute-start.28 = (f32[128,2432]{1,0:T(8,128)S(1)}, f32[128,2432]{1,0:T(8,128)S(1)}, u32[]{:S(2)}, u32[]{:S(2)}) collective-permute-start(f32[128,2432]{1,0:T(8,128)S(1)} %get-tuple-element.196), channel_id=1, source_target_pairs={{0,1},{1,0},{2,3},{3,2},{4,5},{5,4},{6,7},{7,6},{8,9},{9,8},{10,11... | collective-permute-start | bytes 3735560 | tf_op jit(solution)/shard_map/ppermute | solution.py:626
  (11 other events, 138.1 us)

commit v5 on v4

--- a/solution.py
+++ b/solution.py
@@ -505,6 +505,15 @@
     count = tiles * OWN * (C // GROUPS)
     swap = [(0, 1), (1, 0)]
 
+    image = acts[0, 0].reshape(OWN, C)
+    start = cotangent[0].reshape(OWN, C)
+    passing, tail, head = call(
+        edge_kernel,
+        (shape(OWN, C), shape(7 * COLS, C), shape(7 * COLS, C)),
+        (path_mask, image, pass_mask[0, 0].reshape(OWN, C), drop_mask[0, 0], start),
+        True,
+    )
+
     own_kernel = kernels[0].reshape(9, C, C)
     quarters = [
         lax.dynamic_slice_in_dim(own_kernel, core * (C // 2) + q * (C // 4), C // 4, axis=1)
@@ -518,18 +527,6 @@
     near = lax.ppermute(quarters[0], ("member", "z"), route)
     near_two = lax.ppermute(quarters[1], ("member", "z"), route_two)
     flags = jnp.stack([pairs - 1 - pair, member, tile, core]).astype(jnp.int32)
-    acts, pass_mask, drop_mask, cotangent, flags, *quarters = lax.optimization_barrier(
-        (acts, pass_mask, drop_mask, cotangent, flags, *quarters)
-    )
-
-    image = acts[0, 0].reshape(OWN, C)
-    start = cotangent[0].reshape(OWN, C)
-    passing, tail, head = call(
-        edge_kernel,
-        (shape(OWN, C), shape(7 * COLS, C), shape(7 * COLS, C)),
-        (path_mask, image, pass_mask[0, 0].reshape(OWN, C), drop_mask[0, 0], start),
-        True,
-    )
 
     def neighbours(value, step, source=None):
         size = 2 * tiles
@@ -558,7 +555,9 @@
     )
     partner_fields = lax.ppermute(fields, "member", swap)
     gathered = lax.all_to_all(sums, ("member",) + TILE, 0, 0)
-    near, near_two, gathered = lax.optimization_barrier((near, near_two, gathered))
+    near, near_two, gathered, partner_fields = lax.optimization_barrier(
+        (near, near_two, gathered, partner_fields)
+    )
     far = lax.ppermute(near, "core", swap)
     far_two = lax.ppermute(near_two, "core", swap)
     prepared = prepare(

time: 324 us -> 319 us (0.985)
  waiting for transfers between devices: 71.2 us -> 62.3 us
    ppermute x1, waiting for transfers between devices: 10.4 us -> 0.01 us  [on_device(): partner_fields = lax.ppermute(fields, 'member', swap)]
    unnamed x12 -> x20, local copies, waits for them, and re-layouts: 0.03 us -> 3.52 us
where the time goes in v5:
time: 319 us; the launch traced here: 318 us
  blocking collectives  157 us (49%)
  waiting for transfers between devices  62.3 us (20%)
  starting transfers between devices  45.7 us (14%)
  Pallas kernels  44.1 us (14%)
  local copies, waits for them, and re-layouts  5.65 us (2%)
    all_to_all x8, blocking collectives, on_device(): received = lax.all_to_all(sums, TILE, 0, 0)  105 us
    ppermute x23, waiting for transfers between devices, neighbours(): lax.ppermute(value, ALL, [(i, i - jump + step) for i in range(first, last...  57.8 us
    pallas_call x19, Pallas kernels, call(): pl.pallas_call(body, out_shape=out_shape, in_specs=in_specs, out_specs=tu...  35 us
    all_to_all x2, blocking collectives, on_device(): lax.all_to_all(mine.reshape(parts, mine.shape[0] // parts, width), axis,...  34.7 us
    ppermute x23, starting transfers between devices, neighbours(): lax.ppermute(value, ALL, [(i, i - jump + step) for i in range(first, last...  24.6 us
    all_to_all x1, blocking collectives, on_device(): gathered = lax.all_to_all(sums, ('member',) + TILE, 0, 0)  18 us
    ppermute x1, starting transfers between devices, on_device(): near_two = lax.ppermute(quarters[1], ('member', 'z'), route_two)  10.9 us
    pallas_call x1, Pallas kernels, prepare(): pl.pallas_call(functools.partial(prepare_kernel, tiles, count), grid=(9,)...  9.16 us
  transfers between devices with their start and end apart: 29, of which 4 were waited for; matrix products, arithmetic and copies ran while one was open for 0% of the time, Pallas kernels for 2%

profile of v5, /device:TPU:2, one launch (start us, length us, event | category | flops | bytes accessed | tf_op | source)
XLA Modules:
  0.0 318.0 jit_solution(15232531005994109055)
XLA Ops:
  2.2 10.9 %collective-permute-start.1 = (f32[9,64,256]{2,1,0:T(8,128)S(1)}, f32[9,64,256]{2,1,0:T(8,128)S(1)}, u32[]{:S(2)}, u32[]{:S(2)}) collective-permute-start(f32[9,64,256]{2,1,0:T(8,128)S(1)} %get-tuple-element.189), channel_id=1, source_target_pairs={{0,38},{2,32},{4,34},{6,36},{38,0},{32,2},{34,4},{36,6},{1,39},{3,... | collective-permute-start | bytes 1769480 | tf_op jit(solution)/shard_map/ppermute | solution.py:528
  17.9 6.7 %collective-permute-start.3 = (f32[112,256]{1,0:T(8,128)S(1)}, f32[112,256]{1,0:T(8,128)S(1)}, u32[]{:S(2)}, u32[]{:S(2)}) collective-permute-start(f32[112,256]{1,0:T(8,128)S(1)} %get-tuple-element.97), channel_id=1, source_target_pairs={{1,0},{2,1},{3,2},{4,3},{5,4},{6,5},{7,6},{8,7},{9,8},{10,9},{11,1... | collective-permute-start | bytes 344072 | tf_op jit(solution)/shard_map/ppermute | solution.py:536
  24.6 7.4 %collective-permute-done.2.above = f32[112,256]{1,0:T(8,128)S(1)} collective-permute-done((f32[112,256]{1,0:T(8,128)S(1)}, f32[112,256]{1,0:T(8,128)S(1)}, u32[]{:S(2)}, u32[]{:S(2)}) %collective-permute-start.2) | collective-permute-done | bytes 114720 | tf_op jit(solution)/shard_map/ppermute | solution.py:536
  35.7 18.0 %all_to_all.55.gathered = f32[64,1,128]{2,1,0:T(1,128)S(1)} all-to-all(f32[64,1,128]{2,1,0:T(1,128)S(1)} %get-tuple-element.99), channel_id=1, replica_groups=mesh['pair'=8,'member'=2,'x'=4,'z'=4,'core'=2] {'member','x','z','core'}, dimensions={0} | all-to-all | bytes 65536 | tf_op jit(solution)/shard_map/all_to_all | solution.py:557
  62.6 9.2 %shard_map.96 = (bf16[9,256,256]{2,1,0:T(8,128)(2,1)S(1)}, bf16[9,256,256]{2,1,0:T(8,128)(2,1)S(1)}, bf16[9,256,256]{2,1,0:T(8,128)(2,1)S(1)}, bf16[9,256,256]{2...) custom-call(s32[4]{0:T(128)S(1)} %pad_add_fusion.flags, ...), custom_call_target="tpu_custom_call" | custom-call | tf_op jit(solution)/shard_map/pallas_call | solution.py:471
  73.3 12.8 %all_to_all.56.received = f32[32,2,128]{2,1,0:T(2,128)S(1)} all-to-all(f32[32,2,128]{2,1,0:T(2,128)S(1)} %get-tuple-element.114), channel_id=1, replica_groups=mesh['pair'=8,'member'=2,'x'=4,'z'=4,'core'=2] {'x','z','core'}, dimensions={0} | all-to-all | bytes 65536 | tf_op jit(solution)/shard_map/all_to_all | solution.py:587
  90.5 12.8 %all_to_all.57.received.exchanged = f32[32,2,128]{2,1,0:T(2,128)S(1)} all-to-all(f32[32,2,128]{2,1,0:T(2,128)S(1)} %shard_map.99), channel_id=1, replica_groups=mesh['pair'=8,'member'=2,'x'=4,'z'=4,'core'=2] {'x','z','core'}, dimensions={0} | all-to-all | bytes 65536 | tf_op jit(solution)/shard_map/all_to_all | solution.py:606
  103.2 3.1 shard_map.100
  109.4 12.7 %all_to_all.58.received = f32[32,1,128]{2,1,0:T(1,128)S(1)} all-to-all(f32[32,1,128]{2,1,0:T(1,128)S(1)} %shard_map.101), channel_id=1, replica_groups=mesh['pair'=8,'member'=2,'x'=4,'z'=4,'core'=2] {'x','z','core'}, dimensions={0} | all-to-all | bytes 32768 | tf_op jit(solution)/shard_map/all_to_all | solution.py:606
  122.1 3.1 shard_map.102
  128.2 12.7 %all_to_all.59.received = f32[32,1,128]{2,1,0:T(1,128)S(1)} all-to-all(f32[32,1,128]{2,1,0:T(1,128)S(1)} %shard_map.103), channel_id=1, replica_groups=mesh['pair'=8,'member'=2,'x'=4,'z'=4,'core'=2] {'x','z','core'}, dimensions={0} | all-to-all | bytes 32768 | tf_op jit(solution)/shard_map/all_to_all | solution.py:606
  141.0 3.1 shard_map.104
  147.1 12.7 %all_to_all.60.received = f32[32,1,128]{2,1,0:T(1,128)S(1)} all-to-all(f32[32,1,128]{2,1,0:T(1,128)S(1)} %shard_map.105), channel_id=1, replica_groups=mesh['pair'=8,'member'=2,'x'=4,'z'=4,'core'=2] {'x','z','core'}, dimensions={0} | all-to-all | bytes 32768 | tf_op jit(solution)/shard_map/all_to_all | solution.py:606
  159.8 3.1 shard_map.106
  165.9 12.7 %all_to_all.61.received = f32[32,1,128]{2,1,0:T(1,128)S(1)} all-to-all(f32[32,1,128]{2,1,0:T(1,128)S(1)} %shard_map.107), channel_id=1, replica_groups=mesh['pair'=8,'member'=2,'x'=4,'z'=4,'core'=2] {'x','z','core'}, dimensions={0} | all-to-all | bytes 32768 | tf_op jit(solution)/shard_map/all_to_all | solution.py:606
  178.7 3.1 shard_map.108
  185.0 12.7 %all_to_all.62.received = f32[32,1,128]{2,1,0:T(1,128)S(1)} all-to-all(f32[32,1,128]{2,1,0:T(1,128)S(1)} %shard_map.109), channel_id=1, replica_groups=mesh['pair'=8,'member'=2,'x'=4,'z'=4,'core'=2] {'x','z','core'}, dimensions={0} | all-to-all | bytes 32768 | tf_op jit(solution)/shard_map/all_to_all | solution.py:606
  197.7 3.1 shard_map.110
  204.8 50.3 %collective-permute-done.25.main = f32[128,256]{1,0:T(8,128)S(1)} collective-permute-done((f32[128,256]{1,0:T(8,128)S(1)}, f32[128,256]{1,0:T(8,128)S(1)}, u32[]{:S(2)}, u32[]{:S(2)}) %collective-permute-start.25) | collective-permute-done | bytes 131104 | tf_op jit(solution)/shard_map/ppermute | solution.py:536
  256.0 15.4 %all_to_all.63.received = f32[32,1,128]{2,1,0:T(1,128)S(1)} all-to-all(f32[32,1,128]{2,1,0:T(1,128)S(1)} %shard_map.111), channel_id=1, replica_groups=mesh['pair'=8,'member'=2,'x'=4,'z'=4,'core'=2] {'x','z','core'}, dimensions={0} | all-to-all | bytes 32768 | tf_op jit(solution)/shard_map/all_to_all | solution.py:606
  271.5 3.8 %shard_map.112 = (f32[128,256]{1,0:T(8,128)}, f32[32,256]{1,0:T(8,128)}, f32[32,256]{1,0:T(8,128)}, f32[128,256]{1,0:T(8,128)}, f32[128,256]{1,0:T(8,128)S(1)}, /*index=5*/f32[2,256]{1,0:T(2,128)S(1)}) custom-call(s32[4]{0:T(128)S(1)} %pad_add_fusion.flags, f32[32,1,128]{2,1,0:T(1,128)S(1)} %all_to_all.63.received, ...), custom_call_target="tpu_custom_call" | custom-call | tf_op jit(solution)/shard_map/pallas_call | solution.py:453
  278.9 2.9 collective-permute-done.28
  282.0 20.1 %all_to_all.64 = f32[4,32,2432]{2,1,0:T(8,128)S(1)} all-to-all(f32[4,32,2432]{2,1,0:T(8,128)S(1)} %bitcast.80), channel_id=1, replica_groups=mesh['pair'=8,'member'=2,'x'=4,'z'=4,'core'=2] {'x'}, dimensions={0} | all-to-all | bytes 2490368 | tf_op jit(solution)/shard_map/all_to_all | solution.py:629
  302.2 14.5 %all_to_all.65 = f32[4,8,2432]{2,1,0:T(8,128)S(1)} all-to-all(f32[4,8,2432]{2,1,0:T(8,128)S(1)} %bitcast.81), channel_id=1, replica_groups=mesh['pair'=8,'member'=2,'x'=4,'z'=4,'core'=2] {'z'}, dimensions={0} | all-to-all | bytes 622592 | tf_op jit(solution)/shard_map/all_to_all | solution.py:629
  (93 shorter events, 48.7 us)
Async XLA Ops:
  2.2 52.4 %collective-permute-start.1 = (f32[9,64,256]{2,1,0:T(8,128)S(1)}, f32[9,64,256]{2,1,0:T(8,128)S(1)}, u32[]{:S(2)}, u32[]{:S(2)}) collective-permute-start(f32[9,64,256]{2,1,0:T(8,128)S(1)} %get-tuple-element.189), channel_id=1, source_target_pairs={{0,38},{2,32},{4,34},{6,36},{38,0},{32,2},{34,4},{36,6},{1,39},{3,... | collective-permute-start | bytes 1769480 | tf_op jit(solution)/shard_map/ppermute | solution.py:528
  13.1 41.4 %collective-permute-start = (f32[9,64,256]{2,1,0:T(8,128)S(1)}, f32[9,64,256]{2,1,0:T(8,128)}, u32[]{:S(2)}, u32[]{:S(2)}) collective-permute-start(f32[9,64,256]{2,1,0:T(8,128)S(1)} %get-tuple-element.190), channel_id=1, source_target_pairs={{0,32},{2,34},{4,36},{6,38},{32,0},{34,2},{36,4},{38,6},{1,33},{3,... | collective-permute-start | bytes 1769480 | tf_op jit(solution)/shard_map/ppermute | solution.py:527
  16.0 16.0 %collective-permute-start.2 = (f32[112,256]{1,0:T(8,128)S(1)}, f32[112,256]{1,0:T(8,128)S(1)}, u32[]{:S(2)}, u32[]{:S(2)}) collective-permute-start(f32[112,256]{1,0:T(8,128)S(1)} %get-tuple-element.96), channel_id=1, source_target_pairs={{0,1},{1,2},{2,3},{3,4},{4,5},{5,6},{6,7},{7,8},{8,9},{9,10},{10,1... | collective-permute-start | bytes 344072 | tf_op jit(solution)/shard_map/ppermute | solution.py:536
  17.9 14.1 %collective-permute-start.3 = (f32[112,256]{1,0:T(8,128)S(1)}, f32[112,256]{1,0:T(8,128)S(1)}, u32[]{:S(2)}, u32[]{:S(2)}) collective-permute-start(f32[112,256]{1,0:T(8,128)S(1)} %get-tuple-element.97), channel_id=1, source_target_pairs={{1,0},{2,1},{3,2},{4,3},{5,4},{6,5},{7,6},{8,7},{9,8},{10,9},{11,1... | collective-permute-start | bytes 344072 | tf_op jit(solution)/shard_map/ppermute | solution.py:536
  33.0 20.7 %collective-permute-start.4 = (f32[392,256]{1,0:T(8,128)S(1)}, f32[392,256]{1,0:T(8,128)S(1)}, u32[]{:S(2)}, u32[]{:S(2)}) collective-permute-start(f32[392,256]{1,0:T(8,128)S(1)} %get-tuple-element.100.fields), channel_id=1, source_target_pairs={{0,32},{32,0},{1,33},{33,1},{2,34},{34,2},{3,35},{35,3},{4,36},{36... | collective-permute-start | bytes 1204232 | tf_op jit(solution)/shard_map/ppermute | solution.py:556
  54.5 4.4 %collective-permute-start.5 = (f32[9,64,256]{2,1,0:T(8,128)}, f32[9,64,256]{2,1,0:T(8,128)}, u32[]{:S(2)}, u32[]{:S(2)}) collective-permute-start(f32[9,64,256]{2,1,0:T(8,128)} %collective-permute-done.near), channel_id=1, source_target_pairs={{0,1},{1,0},{2,3},{3,2},{4,5},{5,4},{6,7},{7,6},{8,9},{9,8},{10,11... | collective-permute-start | bytes 1769480 | tf_op jit(solution)/shard_map/ppermute | solution.py:561
  56.5 4.2 %collective-permute-start.6 = (f32[9,64,256]{2,1,0:T(8,128)S(1)}, f32[9,64,256]{2,1,0:T(8,128)}, u32[]{:S(2)}, u32[]{:S(2)}) collective-permute-start(f32[9,64,256]{2,1,0:T(8,128)S(1)} %collective-permute-done.1.near_two), channel_id=1, source_target_pairs={{0,1},{1,0},{2,3},{3,2},{4,5},{5,4},{6,7},{7,6},{8,9},{9,8},{10,11... | collective-permute-start | bytes 1769480 | tf_op jit(solution)/shard_map/ppermute | solution.py:562
  87.5 2.0 collective-permute-start.7
  88.2 2.3 collective-permute-start.8
  106.4 2.0 collective-permute-start.10
  107.1 2.3 collective-permute-start.11
  125.2 2.0 collective-permute-start.13
  125.9 2.3 collective-permute-start.14
  144.1 2.0 collective-permute-start.16
  144.8 2.3 collective-permute-start.17
  162.9 2.0 collective-permute-start.19
  163.6 2.3 collective-permute-start.20
  181.8 2.2 collective-permute-start.22
  182.5 2.5 collective-permute-start.23
  183.2 1.9 collective-permute-start.24
  200.9 54.2 %collective-permute-start.25 = (f32[128,256]{1,0:T(8,128)S(1)}, f32[128,256]{1,0:T(8,128)S(1)}, u32[]{:S(2)}, u32[]{:S(2)}) collective-permute-start(f32[128,256]{1,0:T(8,128)S(1)} %get-tuple-element.175), channel_id=1, source_target_pairs={{64,0},{65,1},{66,2},{67,3},{68,4},{69,5},{70,6},{71,7},{72,8},{73... | collective-permute-start | bytes 393224 | tf_op jit(solution)/shard_map/ppermute | solution.py:536
  202.2 53.8 %collective-permute-start.26 = (f32[32,256]{1,0:T(8,128)S(1)}, f32[32,256]{1,0:T(8,128)S(1)}, u32[]{:S(2)}, u32[]{:S(2)}) collective-permute-start(f32[32,256]{1,0:T(8,128)S(1)} %get-tuple-element.176), channel_id=1, source_target_pairs={{64,1},{65,2},{66,3},{67,4},{68,5},{69,6},{70,7},{71,8},{72,9},{73... | collective-permute-start | bytes 98312 | tf_op jit(solution)/shard_map/ppermute | solution.py:536
  203.5 52.6 %collective-permute-start.27 = (f32[32,256]{1,0:T(8,128)S(1)}, f32[32,256]{1,0:T(8,128)S(1)}, u32[]{:S(2)}, u32[]{:S(2)}) collective-permute-start(f32[32,256]{1,0:T(8,128)S(1)} %get-tuple-element.177), channel_id=1, source_target_pairs={{65,0},{66,1},{67,2},{68,3},{69,4},{70,5},{71,6},{72,7},{73,8},{74... | collective-permute-start | bytes 98312 | tf_op jit(solution)/shard_map/ppermute | solution.py:536
  277.0 4.8 %collective-permute-start.28 = (f32[128,2432]{1,0:T(8,128)S(1)}, f32[128,2432]{1,0:T(8,128)S(1)}, u32[]{:S(2)}, u32[]{:S(2)}) collective-permute-start(f32[128,2432]{1,0:T(8,128)S(1)} %get-tuple-element.188), channel_id=1, source_target_pairs={{0,1},{1,0},{2,3},{3,2},{4,5},{5,4},{6,7},{7,6},{8,9},{9,8},{10,11... | collective-permute-start | bytes 3735560 | tf_op jit(solution)/shard_map/ppermute | solution.py:625
  (15 other events, 134.6 us)

commit v6 on v5

--- a/solution.py
+++ b/solution.py
@@ -171,11 +171,11 @@
     a_high, a_low, b_high, b_low, pass_a, norm_a, pass_b, norm_b, params, opening, response,
     high_scr, low_scr, field_scr, flat_scr, full_scr,
 ):
-    tap = pl.program_id(0)
+    row_tap = pl.program_id(0)
     core = flags[3]
     member = flags[1]
 
-    @pl.when(tap == 0)
+    @pl.when(row_tap == 0)
     def _():
         stats = [
             jnp.sum(gathered[which * tiles : (which + 1) * tiles], axis=0) * (1.0 / count)
@@ -218,31 +218,30 @@
         flat_scr[...] = jnp.zeros_like(flat_scr)
         full_scr[...] = jnp.zeros_like(full_scr)
 
-    near_tap = jnp.concatenate([near[0], near_two[0]], axis=0)
-    far_tap = jnp.concatenate([far[0], far_two[0]], axis=0)
-    partner = jnp.concatenate(
-        [jnp.where(core == 0, near_tap, far_tap), jnp.where(core == 0, far_tap, near_tap)], axis=0
-    )
-    kernel_a = jnp.where(member == 1, own[0], partner)
-    kernel_b = jnp.where(member == 1, partner, own[0])
-    high, low = split(kernel_a.T)
-    a_high[0] = high
-    a_low[0] = low
-    high, low = split(kernel_b.T)
-    b_high[0] = high
-    b_low[0] = low
-
-    row_tap = tap // 3
-    col_tap = tap - row_tap * 3
     begin = pl.multiple_of((3 - row_tap) * COLS, COLS)
-    moved = split(field_scr[col_tap, pl.ds(begin, OWN), :])
-    moment = dot3((high_scr[...], low_scr[...]), moved)
-    full_scr[:C, :] += moment[:C, :C] * kernel_a
-    full_scr[C:, :] += moment[C:, :C] * kernel_a
-    flat_scr[:C, :] += moment[:C, C : C + 1] * kernel_a
-    flat_scr[C:, :] += moment[C:, C : C + 1] * kernel_a
-
-    @pl.when(tap == 8)
+    for col_tap in range(3):
+        near_tap = jnp.concatenate([near[col_tap], near_two[col_tap]], axis=0)
+        far_tap = jnp.concatenate([far[col_tap], far_two[col_tap]], axis=0)
+        partner = jnp.concatenate(
+            [jnp.where(core == 0, near_tap, far_tap), jnp.where(core == 0, far_tap, near_tap)],
+            axis=0,
+        )
+        kernel_a = jnp.where(member == 1, own[col_tap], partner)
+        kernel_b = jnp.where(member == 1, partner, own[col_tap])
+        high, low = split(kernel_a.T)
+        a_high[col_tap] = high
+        a_low[col_tap] = low
+        high, low = split(kernel_b.T)
+        b_high[col_tap] = high
+        b_low[col_tap] = low
+        moved = split(field_scr[col_tap, pl.ds(begin, OWN), :])
+        moment = dot3((high_scr[...], low_scr[...]), moved)
+        full_scr[:C, :] += moment[:C, :C] * kernel_a
+        full_scr[C:, :] += moment[C:, :C] * kernel_a
+        flat_scr[:C, :] += moment[:C, C : C + 1] * kernel_a
+        flat_scr[C:, :] += moment[C:, C : C + 1] * kernel_a
+
+    @pl.when(row_tap == 2)
     def _():
         groups = group_matrix()
         contract = (((0,), (1,)), ((), ()))
@@ -465,12 +464,12 @@
 
 
 def prepare(tiles, count, flags, kernel, pieces, gathered, fields, partner_fields):
-    tap = lambda rows: pl.BlockSpec((1, rows, C), lambda i: (i, 0, 0))
+    tap = lambda rows: pl.BlockSpec((3, rows, C), lambda i: (i, 0, 0))
     whole = lambda *dims: pl.BlockSpec(dims, lambda i: (0,) * len(dims))
     tall = 12 * COLS
     return pl.pallas_call(
         functools.partial(prepare_kernel, tiles, count),
-        grid=(9,),
+        grid=(3,),
         out_shape=tuple(shape(9, C, C, dtype=bf16) for _ in range(4))
         + tuple(shape(tall, C) for _ in range(4))
         + (shape(8, C), shape(2, C), shape(GROUPS, LANES)),

time: 319 us -> 317 us (level)
  no operation moved by 1% of the time
where the time goes in v6:
time: 317 us; the launch traced here: 316 us
  blocking collectives  157 us (50%)
  waiting for transfers between devices  62.3 us (20%)
  starting transfers between devices  45.7 us (14%)
  Pallas kernels  41.8 us (13%)
  local copies, waits for them, and re-layouts  5.65 us (2%)
    all_to_all x8, blocking collectives, on_device(): received = lax.all_to_all(sums, TILE, 0, 0)  105 us
    ppermute x23, waiting for transfers between devices, neighbours(): lax.ppermute(value, ALL, [(i, i - jump + step) for i in range(first, last...  57.8 us
    pallas_call x19, Pallas kernels, call(): pl.pallas_call(body, out_shape=out_shape, in_specs=in_specs, out_specs=tu...  35 us
    all_to_all x2, blocking collectives, on_device(): lax.all_to_all(mine.reshape(parts, mine.shape[0] // parts, width), axis,...  34.7 us
    ppermute x23, starting transfers between devices, neighbours(): lax.ppermute(value, ALL, [(i, i - jump + step) for i in range(first, last...  24.6 us
    all_to_all x1, blocking collectives, on_device(): gathered = lax.all_to_all(sums, ('member',) + TILE, 0, 0)  18 us
    ppermute x1, starting transfers between devices, on_device(): near_two = lax.ppermute(quarters[1], ('member', 'z'), route_two)  10.9 us
    pallas_call x1, Pallas kernels, prepare(): pl.pallas_call(functools.partial(prepare_kernel, tiles, count), grid=(3,)...  6.86 us
  transfers between devices with their start and end apart: 29, of which 4 were waited for; matrix products, arithmetic and copies ran while one was open for 0% of the time, Pallas kernels for 2%

profile of v6, /device:TPU:2, one launch (start us, length us, event | category | flops | bytes accessed | tf_op | source)
XLA Modules:
  0.0 315.7 jit_solution(9033850028897072066)
XLA Ops:
  2.2 10.9 %collective-permute-start.1 = (f32[9,64,256]{2,1,0:T(8,128)S(1)}, f32[9,64,256]{2,1,0:T(8,128)S(1)}, u32[]{:S(2)}, u32[]{:S(2)}) collective-permute-start(f32[9,64,256]{2,1,0:T(8,128)S(1)} %get-tuple-element.189), channel_id=1, source_target_pairs={{0,38},{2,32},{4,34},{6,36},{38,0},{32,2},{34,4},{36,6},{1,39},{3,... | collective-permute-start | bytes 1769480 | tf_op jit(solution)/shard_map/ppermute | solution.py:527
  17.9 6.7 %collective-permute-start.3 = (f32[112,256]{1,0:T(8,128)S(1)}, f32[112,256]{1,0:T(8,128)S(1)}, u32[]{:S(2)}, u32[]{:S(2)}) collective-permute-start(f32[112,256]{1,0:T(8,128)S(1)} %get-tuple-element.97), channel_id=1, source_target_pairs={{1,0},{2,1},{3,2},{4,3},{5,4},{6,5},{7,6},{8,7},{9,8},{10,9},{11,1... | collective-permute-start | bytes 344072 | tf_op jit(solution)/shard_map/ppermute | solution.py:535
  24.6 7.4 %collective-permute-done.2.above = f32[112,256]{1,0:T(8,128)S(1)} collective-permute-done((f32[112,256]{1,0:T(8,128)S(1)}, f32[112,256]{1,0:T(8,128)S(1)}, u32[]{:S(2)}, u32[]{:S(2)}) %collective-permute-start.2) | collective-permute-done | bytes 114720 | tf_op jit(solution)/shard_map/ppermute | solution.py:535
  35.7 18.0 %all_to_all.55.gathered = f32[64,1,128]{2,1,0:T(1,128)S(1)} all-to-all(f32[64,1,128]{2,1,0:T(1,128)S(1)} %get-tuple-element.99), channel_id=1, replica_groups=mesh['pair'=8,'member'=2,'x'=4,'z'=4,'core'=2] {'member','x','z','core'}, dimensions={0} | all-to-all | bytes 65536 | tf_op jit(solution)/shard_map/all_to_all | solution.py:556
  62.6 6.9 %shard_map.96 = (bf16[9,256,256]{2,1,0:T(8,128)(2,1)S(1)}, bf16[9,256,256]{2,1,0:T(8,128)(2,1)S(1)}, bf16[9,256,256]{2,1,0:T(8,128)(2,1)S(1)}, bf16[9,256,256]{2...) custom-call(s32[4]{0:T(128)S(1)} %pad_add_fusion.flags, ...), custom_call_target="tpu_custom_call" | custom-call | tf_op jit(solution)/shard_map/pallas_call | solution.py:470
  71.0 12.8 %all_to_all.56.received = f32[32,2,128]{2,1,0:T(2,128)S(1)} all-to-all(f32[32,2,128]{2,1,0:T(2,128)S(1)} %get-tuple-element.114), channel_id=1, replica_groups=mesh['pair'=8,'member'=2,'x'=4,'z'=4,'core'=2] {'x','z','core'}, dimensions={0} | all-to-all | bytes 65536 | tf_op jit(solution)/shard_map/all_to_all | solution.py:586
  88.2 12.8 %all_to_all.57.received.exchanged = f32[32,2,128]{2,1,0:T(2,128)S(1)} all-to-all(f32[32,2,128]{2,1,0:T(2,128)S(1)} %shard_map.99), channel_id=1, replica_groups=mesh['pair'=8,'member'=2,'x'=4,'z'=4,'core'=2] {'x','z','core'}, dimensions={0} | all-to-all | bytes 65536 | tf_op jit(solution)/shard_map/all_to_all | solution.py:605
  101.0 3.1 shard_map.100
  107.1 12.7 %all_to_all.58.received = f32[32,1,128]{2,1,0:T(1,128)S(1)} all-to-all(f32[32,1,128]{2,1,0:T(1,128)S(1)} %shard_map.101), channel_id=1, replica_groups=mesh['pair'=8,'member'=2,'x'=4,'z'=4,'core'=2] {'x','z','core'}, dimensions={0} | all-to-all | bytes 32768 | tf_op jit(solution)/shard_map/all_to_all | solution.py:605
  119.8 3.1 shard_map.102
  125.9 12.7 %all_to_all.59.received = f32[32,1,128]{2,1,0:T(1,128)S(1)} all-to-all(f32[32,1,128]{2,1,0:T(1,128)S(1)} %shard_map.103), channel_id=1, replica_groups=mesh['pair'=8,'member'=2,'x'=4,'z'=4,'core'=2] {'x','z','core'}, dimensions={0} | all-to-all | bytes 32768 | tf_op jit(solution)/shard_map/all_to_all | solution.py:605
  138.7 3.1 shard_map.104
  144.8 12.7 %all_to_all.60.received = f32[32,1,128]{2,1,0:T(1,128)S(1)} all-to-all(f32[32,1,128]{2,1,0:T(1,128)S(1)} %shard_map.105), channel_id=1, replica_groups=mesh['pair'=8,'member'=2,'x'=4,'z'=4,'core'=2] {'x','z','core'}, dimensions={0} | all-to-all | bytes 32768 | tf_op jit(solution)/shard_map/all_to_all | solution.py:605
  157.5 3.1 shard_map.106
  163.6 12.7 %all_to_all.61.received = f32[32,1,128]{2,1,0:T(1,128)S(1)} all-to-all(f32[32,1,128]{2,1,0:T(1,128)S(1)} %shard_map.107), channel_id=1, replica_groups=mesh['pair'=8,'member'=2,'x'=4,'z'=4,'core'=2] {'x','z','core'}, dimensions={0} | all-to-all | bytes 32768 | tf_op jit(solution)/shard_map/all_to_all | solution.py:605
  176.4 3.1 shard_map.108
  182.7 12.7 %all_to_all.62.received = f32[32,1,128]{2,1,0:T(1,128)S(1)} all-to-all(f32[32,1,128]{2,1,0:T(1,128)S(1)} %shard_map.109), channel_id=1, replica_groups=mesh['pair'=8,'member'=2,'x'=4,'z'=4,'core'=2] {'x','z','core'}, dimensions={0} | all-to-all | bytes 32768 | tf_op jit(solution)/shard_map/all_to_all | solution.py:605
  195.5 3.1 shard_map.110
  202.5 50.3 %collective-permute-done.25.main = f32[128,256]{1,0:T(8,128)S(1)} collective-permute-done((f32[128,256]{1,0:T(8,128)S(1)}, f32[128,256]{1,0:T(8,128)S(1)}, u32[]{:S(2)}, u32[]{:S(2)}) %collective-permute-start.25) | collective-permute-done | bytes 131104 | tf_op jit(solution)/shard_map/ppermute | solution.py:535
  253.7 15.4 %all_to_all.63.received = f32[32,1,128]{2,1,0:T(1,128)S(1)} all-to-all(f32[32,1,128]{2,1,0:T(1,128)S(1)} %shard_map.111), channel_id=1, replica_groups=mesh['pair'=8,'member'=2,'x'=4,'z'=4,'core'=2] {'x','z','core'}, dimensions={0} | all-to-all | bytes 32768 | tf_op jit(solution)/shard_map/all_to_all | solution.py:605
  269.2 3.8 %shard_map.112 = (f32[128,256]{1,0:T(8,128)}, f32[32,256]{1,0:T(8,128)}, f32[32,256]{1,0:T(8,128)}, f32[128,256]{1,0:T(8,128)}, f32[128,256]{1,0:T(8,128)S(1)}, /*index=5*/f32[2,256]{1,0:T(2,128)S(1)}) custom-call(s32[4]{0:T(128)S(1)} %pad_add_fusion.flags, f32[32,1,128]{2,1,0:T(1,128)S(1)} %all_to_all.63.received, ...), custom_call_target="tpu_custom_call" | custom-call | tf_op jit(solution)/shard_map/pallas_call | solution.py:452
  276.6 2.9 collective-permute-done.28
  279.7 20.1 %all_to_all.64 = f32[4,32,2432]{2,1,0:T(8,128)S(1)} all-to-all(f32[4,32,2432]{2,1,0:T(8,128)S(1)} %bitcast.80), channel_id=1, replica_groups=mesh['pair'=8,'member'=2,'x'=4,'z'=4,'core'=2] {'x'}, dimensions={0} | all-to-all | bytes 2490368 | tf_op jit(solution)/shard_map/all_to_all | solution.py:628
  299.9 14.5 %all_to_all.65 = f32[4,8,2432]{2,1,0:T(8,128)S(1)} all-to-all(f32[4,8,2432]{2,1,0:T(8,128)S(1)} %bitcast.81), channel_id=1, replica_groups=mesh['pair'=8,'member'=2,'x'=4,'z'=4,'core'=2] {'z'}, dimensions={0} | all-to-all | bytes 622592 | tf_op jit(solution)/shard_map/all_to_all | solution.py:628
  (93 shorter events, 48.7 us)
Async XLA Ops:
  2.2 52.4 %collective-permute-start.1 = (f32[9,64,256]{2,1,0:T(8,128)S(1)}, f32[9,64,256]{2,1,0:T(8,128)S(1)}, u32[]{:S(2)}, u32[]{:S(2)}) collective-permute-start(f32[9,64,256]{2,1,0:T(8,128)S(1)} %get-tuple-element.189), channel_id=1, source_target_pairs={{0,38},{2,32},{4,34},{6,36},{38,0},{32,2},{34,4},{36,6},{1,39},{3,... | collective-permute-start | bytes 1769480 | tf_op jit(solution)/shard_map/ppermute | solution.py:527
  13.1 41.4 %collective-permute-start = (f32[9,64,256]{2,1,0:T(8,128)S(1)}, f32[9,64,256]{2,1,0:T(8,128)}, u32[]{:S(2)}, u32[]{:S(2)}) collective-permute-start(f32[9,64,256]{2,1,0:T(8,128)S(1)} %get-tuple-element.190), channel_id=1, source_target_pairs={{0,32},{2,34},{4,36},{6,38},{32,0},{34,2},{36,4},{38,6},{1,33},{3,... | collective-permute-start | bytes 1769480 | tf_op jit(solution)/shard_map/ppermute | solution.py:526
  16.0 16.0 %collective-permute-start.2 = (f32[112,256]{1,0:T(8,128)S(1)}, f32[112,256]{1,0:T(8,128)S(1)}, u32[]{:S(2)}, u32[]{:S(2)}) collective-permute-start(f32[112,256]{1,0:T(8,128)S(1)} %get-tuple-element.96), channel_id=1, source_target_pairs={{0,1},{1,2},{2,3},{3,4},{4,5},{5,6},{6,7},{7,8},{8,9},{9,10},{10,1... | collective-permute-start | bytes 344072 | tf_op jit(solution)/shard_map/ppermute | solution.py:535
  17.9 14.1 %collective-permute-start.3 = (f32[112,256]{1,0:T(8,128)S(1)}, f32[112,256]{1,0:T(8,128)S(1)}, u32[]{:S(2)}, u32[]{:S(2)}) collective-permute-start(f32[112,256]{1,0:T(8,128)S(1)} %get-tuple-element.97), channel_id=1, source_target_pairs={{1,0},{2,1},{3,2},{4,3},{5,4},{6,5},{7,6},{8,7},{9,8},{10,9},{11,1... | collective-permute-start | bytes 344072 | tf_op jit(solution)/shard_map/ppermute | solution.py:535
  33.0 20.7 %collective-permute-start.4 = (f32[392,256]{1,0:T(8,128)S(1)}, f32[392,256]{1,0:T(8,128)S(1)}, u32[]{:S(2)}, u32[]{:S(2)}) collective-permute-start(f32[392,256]{1,0:T(8,128)S(1)} %get-tuple-element.100.fields), channel_id=1, source_target_pairs={{0,32},{32,0},{1,33},{33,1},{2,34},{34,2},{3,35},{35,3},{4,36},{36... | collective-permute-start | bytes 1204232 | tf_op jit(solution)/shard_map/ppermute | solution.py:555
  54.5 4.4 %collective-permute-start.5 = (f32[9,64,256]{2,1,0:T(8,128)}, f32[9,64,256]{2,1,0:T(8,128)}, u32[]{:S(2)}, u32[]{:S(2)}) collective-permute-start(f32[9,64,256]{2,1,0:T(8,128)} %collective-permute-done.near), channel_id=1, source_target_pairs={{0,1},{1,0},{2,3},{3,2},{4,5},{5,4},{6,7},{7,6},{8,9},{9,8},{10,11... | collective-permute-start | bytes 1769480 | tf_op jit(solution)/shard_map/ppermute | solution.py:560
  56.5 4.2 %collective-permute-start.6 = (f32[9,64,256]{2,1,0:T(8,128)S(1)}, f32[9,64,256]{2,1,0:T(8,128)}, u32[]{:S(2)}, u32[]{:S(2)}) collective-permute-start(f32[9,64,256]{2,1,0:T(8,128)S(1)} %collective-permute-done.1.near_two), channel_id=1, source_target_pairs={{0,1},{1,0},{2,3},{3,2},{4,5},{5,4},{6,7},{7,6},{8,9},{9,8},{10,11... | collective-permute-start | bytes 1769480 | tf_op jit(solution)/shard_map/ppermute | solution.py:561
  85.2 2.0 collective-permute-start.7
  85.9 2.3 collective-permute-start.8
  104.1 2.0 collective-permute-start.10
  104.8 2.3 collective-permute-start.11
  122.9 2.0 collective-permute-start.13
  123.6 2.3 collective-permute-start.14
  141.8 2.0 collective-permute-start.16
  142.5 2.3 collective-permute-start.17
  160.7 2.0 collective-permute-start.19
  161.3 2.3 collective-permute-start.20
  179.5 2.2 collective-permute-start.22
  180.2 2.5 collective-permute-start.23
  180.9 1.9 collective-permute-start.24
  198.6 54.2 %collective-permute-start.25 = (f32[128,256]{1,0:T(8,128)S(1)}, f32[128,256]{1,0:T(8,128)S(1)}, u32[]{:S(2)}, u32[]{:S(2)}) collective-permute-start(f32[128,256]{1,0:T(8,128)S(1)} %get-tuple-element.175), channel_id=1, source_target_pairs={{64,0},{65,1},{66,2},{67,3},{68,4},{69,5},{70,6},{71,7},{72,8},{73... | collective-permute-start | bytes 393224 | tf_op jit(solution)/shard_map/ppermute | solution.py:535
  199.9 53.8 %collective-permute-start.26 = (f32[32,256]{1,0:T(8,128)S(1)}, f32[32,256]{1,0:T(8,128)S(1)}, u32[]{:S(2)}, u32[]{:S(2)}) collective-permute-start(f32[32,256]{1,0:T(8,128)S(1)} %get-tuple-element.176), channel_id=1, source_target_pairs={{64,1},{65,2},{66,3},{67,4},{68,5},{69,6},{70,7},{71,8},{72,9},{73... | collective-permute-start | bytes 98312 | tf_op jit(solution)/shard_map/ppermute | solution.py:535
  201.2 52.6 %collective-permute-start.27 = (f32[32,256]{1,0:T(8,128)S(1)}, f32[32,256]{1,0:T(8,128)S(1)}, u32[]{:S(2)}, u32[]{:S(2)}) collective-permute-start(f32[32,256]{1,0:T(8,128)S(1)} %get-tuple-element.177), channel_id=1, source_target_pairs={{65,0},{66,1},{67,2},{68,3},{69,4},{70,5},{71,6},{72,7},{73,8},{74... | collective-permute-start | bytes 98312 | tf_op jit(solution)/shard_map/ppermute | solution.py:535
  274.7 4.8 %collective-permute-start.28 = (f32[128,2432]{1,0:T(8,128)S(1)}, f32[128,2432]{1,0:T(8,128)S(1)}, u32[]{:S(2)}, u32[]{:S(2)}) collective-permute-start(f32[128,2432]{1,0:T(8,128)S(1)} %get-tuple-element.188), channel_id=1, source_target_pairs={{0,1},{1,0},{2,3},{3,2},{4,5},{5,4},{6,7},{7,6},{8,9},{9,8},{10,11... | collective-permute-start | bytes 3735560 | tf_op jit(solution)/shard_map/ppermute | solution.py:624
  (15 other events, 134.6 us)
